TPU v7x, 32 devices: a whole 2x2x4 slice. The times are simulated.
32 devices in a mesh: beam: 4 (over z), lat: 8 (over y, x, core).
Axes of the slice: x: 2, y: 2, z: 4, core: 2. Of those that a mesh axis runs over, the one named last changes fastest.
Arguments:
- contrast: float32 [2, 4, 1024, 256], P(None, 'beam', 'lat'), may hold values from -0.15 to 0.15
- probe: float32 [2, 128, 128], replicated, may hold values from -6 to 6
- offset_x: int32 [64], P('lat'), may hold values from 0 to 127
- offset_y: int32 [64], P('lat'), may hold values from 0 to 128
- probe_count: int32 [8], P('lat'), may hold values from 1 to 8, 48 in all
- measured: float32 [64, 128, 128], P('lat'), may hold values from 0 to 4
Outputs:
- object_gradient: float32 [2, 4, 1024, 256], P(None, 'beam', 'lat')
Inputs may be any that keep to these rules, and one draw needn't show every extreme that they name: `probe_count`: slots below this count hold probes; the others hold none and add nothing; some lat index has all 8. `offset_x`: a probe's block may reach into the next lat index's columns.
All inputs are finite; a program needn't handle non-finite values. No bound on the sum of `probe_count` on one device may be relied on, other than what follows from the above.
Results may differ from a plain program's by a relative error of at most 0.038.
Values may be sent and summed in bfloat16 or wider, within the bound.
No kernel may reach another device: no remote copies, remote signals or barrier semaphores. Data moves between devices by JAX's collectives and lax.ppermute only.
A program may use at most 64 MiB of HBM per device.

v0:
```python
import math

import jax
import jax.numpy as jnp
from jax import lax
from jax.sharding import PartitionSpec as P


def shifted_2(value, axis, by):
    length = lax.axis_size(axis)
    pairs = [(i, i + by) for i in range(length) if 0 <= i + by < length]
    return lax.ppermute(value, axis, pairs)


def tables(order):
    index = jnp.arange(order, dtype=jnp.int32)
    product = index[:, None] * index[None, :] % order
    theta = product.astype(jnp.float32) * (2.0 * math.pi / order)
    factor = 1.0 / math.sqrt(order)
    shifted = (index + order // 2) % order - order // 2
    quad = (shifted[:, None] * shifted[:, None] + shifted[None, :] * shifted[None, :]) % (4 * order)
    phase = quad.astype(jnp.float32) * (-math.pi / (2 * order))
    return (jnp.cos(theta) * factor, -jnp.sin(theta) * factor, jnp.cos(phase), jnp.sin(phase))


def left_product(matrix, field):
    return jnp.einsum("mn,...nk->...mk", matrix, field, precision=lax.Precision.HIGHEST)


def right_product(field, matrix):
    return jnp.einsum("...mn,nk->...mk", field, matrix, precision=lax.Precision.HIGHEST)


def both_sides(field_re, field_im, matrix_re, matrix_im):
    half_re = left_product(matrix_re, field_re) - left_product(matrix_im, field_im)
    half_im = left_product(matrix_re, field_im) + left_product(matrix_im, field_re)
    full_re = right_product(half_re, matrix_re) - right_product(half_im, matrix_im)
    full_im = right_product(half_re, matrix_im) + right_product(half_im, matrix_re)
    return (full_re, full_im)


def propagate(field_re, field_im, tabs, sign):
    dft_re, dft_im, kernel_re, kernel_im = tabs
    spec_re, spec_im = both_sides(field_re, field_im, dft_re, dft_im)
    signed_im = sign * kernel_im
    mixed_re = spec_re * kernel_re - spec_im * signed_im
    mixed_im = spec_re * signed_im + spec_im * kernel_re
    return both_sides(mixed_re, mixed_im, dft_re, -dft_im)


def far_field(exit_re, exit_im, observed, live, tabs):
    dft_re, dft_im = (tabs[0], tabs[1])
    far_re, far_im = both_sides(exit_re, exit_im, dft_re, dft_im)
    misfit = live[:, None, None] * (far_re * far_re + far_im * far_im - observed)
    return both_sides(misfit * far_re, misfit * far_im, dft_re, -dft_im)


def on_device(contrast, probe, offset_x, offset_y, probe_count, measured):
    patch_size = probe.shape[1]
    slices = contrast.shape[1]
    tile_cols = contrast.shape[2]
    height = contrast.shape[3]
    slot_count = offset_x.shape[0]
    beam_size = lax.axis_size("beam")
    group_index = lax.axis_index("beam")
    tabs = tables(patch_size)
    anchor = jnp.zeros((), jnp.int32)
    rim_cols = shifted_2(contrast.astype(jnp.bfloat16), "lat", -1).astype(contrast.dtype)
    extended = jnp.concatenate([contrast, rim_cols], axis=2)

    def cut_block(x_start, y_start):
        return lax.dynamic_slice(
            extended, (anchor, anchor, x_start, y_start), (2, slices, patch_size, patch_size)
        )

    patches = jax.vmap(cut_block)(offset_x, offset_y)
    trans_re = 1.0 + jnp.transpose(patches[:, 0], (1, 0, 2, 3))
    trans_im = jnp.transpose(patches[:, 1], (1, 0, 2, 3))
    live_count = probe_count[0]
    live = (jnp.arange(slot_count, dtype=jnp.int32) < live_count).astype(jnp.float32)
    batch_size = 2
    batches = slot_count // batch_size
    steps = beam_size + batches - 1
    block_shape = (batch_size, patch_size, patch_size)

    def take(array, layer_index, first_slot):
        return lax.dynamic_slice(
            array, (jnp.int32(layer_index), first_slot, anchor, anchor), (1,) + block_shape
        )[0]

    def forward_step(step_index, loop_state):
        incoming, kept_re, kept_im, exit_re, exit_im = loop_state
        batch = step_index - group_index
        first_slot = jnp.clip(batch, 0, batches - 1) * batch_size
        active = (batch >= 0) & (batch < batches) & (first_slot < live_count)
        first_wave = jnp.broadcast_to(probe[:, None], (2,) + block_shape)
        wave = jnp.where(group_index == 0, first_wave, incoming.astype(jnp.float32))

        def forward_run_batch(state):
            kept_re, kept_im, exit_re, exit_im = state
            wave_re, wave_im = (wave[0], wave[1])
            place = (jnp.int32(0), first_slot, anchor, anchor)
            kept_re = lax.dynamic_update_slice(kept_re, wave_re[None], place)
            kept_im = lax.dynamic_update_slice(kept_im, wave_im[None], place)
            group_re = take(trans_re, 0, first_slot)
            group_im = take(trans_im, 0, first_slot)
            mult_re = group_re * wave_re - group_im * wave_im
            mult_im = group_re * wave_im + group_im * wave_re
            wave_re, wave_im = propagate(mult_re, mult_im, tabs, 1.0)
            exit_re = lax.dynamic_update_slice(exit_re, wave_re, (first_slot, anchor, anchor))
            exit_im = lax.dynamic_update_slice(exit_im, wave_im, (first_slot, anchor, anchor))
            outgoing = jnp.stack([wave_re, wave_im]).astype(jnp.bfloat16)
            return (kept_re, kept_im, exit_re, exit_im, outgoing)

        def forward_pass_batch(state):
            return state + (jnp.zeros((2,) + block_shape, jnp.bfloat16),)

        kept_re, kept_im, exit_re, exit_im, outgoing = lax.cond(
            active, forward_run_batch, forward_pass_batch, (kept_re, kept_im, exit_re, exit_im)
        )
        incoming = shifted_2(outgoing, "beam", 1)
        return (incoming, kept_re, kept_im, exit_re, exit_im)

    stored_shape = (slices, slot_count, patch_size, patch_size)
    exit_shape = (slot_count, patch_size, patch_size)
    start_state = (
        jnp.zeros((2,) + block_shape, jnp.bfloat16),
        jnp.zeros(stored_shape, jnp.float32),
        jnp.zeros(stored_shape, jnp.float32),
        jnp.zeros(exit_shape, jnp.float32),
        jnp.zeros(exit_shape, jnp.float32),
    )
    unused, kept_re, kept_im, exit_re, exit_im = lax.fori_loop(0, steps, forward_step, start_state)

    def final_far(state):
        return far_field(state[0], state[1], measured, live, tabs)

    def empty_far(state):
        return (jnp.zeros(exit_shape, jnp.float32), jnp.zeros(exit_shape, jnp.float32))

    last_re, last_im = lax.cond(
        group_index == beam_size - 1, final_far, empty_far, (exit_re, exit_im)
    )
    last_adjoint = jnp.stack([last_re, last_im])

    def back_step(step_index, loop_state):
        incoming, grad_re, grad_im = loop_state
        batch = step_index - (beam_size - 1 - group_index)
        first_slot = jnp.clip(batch, 0, batches - 1) * batch_size
        active = (batch >= 0) & (batch < batches) & (first_slot < live_count)
        own_adjoint = lax.dynamic_slice_in_dim(last_adjoint, first_slot, batch_size, 1)
        adjoint = jnp.where(group_index == beam_size - 1, own_adjoint, incoming.astype(jnp.float32))

        def back_run_batch(state):
            grad_re, grad_im = state
            adj_re, adj_im = (adjoint[0], adjoint[1])
            for layer_index in reversed(range(slices)):
                back_re, back_im = propagate(adj_re, adj_im, tabs, -1.0)
                psi_re = take(kept_re, layer_index, first_slot)
                psi_im = take(kept_im, layer_index, first_slot)
                place = (jnp.int32(layer_index), first_slot, anchor, anchor)
                grad_re = lax.dynamic_update_slice(
                    grad_re, (psi_re * back_re + psi_im * back_im)[None], place
                )
                grad_im = lax.dynamic_update_slice(
                    grad_im, (psi_re * back_im - psi_im * back_re)[None], place
                )
                group_re = take(trans_re, layer_index, first_slot)
                group_im = take(trans_im, layer_index, first_slot)
                adj_re, adj_im = (
                    group_re * back_re + group_im * back_im,
                    group_re * back_im - group_im * back_re,
                )
            outgoing = jnp.stack([adj_re, adj_im]).astype(jnp.bfloat16)
            return (grad_re, grad_im, outgoing)

        def back_pass_batch(state):
            return state + (jnp.zeros((2,) + block_shape, jnp.bfloat16),)

        grad_re, grad_im, outgoing = lax.cond(
            active, back_run_batch, back_pass_batch, (grad_re, grad_im)
        )
        incoming = shifted_2(outgoing, "beam", -1)
        return (incoming, grad_re, grad_im)

    back_state = (
        jnp.zeros((2,) + block_shape, jnp.bfloat16),
        jnp.zeros(stored_shape, jnp.float32),
        jnp.zeros(stored_shape, jnp.float32),
    )
    unused, grad_re, grad_im = lax.fori_loop(0, steps, back_step, back_state)
    grad_ext = jnp.zeros((2, slices, tile_cols + patch_size, height), jnp.float32)
    for slot_index in range(slot_count):
        piece = jnp.stack([grad_re[:, slot_index], grad_im[:, slot_index]])
        place = (anchor, anchor, offset_x[slot_index], offset_y[slot_index])
        current = lax.dynamic_slice(grad_ext, place, piece.shape)
        grad_ext = lax.dynamic_update_slice(grad_ext, current + piece, place)
    arrived = shifted_2(grad_ext[:, :, tile_cols:].astype(jnp.bfloat16), "lat", 1).astype(
        jnp.float32
    )
    own_cols = grad_ext[:, :, :tile_cols]
    return own_cols.at[:, :, :patch_size].add(arrived)


def solution(mesh):
    in_specs = (
        P(None, "beam", "lat", None),
        P(),
        P("lat"),
        P("lat"),
        P("lat"),
        P("lat", None, None),
    )
    out_specs = P(None, "beam", "lat", None)
    return jax.shard_map(
        on_device, mesh=mesh, in_specs=in_specs, out_specs=out_specs, check_vma=False
    )
```

profile of v0, /device:TPU:5, one launch (start us, length us, event | category | flops | bytes accessed | tf_op | source)
XLA Modules:
  0.0 338.4 jit_solution(5029959316353346334)
XLA Ops:
  1.0 2.7 collective-permute-start.2
  35.7 16.1 %while.50 = (s32[]{:T(128)}, f32[2,1,256,256]{3,2,1,0:T(8,128)S(1)}, s32[8,4]{0,1:T(4,128)S(1)}, f32[8,2,1,128,128]{4,3,0,2,1:T(8,128)S(1)}, s32[]{:T(128)}) while((s32[]{:T(128)}, f32[2,1,256,256]{3,2,1,0:T(8,128)S(1)}, s32[8,4]{0,1:T(4,128)S(1)}, f32[8,2,1,128,128]{4,3,0,2,1:T(8,128)S(1)}, s32[]{:T(128)}) %tuple.262), condition=%wide.while_cond.1, body=%wide.while_body.1.sunk | while | flops 2 | bytes 262269 | solution.py:72
  54.9 86.4 %while.51 = (s32[]{:T(128)}, bf16[2,2,128,128]{3,2,1,0:T(8,128)(2,1)S(1)}, f32[1,8,128,128]{2,3,1,0:T(8,128)}, f32[1,8,128,128]{2,3,1,0:T(8,128)}, f32[8,128,128...) while((s32[]{:T(128)}, ...), condition=%wide.region_3.4_spmd.clone.clone.clone, body=%wide.region_0.3_spmd.clone.clone.clone.sunk | while | flops 806993920 | bytes 11207714 | solution.py:133
  55.7 8.7 %conditional.12 = (f32[1,8,128,128]{2,3,1,0:T(8,128)}, f32[1,8,128,128]{2,3,1,0:T(8,128)}, f32[8,128,128]{2,1,0:T(8,128)S(1)}, f32[8,128,128]{2,1,0:T(8,128)S(1)}, bf16[2,2,128,128]{3,2,1,0:T(8,128)(2,1)S(1)}) conditional(s32[]{:T(128)} %convert_element_type.248, (f32[1,8,128,128]{2,3,1,0:T(8,128)}, f32[1,8,128,128]{2,3,1,0:T(8,128)}, ...), branch_computations={%region_1.1_spmd, %region_2.2_spmd.clone} | conditional | flops 806535168 | bytes 10485843 | solution.py:118
  68.7 8.8 %conditional.12 = (f32[1,8,128,128]{2,3,1,0:T(8,128)}, f32[1,8,128,128]{2,3,1,0:T(8,128)}, f32[8,128,128]{2,1,0:T(8,128)S(1)}, f32[8,128,128]{2,1,0:T(8,128)S(1)}, bf16[2,2,128,128]{3,2,1,0:T(8,128)(2,1)S(1)}) conditional(s32[]{:T(128)} %convert_element_type.248, (f32[1,8,128,128]{2,3,1,0:T(8,128)}, f32[1,8,128,128]{2,3,1,0:T(8,128)}, ...), branch_computations={%region_1.1_spmd, %region_2.2_spmd.clone} | conditional | flops 806535168 | bytes 10485843 | solution.py:118
  77.5 4.1 %collective-permute-start = (bf16[2,2,128,128]{3,2,1,0:T(8,128)(2,1)S(1)}, bf16[2,2,128,128]{3,2,1,0:T(8,128)(2,1)S(1)}, u32[]{:S(2)}, u32[]{:S(2)}) collective-permute-start(bf16[2,2,128,128]{3,2,1,0:T(8,128)(2,1)S(1)} %get-tuple-element.1888), channel_id=1, source_target_pairs={{0,8},{8,16},{16,24},{1,9},{9,17},{17,25},{2,10},{10,18},{18,26},{... | collective-permute-start | bytes 393224 | tf_op jit(solution)/shard_map/while/body/eval_jaxpr/ppermute | solution.py:12
  84.2 8.8 %conditional.12 = (f32[1,8,128,128]{2,3,1,0:T(8,128)}, f32[1,8,128,128]{2,3,1,0:T(8,128)}, f32[8,128,128]{2,1,0:T(8,128)S(1)}, f32[8,128,128]{2,1,0:T(8,128)S(1)}, bf16[2,2,128,128]{3,2,1,0:T(8,128)(2,1)S(1)}) conditional(s32[]{:T(128)} %convert_element_type.248, (f32[1,8,128,128]{2,3,1,0:T(8,128)}, f32[1,8,128,128]{2,3,1,0:T(8,128)}, ...), branch_computations={%region_1.1_spmd, %region_2.2_spmd.clone} | conditional | flops 806535168 | bytes 10485843 | solution.py:118
  93.0 3.8 %collective-permute-start = (bf16[2,2,128,128]{3,2,1,0:T(8,128)(2,1)S(1)}, bf16[2,2,128,128]{3,2,1,0:T(8,128)(2,1)S(1)}, u32[]{:S(2)}, u32[]{:S(2)}) collective-permute-start(bf16[2,2,128,128]{3,2,1,0:T(8,128)(2,1)S(1)} %get-tuple-element.1888), channel_id=1, source_target_pairs={{0,8},{8,16},{16,24},{1,9},{9,17},{17,25},{2,10},{10,18},{18,26},{... | collective-permute-start | bytes 393224 | tf_op jit(solution)/shard_map/while/body/eval_jaxpr/ppermute | solution.py:12
  99.6 12.5 %collective-permute-start = (bf16[2,2,128,128]{3,2,1,0:T(8,128)(2,1)S(1)}, bf16[2,2,128,128]{3,2,1,0:T(8,128)(2,1)S(1)}, u32[]{:S(2)}, u32[]{:S(2)}) collective-permute-start(bf16[2,2,128,128]{3,2,1,0:T(8,128)(2,1)S(1)} %get-tuple-element.1888), channel_id=1, source_target_pairs={{0,8},{8,16},{16,24},{1,9},{9,17},{17,25},{2,10},{10,18},{18,26},{... | collective-permute-start | bytes 393224 | tf_op jit(solution)/shard_map/while/body/eval_jaxpr/ppermute | solution.py:12
  114.8 3.8 %collective-permute-start = (bf16[2,2,128,128]{3,2,1,0:T(8,128)(2,1)S(1)}, bf16[2,2,128,128]{3,2,1,0:T(8,128)(2,1)S(1)}, u32[]{:S(2)}, u32[]{:S(2)}) collective-permute-start(bf16[2,2,128,128]{3,2,1,0:T(8,128)(2,1)S(1)} %get-tuple-element.1888), channel_id=1, source_target_pairs={{0,8},{8,16},{16,24},{1,9},{9,17},{17,25},{2,10},{10,18},{18,26},{... | collective-permute-start | bytes 393224 | tf_op jit(solution)/shard_map/while/body/eval_jaxpr/ppermute | solution.py:12
  121.4 10.6 %collective-permute-start = (bf16[2,2,128,128]{3,2,1,0:T(8,128)(2,1)S(1)}, bf16[2,2,128,128]{3,2,1,0:T(8,128)(2,1)S(1)}, u32[]{:S(2)}, u32[]{:S(2)}) collective-permute-start(bf16[2,2,128,128]{3,2,1,0:T(8,128)(2,1)S(1)} %get-tuple-element.1888), channel_id=1, source_target_pairs={{0,8},{8,16},{16,24},{1,9},{9,17},{17,25},{2,10},{10,18},{18,26},{... | collective-permute-start | bytes 393224 | tf_op jit(solution)/shard_map/while/body/eval_jaxpr/ppermute | solution.py:12
  134.8 3.8 %collective-permute-start = (bf16[2,2,128,128]{3,2,1,0:T(8,128)(2,1)S(1)}, bf16[2,2,128,128]{3,2,1,0:T(8,128)(2,1)S(1)}, u32[]{:S(2)}, u32[]{:S(2)}) collective-permute-start(bf16[2,2,128,128]{3,2,1,0:T(8,128)(2,1)S(1)} %get-tuple-element.1888), channel_id=1, source_target_pairs={{0,8},{8,16},{16,24},{1,9},{9,17},{17,25},{2,10},{10,18},{18,26},{... | collective-permute-start | bytes 393224 | tf_op jit(solution)/shard_map/while/body/eval_jaxpr/ppermute | solution.py:12
  138.6 2.7 collective-permute-done
  148.2 130.9 %while.52 = (s32[]{:T(128)}, bf16[2,2,128,128]{3,2,1,0:T(8,128)(2,1)S(1)}, f32[1,8,128,128]{3,2,1,0:T(8,128)}, f32[1,8,128,128]{3,2,1,0:T(8,128)}, s32[]{:T(128)...) while((s32[]{:T(128)}, ...), condition=%wide.region_9.10_spmd.clone.clone.clone, body=%wide.region_6.9_spmd.clone.clone.clone.sunk | while | flops 807206912 | bytes 11207686 | solution.py:191
  150.4 10.9 %collective-permute-done.1 = bf16[2,2,128,128]{3,2,1,0:T(8,128)(2,1)S(1)} collective-permute-done((bf16[2,2,128,128]{3,2,1,0:T(8,128)(2,1)S(1)}, bf16[2,2,128,128]{3,2,1,0:T(8,128)(2,1)S(1)}, u32[]{:S(2)}, u32[]{:S(2)}) %collective-permute-start.1) | collective-permute-done | bytes 131104 | tf_op jit(solution)/shard_map/while/body/eval_jaxpr/ppermute | solution.py:12
  163.5 6.9 %collective-permute-done.1 = bf16[2,2,128,128]{3,2,1,0:T(8,128)(2,1)S(1)} collective-permute-done((bf16[2,2,128,128]{3,2,1,0:T(8,128)(2,1)S(1)}, bf16[2,2,128,128]{3,2,1,0:T(8,128)(2,1)S(1)}, u32[]{:S(2)}, u32[]{:S(2)}) %collective-permute-start.1) | collective-permute-done | bytes 131104 | tf_op jit(solution)/shard_map/while/body/eval_jaxpr/ppermute | solution.py:12
  172.5 54.3 %collective-permute-done.1 = bf16[2,2,128,128]{3,2,1,0:T(8,128)(2,1)S(1)} collective-permute-done((bf16[2,2,128,128]{3,2,1,0:T(8,128)(2,1)S(1)}, bf16[2,2,128,128]{3,2,1,0:T(8,128)(2,1)S(1)}, u32[]{:S(2)}, u32[]{:S(2)}) %collective-permute-start.1) | collective-permute-done | bytes 131104 | tf_op jit(solution)/shard_map/while/body/eval_jaxpr/ppermute | solution.py:12
  227.7 8.7 %conditional.13 = (f32[1,8,128,128]{3,2,1,0:T(8,128)}, f32[1,8,128,128]{3,2,1,0:T(8,128)}, bf16[2,2,128,128]{3,2,1,0:T(8,128)(2,1)S(1)}) conditional(s32[]{:T(128)} %convert_element_type.250, (f32[1,8,128,128]{3,2,1,0:T(8,128)}, f32[1,8,128,128]{3,2,1,0:T(8,128)}) %tuple.256, (s32[]{:T(128)}, f32[1,8,128,128]{3,2,1,0:T(8,128)S(1)}, pred[]{:T(512)}, ...), branch_computations={%region_7.7_spmd, %region_8.8_spmd.clone} | conditional | flops 806748160 | bytes 10485831 | solution.py:180
  237.7 4.5 %collective-permute-done.1 = bf16[2,2,128,128]{3,2,1,0:T(8,128)(2,1)S(1)} collective-permute-done((bf16[2,2,128,128]{3,2,1,0:T(8,128)(2,1)S(1)}, bf16[2,2,128,128]{3,2,1,0:T(8,128)(2,1)S(1)}, u32[]{:S(2)}, u32[]{:S(2)}) %collective-permute-start.1) | collective-permute-done | bytes 131104 | tf_op jit(solution)/shard_map/while/body/eval_jaxpr/ppermute | solution.py:12
  242.9 8.7 %conditional.13 = (f32[1,8,128,128]{3,2,1,0:T(8,128)}, f32[1,8,128,128]{3,2,1,0:T(8,128)}, bf16[2,2,128,128]{3,2,1,0:T(8,128)(2,1)S(1)}) conditional(s32[]{:T(128)} %convert_element_type.250, (f32[1,8,128,128]{3,2,1,0:T(8,128)}, f32[1,8,128,128]{3,2,1,0:T(8,128)}) %tuple.256, (s32[]{:T(128)}, f32[1,8,128,128]{3,2,1,0:T(8,128)S(1)}, pred[]{:T(512)}, ...), branch_computations={%region_7.7_spmd, %region_8.8_spmd.clone} | conditional | flops 806748160 | bytes 10485831 | solution.py:180
  253.0 4.4 %collective-permute-done.1 = bf16[2,2,128,128]{3,2,1,0:T(8,128)(2,1)S(1)} collective-permute-done((bf16[2,2,128,128]{3,2,1,0:T(8,128)(2,1)S(1)}, bf16[2,2,128,128]{3,2,1,0:T(8,128)(2,1)S(1)}, u32[]{:S(2)}, u32[]{:S(2)}) %collective-permute-start.1) | collective-permute-done | bytes 131104 | tf_op jit(solution)/shard_map/while/body/eval_jaxpr/ppermute | solution.py:12
  258.2 8.7 %conditional.13 = (f32[1,8,128,128]{3,2,1,0:T(8,128)}, f32[1,8,128,128]{3,2,1,0:T(8,128)}, bf16[2,2,128,128]{3,2,1,0:T(8,128)(2,1)S(1)}) conditional(s32[]{:T(128)} %convert_element_type.250, (f32[1,8,128,128]{3,2,1,0:T(8,128)}, f32[1,8,128,128]{3,2,1,0:T(8,128)}) %tuple.256, (s32[]{:T(128)}, f32[1,8,128,128]{3,2,1,0:T(8,128)S(1)}, pred[]{:T(512)}, ...), branch_computations={%region_7.7_spmd, %region_8.8_spmd.clone} | conditional | flops 806748160 | bytes 10485831 | solution.py:180
  268.2 4.4 %collective-permute-done.1 = bf16[2,2,128,128]{3,2,1,0:T(8,128)(2,1)S(1)} collective-permute-done((bf16[2,2,128,128]{3,2,1,0:T(8,128)(2,1)S(1)}, bf16[2,2,128,128]{3,2,1,0:T(8,128)(2,1)S(1)}, u32[]{:S(2)}, u32[]{:S(2)}) %collective-permute-start.1) | collective-permute-done | bytes 131104 | tf_op jit(solution)/shard_map/while/body/eval_jaxpr/ppermute | solution.py:12
  274.8 4.4 %collective-permute-done.1 = bf16[2,2,128,128]{3,2,1,0:T(8,128)(2,1)S(1)} collective-permute-done((bf16[2,2,128,128]{3,2,1,0:T(8,128)(2,1)S(1)}, bf16[2,2,128,128]{3,2,1,0:T(8,128)(2,1)S(1)}, u32[]{:S(2)}, u32[]{:S(2)}) %collective-permute-start.1) | collective-permute-done | bytes 131104 | tf_op jit(solution)/shard_map/while/body/eval_jaxpr/ppermute | solution.py:12
  281.4 2.2 dynamic_update_slice.44
  283.8 2.5 dynamic_update_slice.45
  286.4 2.5 dynamic_update_slice.46
  289.0 2.4 dynamic_update_slice.47
  291.5 2.4 dynamic_update_slice.48
  294.0 2.4 dynamic_update_slice.49
  298.9 2.4 dynamic_update_slice.51
  301.3 34.5 %collective-permute-start.3 = (bf16[2,1,128,256]{3,2,1,0:T(8,128)(2,1)S(1)}, bf16[2,1,128,256]{3,2,1,0:T(8,128)(2,1)S(1)}, u32[]{:S(2)}, u32[]{:S(2)}) collective-permute-start(bf16[2,1,128,256]{3,2,1,0:T(8,128)(2,1)S(1)} %slice.228), channel_id=1, source_target_pairs={{0,1},{1,2},{2,3},{3,4},{4,5},{5,6},{6,7},{8,9},{9,10},{10,11},{11... | collective-permute-start | bytes 393224 | tf_op jit(solution)/shard_map/ppermute | solution.py:12
  (281 shorter events, 113.7 us)
Async XLA Ops:
  0.0 3.7 %copy-start.4 = (s32[8]{0:T(128)S(1)}, s32[8]{0:T(128)}, u32[]{:S(2)}) copy-start(s32[8]{0:T(128)} %param.22) | copy-start | bytes 100
  0.0 4.4 %copy-start.5 = (s32[8]{0:T(128)S(1)}, s32[8]{0:T(128)}, u32[]{:S(2)}) copy-start(s32[8]{0:T(128)} %param.23) | copy-start | bytes 100
  1.0 24.5 %copy-start.3 = (f32[2,128,128]{2,1,0:T(8,128)S(1)}, f32[2,128,128]{2,1,0:T(8,128)}, u32[]{:S(2)}) copy-start(f32[2,128,128]{2,1,0:T(8,128)} %param.21) | copy-start | bytes 393220
  1.0 34.6 %collective-permute-start.2 = (bf16[2,1,128,256]{3,2,1,0:T(8,128)(2,1)S(1)}, bf16[2,1,128,256]{3,2,1,0:T(8,128)(2,1)S(1)}, u32[]{:S(2)}, u32[]{:S(2)}) collective-permute-start(bf16[2,1,128,256]{3,2,1,0:T(8,128)(2,1)S(1)} %convert_element_type.169), channel_id=1, source_target_pairs={{1,0},{2,1},{3,2},{4,3},{5,4},{6,5},{7,6},{9,8},{10,9},{11,10},{12... | collective-permute-start | bytes 393224 | tf_op jit(solution)/shard_map/ppermute | solution.py:12
  25.6 10.0 %copy-start.1 = (f32[2,1,128,256]{3,2,1,0:T(8,128)S(1)}, f32[2,1,128,256]{3,2,1,0:T(8,128)}, u32[]{:S(2)}) copy-start(f32[2,1,128,256]{3,2,1,0:T(8,128)} %param.20) | copy-start | bytes 786436
  64.4 3.5 %collective-permute-start = (bf16[2,2,128,128]{3,2,1,0:T(8,128)(2,1)S(1)}, bf16[2,2,128,128]{3,2,1,0:T(8,128)(2,1)S(1)}, u32[]{:S(2)}, u32[]{:S(2)}) collective-permute-start(bf16[2,2,128,128]{3,2,1,0:T(8,128)(2,1)S(1)} %get-tuple-element.1888), channel_id=1, source_target_pairs={{0,8},{8,16},{16,24},{1,9},{9,17},{17,25},{2,10},{10,18},{18,26},{... | collective-permute-start | bytes 393224 | tf_op jit(solution)/shard_map/while/body/eval_jaxpr/ppermute | solution.py:12
  77.5 6.0 %collective-permute-start = (bf16[2,2,128,128]{3,2,1,0:T(8,128)(2,1)S(1)}, bf16[2,2,128,128]{3,2,1,0:T(8,128)(2,1)S(1)}, u32[]{:S(2)}, u32[]{:S(2)}) collective-permute-start(bf16[2,2,128,128]{3,2,1,0:T(8,128)(2,1)S(1)} %get-tuple-element.1888), channel_id=1, source_target_pairs={{0,8},{8,16},{16,24},{1,9},{9,17},{17,25},{2,10},{10,18},{18,26},{... | collective-permute-start | bytes 393224 | tf_op jit(solution)/shard_map/while/body/eval_jaxpr/ppermute | solution.py:12
  93.0 5.7 %collective-permute-start = (bf16[2,2,128,128]{3,2,1,0:T(8,128)(2,1)S(1)}, bf16[2,2,128,128]{3,2,1,0:T(8,128)(2,1)S(1)}, u32[]{:S(2)}, u32[]{:S(2)}) collective-permute-start(bf16[2,2,128,128]{3,2,1,0:T(8,128)(2,1)S(1)} %get-tuple-element.1888), channel_id=1, source_target_pairs={{0,8},{8,16},{16,24},{1,9},{9,17},{17,25},{2,10},{10,18},{18,26},{... | collective-permute-start | bytes 393224 | tf_op jit(solution)/shard_map/while/body/eval_jaxpr/ppermute | solution.py:12
  99.6 14.4 %collective-permute-start = (bf16[2,2,128,128]{3,2,1,0:T(8,128)(2,1)S(1)}, bf16[2,2,128,128]{3,2,1,0:T(8,128)(2,1)S(1)}, u32[]{:S(2)}, u32[]{:S(2)}) collective-permute-start(bf16[2,2,128,128]{3,2,1,0:T(8,128)(2,1)S(1)} %get-tuple-element.1888), channel_id=1, source_target_pairs={{0,8},{8,16},{16,24},{1,9},{9,17},{17,25},{2,10},{10,18},{18,26},{... | collective-permute-start | bytes 393224 | tf_op jit(solution)/shard_map/while/body/eval_jaxpr/ppermute | solution.py:12
  114.8 5.7 %collective-permute-start = (bf16[2,2,128,128]{3,2,1,0:T(8,128)(2,1)S(1)}, bf16[2,2,128,128]{3,2,1,0:T(8,128)(2,1)S(1)}, u32[]{:S(2)}, u32[]{:S(2)}) collective-permute-start(bf16[2,2,128,128]{3,2,1,0:T(8,128)(2,1)S(1)} %get-tuple-element.1888), channel_id=1, source_target_pairs={{0,8},{8,16},{16,24},{1,9},{9,17},{17,25},{2,10},{10,18},{18,26},{... | collective-permute-start | bytes 393224 | tf_op jit(solution)/shard_map/while/body/eval_jaxpr/ppermute | solution.py:12
  121.4 12.6 %collective-permute-start = (bf16[2,2,128,128]{3,2,1,0:T(8,128)(2,1)S(1)}, bf16[2,2,128,128]{3,2,1,0:T(8,128)(2,1)S(1)}, u32[]{:S(2)}, u32[]{:S(2)}) collective-permute-start(bf16[2,2,128,128]{3,2,1,0:T(8,128)(2,1)S(1)} %get-tuple-element.1888), channel_id=1, source_target_pairs={{0,8},{8,16},{16,24},{1,9},{9,17},{17,25},{2,10},{10,18},{18,26},{... | collective-permute-start | bytes 393224 | tf_op jit(solution)/shard_map/while/body/eval_jaxpr/ppermute | solution.py:12
  134.8 6.5 %collective-permute-start = (bf16[2,2,128,128]{3,2,1,0:T(8,128)(2,1)S(1)}, bf16[2,2,128,128]{3,2,1,0:T(8,128)(2,1)S(1)}, u32[]{:S(2)}, u32[]{:S(2)}) collective-permute-start(bf16[2,2,128,128]{3,2,1,0:T(8,128)(2,1)S(1)} %get-tuple-element.1888), channel_id=1, source_target_pairs={{0,8},{8,16},{16,24},{1,9},{9,17},{17,25},{2,10},{10,18},{18,26},{... | collective-permute-start | bytes 393224 | tf_op jit(solution)/shard_map/while/body/eval_jaxpr/ppermute | solution.py:12
  141.3 1.3 copy-start
  149.1 12.2 %collective-permute-start.1 = (bf16[2,2,128,128]{3,2,1,0:T(8,128)(2,1)S(1)}, bf16[2,2,128,128]{3,2,1,0:T(8,128)(2,1)S(1)}, u32[]{:S(2)}, u32[]{:S(2)}) collective-permute-start(bf16[2,2,128,128]{3,2,1,0:T(8,128)(2,1)S(1)} %get-tuple-element.1908), channel_id=1, source_target_pairs={{8,0},{16,8},{24,16},{9,1},{17,9},{25,17},{10,2},{18,10},{26,18},{... | collective-permute-start | bytes 393224 | tf_op jit(solution)/shard_map/while/body/eval_jaxpr/ppermute | solution.py:12
  162.2 8.2 %collective-permute-start.1 = (bf16[2,2,128,128]{3,2,1,0:T(8,128)(2,1)S(1)}, bf16[2,2,128,128]{3,2,1,0:T(8,128)(2,1)S(1)}, u32[]{:S(2)}, u32[]{:S(2)}) collective-permute-start(bf16[2,2,128,128]{3,2,1,0:T(8,128)(2,1)S(1)} %get-tuple-element.1908), channel_id=1, source_target_pairs={{8,0},{16,8},{24,16},{9,1},{17,9},{25,17},{10,2},{18,10},{26,18},{... | collective-permute-start | bytes 393224 | tf_op jit(solution)/shard_map/while/body/eval_jaxpr/ppermute | solution.py:12
  171.2 55.6 %collective-permute-start.1 = (bf16[2,2,128,128]{3,2,1,0:T(8,128)(2,1)S(1)}, bf16[2,2,128,128]{3,2,1,0:T(8,128)(2,1)S(1)}, u32[]{:S(2)}, u32[]{:S(2)}) collective-permute-start(bf16[2,2,128,128]{3,2,1,0:T(8,128)(2,1)S(1)} %get-tuple-element.1908), channel_id=1, source_target_pairs={{8,0},{16,8},{24,16},{9,1},{17,9},{25,17},{10,2},{18,10},{26,18},{... | collective-permute-start | bytes 393224 | tf_op jit(solution)/shard_map/while/body/eval_jaxpr/ppermute | solution.py:12
  236.4 5.8 %collective-permute-start.1 = (bf16[2,2,128,128]{3,2,1,0:T(8,128)(2,1)S(1)}, bf16[2,2,128,128]{3,2,1,0:T(8,128)(2,1)S(1)}, u32[]{:S(2)}, u32[]{:S(2)}) collective-permute-start(bf16[2,2,128,128]{3,2,1,0:T(8,128)(2,1)S(1)} %get-tuple-element.1908), channel_id=1, source_target_pairs={{8,0},{16,8},{24,16},{9,1},{17,9},{25,17},{10,2},{18,10},{26,18},{... | collective-permute-start | bytes 393224 | tf_op jit(solution)/shard_map/while/body/eval_jaxpr/ppermute | solution.py:12
  251.7 5.7 %collective-permute-start.1 = (bf16[2,2,128,128]{3,2,1,0:T(8,128)(2,1)S(1)}, bf16[2,2,128,128]{3,2,1,0:T(8,128)(2,1)S(1)}, u32[]{:S(2)}, u32[]{:S(2)}) collective-permute-start(bf16[2,2,128,128]{3,2,1,0:T(8,128)(2,1)S(1)} %get-tuple-element.1908), channel_id=1, source_target_pairs={{8,0},{16,8},{24,16},{9,1},{17,9},{25,17},{10,2},{18,10},{26,18},{... | collective-permute-start | bytes 393224 | tf_op jit(solution)/shard_map/while/body/eval_jaxpr/ppermute | solution.py:12
  266.9 5.7 %collective-permute-start.1 = (bf16[2,2,128,128]{3,2,1,0:T(8,128)(2,1)S(1)}, bf16[2,2,128,128]{3,2,1,0:T(8,128)(2,1)S(1)}, u32[]{:S(2)}, u32[]{:S(2)}) collective-permute-start(bf16[2,2,128,128]{3,2,1,0:T(8,128)(2,1)S(1)} %get-tuple-element.1908), channel_id=1, source_target_pairs={{8,0},{16,8},{24,16},{9,1},{17,9},{25,17},{10,2},{18,10},{26,18},{... | collective-permute-start | bytes 393224 | tf_op jit(solution)/shard_map/while/body/eval_jaxpr/ppermute | solution.py:12
  273.5 5.7 %collective-permute-start.1 = (bf16[2,2,128,128]{3,2,1,0:T(8,128)(2,1)S(1)}, bf16[2,2,128,128]{3,2,1,0:T(8,128)(2,1)S(1)}, u32[]{:S(2)}, u32[]{:S(2)}) collective-permute-start(bf16[2,2,128,128]{3,2,1,0:T(8,128)(2,1)S(1)} %get-tuple-element.1908), channel_id=1, source_target_pairs={{8,0},{16,8},{24,16},{9,1},{17,9},{25,17},{10,2},{18,10},{26,18},{... | collective-permute-start | bytes 393224 | tf_op jit(solution)/shard_map/while/body/eval_jaxpr/ppermute | solution.py:12
  301.3 36.4 %collective-permute-start.3 = (bf16[2,1,128,256]{3,2,1,0:T(8,128)(2,1)S(1)}, bf16[2,1,128,256]{3,2,1,0:T(8,128)(2,1)S(1)}, u32[]{:S(2)}, u32[]{:S(2)}) collective-permute-start(bf16[2,1,128,256]{3,2,1,0:T(8,128)(2,1)S(1)} %slice.228), channel_id=1, source_target_pairs={{0,1},{1,2},{2,3},{3,4},{4,5},{5,6},{6,7},{8,9},{9,10},{10,11},{11... | collective-permute-start | bytes 393224 | tf_op jit(solution)/shard_map/ppermute | solution.py:12
where the time goes:
time: 341 us; the launch traced here: 338 us
  waiting for transfers between devices  106 us (31%)
  starting transfers between devices  86.1 us (25%)
  local copies, waits for them, and re-layouts  50.3 us (15%)
  matrix products  39.7 us (12%)
  between operations  30.5 us (9%)
  other arithmetic  14.3 us (4%)
  loops' own time  11.4 us (3%)
    ppermute x16, waiting for transfers between devices, shifted_2(): return lax.ppermute(value, axis, pairs)  106 us
    ppermute x16, starting transfers between devices, shifted_2(): return lax.ppermute(value, axis, pairs)  86.1 us
    dot_general x48, matrix products, right_product(): jnp.einsum('...mn,nk->...mk', field, matrix, precision=lax.Precision.HIGH...  23.5 us
    dynamic_update_slice x8, local copies, waits for them, and re-layouts, on_device(): grad_ext = lax.dynamic_update_slice(grad_ext, current + piece, place)  18.9 us
    dot_general x48, matrix products, left_product(): jnp.einsum('mn,...nk->...mk', matrix, field, precision=lax.Precision.HIGH...  16.2 us
    gather x24, local copies, waits for them, and re-layouts  15.9 us
  transfers between devices with their start and end apart: 16, of which 15 were waited for; matrix products, arithmetic and copies ran while one was open for 0% of the time, Pallas kernels for 0%

commit v1 on v0

v1 whole, which is shorter than its diff:
```python
import functools
import math

import jax
import jax.numpy as jnp
import ml_dtypes
import numpy as np
from jax import lax
from jax.experimental import pallas as pl
from jax.experimental.pallas import tpu as pltpu
from jax.sharding import PartitionSpec as P

AXES = ("beam", "lat")


def matrices(order):
    index = np.arange(order)
    dft = np.exp(-2j * np.pi * (index[:, None] * index[None, :] % order) / order) / math.sqrt(order)
    freq = (index + order // 2) % order - order // 2
    phase = np.exp(-1j * np.pi * (freq * freq % (4 * order)) / (2 * order))
    prop = (dft.conj() * phase) @ dft
    parts = np.stack([prop.real, prop.imag, dft.real, dft.imag])
    high = parts.astype(ml_dtypes.bfloat16)
    low = (parts - high.astype(np.float64)).astype(ml_dtypes.bfloat16)
    return np.stack([high, low])


def place(n, lats, slice_index):
    first, second = n // 2 - 1, n // 2
    mirror = n - 1 - slice_index
    to = {slice_index: first, mirror: second}
    if slice_index not in (first, second):
        to[first] = min(slice_index, mirror)
        to[second] = max(slice_index, mirror)
    pairs = []
    for b in range(n):
        for l in range(lats):
            goal = to.get(b, b)
            if goal == second:
                spot = (goal, (l - 1) % lats)
            elif goal == b:
                spot = (goal, l ^ 1)
            else:
                spot = (goal, l)
            pairs.append((b * lats + l, spot[0] * lats + spot[1]))
    return pairs


def swap(n, lats):
    return [(b * lats + l, b * lats + (l ^ 1)) for b in range(n) for l in range(lats)]


def kernel(
    n, lats, slots, mine_ref, near_ref, mats_ref, own_ref, other_ref, probe_ref, meas_ref, near_meas_ref,
    keep_ref, send_ref, full_ref, trn_ref, psi_ref,
):
    order = probe_ref.shape[-1]
    tile = own_ref.shape[2]
    half = slots // 2
    first, second = n // 2 - 1, n // 2
    group = lax.axis_index("beam")
    lat = lax.axis_index("lat")
    side = lax.rem(lat, 2)
    at_first = group == first
    at_second = group == second
    base = jnp.where(at_first, lat - side, lat + 1 - side)
    local = base == lat
    beyond = base + 1 >= lats

    def scalar(i):
        return jnp.where(local, mine_ref[i], near_ref[i])

    slot_of = [side * half + s for s in range(half)]
    xs = [scalar(slot_of[s]) for s in range(half)]
    ys = [scalar(slots + slot_of[s]) for s in range(half)]
    count = scalar(2 * slots)

    for h in range(2):
        for m in range(2):
            re, im = mats_ref[h, 2 * m], mats_ref[h, 2 * m + 1]
            full_ref[h, 2 * m, :order, :order] = re
            full_ref[h, 2 * m, :order, order:] = -im
            full_ref[h, 2 * m, order:, :order] = im
            full_ref[h, 2 * m, order:, order:] = re
            full_ref[h, 2 * m + 1, :order, :order] = re
            full_ref[h, 2 * m + 1, :order, order:] = im
            full_ref[h, 2 * m + 1, order:, :order] = -im
            full_ref[h, 2 * m + 1, order:, order:] = re

    lane = lax.broadcasted_iota(jnp.int32, (order, order), 1)

    def stacked(k):
        return jnp.where(at_second, n - 1 - k, k)

    def column(axis, shape):
        index = lax.broadcasted_iota(jnp.int32, shape, axis)
        other_side = jnp.where(index >= tile, 1 - side, side)
        return jnp.where(index >= tile, index - tile, index) + other_side * tile

    wide, tall = (order, 2 * tile), (2 * tile, order)
    last = jnp.where(beyond, tile, 2 * tile)
    from_col = column(1, wide)
    cut_at = jnp.where(from_col < last, from_col - lax.broadcasted_iota(jnp.int32, wide, 0), -1)
    cuts = jnp.concatenate([jnp.where(cut_at == x, 1.0, 0.0) for x in xs], axis=0).astype(jnp.bfloat16)
    put_at = column(0, tall) - lax.broadcasted_iota(jnp.int32, tall, 1)
    puts = jnp.concatenate([jnp.where(put_at == x, 1.0, 0.0) for x in xs], axis=1).astype(jnp.bfloat16)

    def dot(a, b):
        return jnp.dot(a, b, preferred_element_type=jnp.float32)

    def cut(k, c):
        i = stacked(k)
        own, other = own_ref[i, c], other_ref[i, c]
        if k == first:
            own, other = jnp.where(at_first, other, own), jnp.where(at_first, own, other)
        blocks = dot(cuts, jnp.concatenate([own, other], axis=0))
        out = []
        for s in range(half):
            rows = slice(s * order, (s + 1) * order)
            turn = lax.rem(order - ys[s], order)
            left = pltpu.roll(blocks[rows, :order], turn, 1)
            right = pltpu.roll(blocks[rows, order:], turn, 1)
            out.append(jnp.where(lane < order - ys[s], left, right))
        return out

    def put(k, c, values):
        rows = []
        for s, value in enumerate(values):
            value = pltpu.roll(value, lax.rem(ys[s], order), 1)
            rows.append(
                jnp.concatenate(
                    [jnp.where(lane >= ys[s], value, 0.0), jnp.where(lane < ys[s], value, 0.0)], axis=1
                ).astype(jnp.bfloat16)
            )
        total = dot(puts, jnp.concatenate(rows, axis=0))
        i = stacked(k)
        keep_ref[i, c] = total[:tile]
        send_ref[i, c] = total[tile:].astype(jnp.bfloat16)

    def sandwich(pair, m, conj):
        right = 2 * m + (0 if conj else 1)
        left = 2 * m + (1 if conj else 0)
        rows = jnp.concatenate([jnp.concatenate(w, axis=1) for w in pair], axis=0).astype(jnp.bfloat16)
        y = dot(rows, full_ref[0, right]) + dot(rows, full_ref[1, right])
        y = y.astype(jnp.bfloat16)
        cols = jnp.concatenate(
            [
                jnp.concatenate([y[:order, :order], y[order:, :order]], axis=1),
                jnp.concatenate([y[:order, order:], y[order:, order:]], axis=1),
            ],
            axis=0,
        )
        z = dot(full_ref[0, left], cols) + dot(full_ref[1, left], cols)
        return [(z[:order, :order], z[order:, :order]), (z[:order, order:], z[order:, order:])]

    pairs = [(s, s + 1) for s in range(0, half, 2)]
    waves = [[(probe_ref[0], probe_ref[1])] * 2 for _ in pairs]
    for k in range(n):
        cut_re, cut_im = cut(k, 0), cut(k, 1)
        for j, pair in enumerate(pairs):
            mult = []
            for q, s in enumerate(pair):
                re, im = waves[j][q]
                psi_ref[k, s, 0] = re
                psi_ref[k, s, 1] = im
                t_re, t_im = 1.0 + cut_re[s], cut_im[s]
                trn_ref[k, s, 0] = t_re
                trn_ref[k, s, 1] = t_im
                mult.append((t_re * re - t_im * im, t_re * im + t_im * re))
            waves[j] = sandwich(mult, 0 if k < n - 1 else 1, False)

    back = [None] * len(pairs)
    for j, pair in enumerate(pairs):
        scaled = []
        for q, s in enumerate(pair):
            re, im = waves[j][q]
            slot = slot_of[s]
            seen = jnp.where(local, meas_ref[slot], near_meas_ref[slot])
            misfit = jnp.where(slot < count, re * re + im * im - seen, 0.0)
            scaled.append((misfit * re, misfit * im))
        back[j] = sandwich(scaled, 1, True)
    for k in reversed(range(n)):
        grad_re, grad_im = [], []
        for j, pair in enumerate(pairs):
            mult = []
            for q, s in enumerate(pair):
                re, im = back[j][q]
                p_re, p_im = psi_ref[k, s, 0], psi_ref[k, s, 1]
                grad_re.append(p_re * re + p_im * im)
                grad_im.append(p_re * im - p_im * re)
                if k > 0:
                    t_re, t_im = trn_ref[k, s, 0], trn_ref[k, s, 1]
                    mult.append((t_re * re + t_im * im, t_re * im - t_im * re))
            if k > 0:
                back[j] = sandwich(mult, 0, True)
        put(k, 0, grad_re)
        put(k, 1, grad_im)


def on_device(contrast, probe, offset_x, offset_y, probe_count, measured):
    n, lats = lax.axis_size("beam"), lax.axis_size("lat")
    order, tile, height = probe.shape[1], contrast.shape[2], contrast.shape[3]
    slots = offset_x.shape[0]
    half = slots // 2
    first, second = n // 2 - 1, n // 2
    lat, group = lax.axis_index("lat"), lax.axis_index("beam")
    routes = [place(n, lats, a) for a in range(n)]
    turn = sorted(range(n), key=lambda a: (a in (first, second), a in (second,), a))
    partner = swap(n, lats)

    mine = jnp.concatenate([offset_x, offset_y, probe_count])
    near = lax.ppermute(mine, AXES, partner)
    near_measured = lax.ppermute(measured, AXES, partner)
    own_tile = contrast[:, 0].astype(jnp.bfloat16)[None]
    arrived = {a: lax.ppermute(own_tile, AXES, routes[a]) for a in turn}
    own = jnp.concatenate([arrived[a] for a in range(n)], axis=0)
    other = lax.ppermute(own, AXES, partner)

    smem = pl.BlockSpec(memory_space=pltpu.SMEM)
    vmem = pl.BlockSpec(memory_space=pltpu.VMEM)
    mats = jnp.asarray(matrices(order))
    tiles = (n, 2, tile, height)
    keep, send = pl.pallas_call(
        functools.partial(kernel, n, lats, slots),
        out_shape=(jax.ShapeDtypeStruct(tiles, jnp.float32), jax.ShapeDtypeStruct(tiles, jnp.bfloat16)),
        in_specs=[smem, smem] + [vmem] * 6,
        out_specs=(vmem, vmem),
        scratch_shapes=[
            pltpu.VMEM((2, 4, 2 * order, 2 * order), jnp.bfloat16),
            pltpu.VMEM((n, half, 2, order, order), jnp.float32),
            pltpu.VMEM((n, half, 2, order, order), jnp.float32),
        ],
        compiler_params=pltpu.CompilerParams(vmem_limit_bytes=(16 + 2 * n) << 20),
    )(mine, near, mats, own, other, probe, measured, near_measured)

    from_partner = lax.ppermute(send, AXES, partner)
    totals = [(keep[i] + from_partner[i].astype(jnp.float32)).astype(jnp.bfloat16) for i in range(n)]
    returned = {a: lax.ppermute(totals[a], AXES, [(d, s) for s, d in routes[a]]) for a in turn}
    from_first = totals[first]
    from_second = returned[n - 1]
    for g in range(n):
        if g != first:
            from_first = jnp.where(group == g, returned[g], from_first)
        from_second = jnp.where(group == g, returned[n - 1 - g], from_second)
    from_second = jnp.where(lat == 0, 0.0, from_second.astype(jnp.float32))
    return (from_first.astype(jnp.float32) + from_second)[:, None]


def solution(mesh):
    in_specs = (
        P(None, "beam", "lat", None),
        P(),
        P("lat"),
        P("lat"),
        P("lat"),
        P("lat", None, None),
    )
    out_specs = P(None, "beam", "lat", None)
    return jax.shard_map(
        on_device, mesh=mesh, in_specs=in_specs, out_specs=out_specs, check_vma=False
    )
```

time: 341 us -> 35.2 us (0.10)
  the two profiles are of different devices: /device:TPU:5 before, /device:TPU:0 now
where the time goes in v1:
time: 35.2 us; the launch traced here: 35.1 us
  waiting for transfers between devices  14.4 us (41%)
  starting transfers between devices  11.7 us (33%)
  Pallas kernels  6.17 us (18%)
  other arithmetic  1.99 us (6%)
  between operations  0.79 us (2%)
    ppermute x4, waiting for transfers between devices, on_device(): lax.ppermute(totals[a], AXES, [(d, s) for s, d in routes[a]])  8.08 us
    ppermute x4, starting transfers between devices, on_device(): arrived = {a: lax.ppermute(own_tile, AXES, routes[a]) for a in turn}  7.7 us
    pallas_call x1, Pallas kernels, on_device(): pl.pallas_call(functools.partial(kernel, n, lats, slots), out_shape=(jax....  6.17 us
    ppermute x4, waiting for transfers between devices, on_device(): arrived = {a: lax.ppermute(own_tile, AXES, routes[a]) for a in turn}  3.85 us
    ppermute x4, starting transfers between devices, on_device(): lax.ppermute(totals[a], AXES, [(d, s) for s, d in routes[a]])  3.02 us
    ppermute x1, waiting for transfers between devices, on_device(): from_partner = lax.ppermute(send, AXES, partner)  1.61 us
    convert_element_type x1, other arithmetic, on_device(): own_tile = contrast[:, 0].astype(jnp.bfloat16)[None]  0.96 us
    ppermute x1, waiting for transfers between devices, on_device(): near = lax.ppermute(mine, AXES, partner)  0.82 us
  transfers between devices with their start and end apart: 12, of which 5 were waited for; matrix products, arithmetic and copies ran while one was open for 0% of the time, Pallas kernels for 0%

profile of v1, /device:TPU:0, one launch (start us, length us, event | category | flops | bytes accessed | tf_op | source)
XLA Modules:
  0.0 35.1 jit_solution(13748254879483008518)
XLA Ops:
  0.0 1.0 %fusion.4 = bf16[1,2,128,256]{3,2,1,0:T(8,128)(2,1)S(1)} fusion(f32[2,1,128,256]{3,2,1,0:T(8,128)} %param.7), kind=kLoop, calls=%fused_computation.10 | loop fusion | flops 65536 | bytes 393216 | tf_op jit(solution)/shard_map/convert_element_type | solution.py:214
  1.0 0.0 copy-start
  1.0 3.1 %collective-permute-start.1 = (bf16[1,2,128,256]{3,2,1,0:T(8,128)(2,1)S(1)}, bf16[1,2,128,256]{3,2,1,0:T(8,128)(2,1)S(1)}, u32[]{:S(2)}, u32[]{:S(2)}) collective-permute-start(bf16[1,2,128,256]{3,2,1,0:T(8,128)(2,1)S(1)} %fusion.4), channel_id=1, source_target_pairs={{0,8},{1,9},{2,10},{3,11},{4,12},{5,13},{6,14},{7,15},{8,0},{9,1},... | collective-permute-start | bytes 393224 | tf_op jit(solution)/shard_map/ppermute | solution.py:215
  4.0 0.0 collective-permute-start.2
  4.0 0.5 %collective-permute-start.3 = (bf16[1,2,128,256]{3,2,1,0:T(8,128)(2,1)S(1)}, bf16[1,2,128,256]{3,2,1,0:T(8,128)(2,1)S(1)}, u32[]{:S(2)}, u32[]{:S(2)}) collective-permute-start(bf16[1,2,128,256]{3,2,1,0:T(8,128)(2,1)S(1)} %fusion.4), channel_id=1, source_target_pairs={{0,1},{1,0},{2,3},{3,2},{4,5},{5,4},{6,7},{7,6},{8,23},{9,16},{10,... | collective-permute-start | bytes 393224 | tf_op jit(solution)/shard_map/ppermute | solution.py:215
  4.6 4.1 %collective-permute-start.4 = (bf16[1,2,128,256]{3,2,1,0:T(8,128)(2,1)S(1)}, bf16[1,2,128,256]{3,2,1,0:T(8,128)(2,1)S(1)}, u32[]{:S(2)}, u32[]{:S(2)}) collective-permute-start(bf16[1,2,128,256]{3,2,1,0:T(8,128)(2,1)S(1)} %fusion.4), channel_id=1, source_target_pairs={{0,23},{1,16},{2,17},{3,18},{4,19},{5,20},{6,21},{7,22},{8,0},{9,1... | collective-permute-start | bytes 393224 | tf_op jit(solution)/shard_map/ppermute | solution.py:215
  8.7 0.0 collective-permute-start.6
  8.7 0.0 collective-permute-done.1
  8.7 0.0 collective-permute-done.2
  8.7 0.0 copy-start.1
  8.7 0.0 collective-permute-done.3
  8.8 0.0 copy-start.2
  8.8 3.8 %collective-permute-done.4 = bf16[1,2,128,256]{3,2,1,0:T(8,128)(2,1)S(1)} collective-permute-done((bf16[1,2,128,256]{3,2,1,0:T(8,128)(2,1)S(1)}, bf16[1,2,128,256]{3,2,1,0:T(8,128)(2,1)S(1)}, u32[]{:S(2)}, u32[]{:S(2)}) %collective-permute-start.4) | collective-permute-done | bytes 131104 | tf_op jit(solution)/shard_map/ppermute | solution.py:215
  12.6 0.0 copy-start.3
  12.6 0.0 copy-start.4
  12.7 0.1 collective-permute-start.5
  13.4 0.1 pad_add_fusion.mine_ref
  13.5 0.5 %collective-permute-start = (s32[17]{0:T(128)S(1)}, s32[17]{0:T(128)S(1)}, u32[]{:S(2)}, u32[]{:S(2)}) collective-permute-start(s32[17]{0:T(128)S(1)} %pad_add_fusion.mine_ref), channel_id=1, source_target_pairs={{0,1},{1,0},{2,3},{3,2},{4,5},{5,4},{6,7},{7,6},{8,9},{9,8},{10,11... | collective-permute-start | bytes 212 | tf_op jit(solution)/shard_map/ppermute | solution.py:212
  14.0 0.8 %collective-permute-done.near_ref = s32[17]{0:T(128)S(1)} collective-permute-done((s32[17]{0:T(128)S(1)}, s32[17]{0:T(128)S(1)}, u32[]{:S(2)}, u32[]{:S(2)}) %collective-permute-start) | collective-permute-done | bytes 100 | tf_op jit(solution)/shard_map/ppermute | solution.py:212
  14.8 0.0 collective-permute-done.6.near_meas_ref
  14.8 0.0 collective-permute-done.5.other_ref
  14.8 6.2 %shard_map.73 = (f32[4,2,128,256]{3,2,1,0:T(8,128)S(1)}, bf16[4,2,128,256]{3,2,1,0:T(8,128)(2,1)S(1)}) custom-call(s32[17]{0:T(128)S(1)} %pad_add_fusion.mine_ref, s32[17]{0:T(128)S(1)} %collective-permute-done.near_ref, bf16[2,4,128,128]{3,2,1,0:T(8,128)(2,1)S(1)} %copy-done.1, bf16[4,2,128,256]{3,2,1,0:T(8,128)(2,1)S(1)} %constant_dynamic-update-slice_fusion.own_ref, ...), custom_call_target="tpu_custom_call" | custom-call | tf_op jit(solution)/shard_map/pallas_call | solution.py:223
  21.0 0.4 %collective-permute-start.7 = (bf16[4,2,128,256]{3,2,1,0:T(8,128)(2,1)S(1)}, bf16[4,2,128,256]{3,2,1,0:T(8,128)(2,1)S(1)}, u32[]{:S(2)}, u32[]{:S(2)}) collective-permute-start(bf16[4,2,128,256]{3,2,1,0:T(8,128)(2,1)S(1)} %get-tuple-element.8), channel_id=1, source_target_pairs={{0,1},{1,0},{2,3},{3,2},{4,5},{5,4},{6,7},{7,6},{8,9},{9,8},{10,11... | collective-permute-start | bytes 1572872 | tf_op jit(solution)/shard_map/ppermute | solution.py:236
  21.4 1.6 %collective-permute-done.7 = bf16[4,2,128,256]{3,2,1,0:T(8,128)(2,1)S(1)} collective-permute-done((bf16[4,2,128,256]{3,2,1,0:T(8,128)(2,1)S(1)}, bf16[4,2,128,256]{3,2,1,0:T(8,128)(2,1)S(1)}, u32[]{:S(2)}, u32[]{:S(2)}) %collective-permute-start.7) | collective-permute-done | bytes 524320 | tf_op jit(solution)/shard_map/ppermute | solution.py:236
  23.0 0.2 fusion
  23.2 0.3 collective-permute-start.11
  23.5 2.6 %collective-permute-start.10 = (bf16[2,128,256]{2,1,0:T(8,128)(2,1)S(1)}, bf16[2,128,256]{2,1,0:T(8,128)(2,1)S(1)}, u32[]{:S(2)}, u32[]{:S(2)}) collective-permute-start(bf16[2,128,256]{2,1,0:T(8,128)(2,1)S(1)} %get-tuple-element.11), channel_id=1, source_target_pairs={{8,0},{9,1},{10,2},{11,3},{12,4},{13,5},{14,6},{15,7},{0,8},{1,9},... | collective-permute-start | bytes 393224 | tf_op jit(solution)/shard_map/ppermute | solution.py:238
  26.2 0.0 collective-permute-start.8
  26.2 3.8 %collective-permute-done.10 = bf16[2,128,256]{2,1,0:T(8,128)(2,1)S(1)} collective-permute-done((bf16[2,128,256]{2,1,0:T(8,128)(2,1)S(1)}, bf16[2,128,256]{2,1,0:T(8,128)(2,1)S(1)}, u32[]{:S(2)}, u32[]{:S(2)}) %collective-permute-start.10) | collective-permute-done | bytes 131104 | tf_op jit(solution)/shard_map/ppermute | solution.py:238
  30.0 4.2 %collective-permute-done.8 = bf16[2,128,256]{2,1,0:T(8,128)(2,1)S(1)} collective-permute-done((bf16[2,128,256]{2,1,0:T(8,128)(2,1)S(1)}, bf16[2,128,256]{2,1,0:T(8,128)(2,1)S(1)}, u32[]{:S(2)}, u32[]{:S(2)}) %collective-permute-start.8) | collective-permute-done | bytes 131104 | tf_op jit(solution)/shard_map/ppermute | solution.py:238
  34.3 0.0 collective-permute-done.9
  34.3 0.8 %add_bitcast_fusion = f32[2,1,128,256]{3,2,1,0:T(8,128)} fusion(bf16[2,128,256]{2,1,0:T(8,128)(2,1)S(1)} %collective-permute-done.10, bf16[2,128,256]{2,1,0:T(8,128)(2,1)S(1)} %collective-permute-done.11, bf16[2,128,256]{2,1,0:T(8,128)(2,1)S(1)} %collective-permute-done.9, bf16[2,128,256]{2,1,0:T(8,128)(2,1)S(1)} %collective-permute-done.8, ...), kind=kLoop, calls=%fused_computation.1 | loop fusion | flops 655360 | bytes 917509 | tf_op jit(solution)/shard_map/broadcast_in_dim | solution.py:246
  (11 shorter events, 0.1 us)
Async XLA Ops:
  1.0 13.9 %copy-start = (f32[8,128,128]{2,1,0:T(8,128)S(1)}, f32[8,128,128]{2,1,0:T(8,128)}, u32[]{:S(2)}) copy-start(f32[8,128,128]{2,1,0:T(8,128)} %meas_ref.1) | copy-start | bytes 1572868
  1.0 7.7 %collective-permute-start.1 = (bf16[1,2,128,256]{3,2,1,0:T(8,128)(2,1)S(1)}, bf16[1,2,128,256]{3,2,1,0:T(8,128)(2,1)S(1)}, u32[]{:S(2)}, u32[]{:S(2)}) collective-permute-start(bf16[1,2,128,256]{3,2,1,0:T(8,128)(2,1)S(1)} %fusion.4), channel_id=1, source_target_pairs={{0,8},{1,9},{2,10},{3,11},{4,12},{5,13},{6,14},{7,15},{8,0},{9,1},... | collective-permute-start | bytes 393224 | tf_op jit(solution)/shard_map/ppermute | solution.py:215
  4.0 4.7 %collective-permute-start.2 = (bf16[1,2,128,256]{3,2,1,0:T(8,128)(2,1)S(1)}, bf16[1,2,128,256]{3,2,1,0:T(8,128)(2,1)S(1)}, u32[]{:S(2)}, u32[]{:S(2)}) collective-permute-start(bf16[1,2,128,256]{3,2,1,0:T(8,128)(2,1)S(1)} %fusion.4), channel_id=1, source_target_pairs={{0,1},{1,0},{2,3},{3,2},{4,5},{5,4},{6,7},{7,6},{8,9},{9,8},{10,11... | collective-permute-start | bytes 393224 | tf_op jit(solution)/shard_map/ppermute | solution.py:215
  4.0 4.7 %collective-permute-start.3 = (bf16[1,2,128,256]{3,2,1,0:T(8,128)(2,1)S(1)}, bf16[1,2,128,256]{3,2,1,0:T(8,128)(2,1)S(1)}, u32[]{:S(2)}, u32[]{:S(2)}) collective-permute-start(bf16[1,2,128,256]{3,2,1,0:T(8,128)(2,1)S(1)} %fusion.4), channel_id=1, source_target_pairs={{0,1},{1,0},{2,3},{3,2},{4,5},{5,4},{6,7},{7,6},{8,23},{9,16},{10,... | collective-permute-start | bytes 393224 | tf_op jit(solution)/shard_map/ppermute | solution.py:215
  4.6 8.1 %collective-permute-start.4 = (bf16[1,2,128,256]{3,2,1,0:T(8,128)(2,1)S(1)}, bf16[1,2,128,256]{3,2,1,0:T(8,128)(2,1)S(1)}, u32[]{:S(2)}, u32[]{:S(2)}) collective-permute-start(bf16[1,2,128,256]{3,2,1,0:T(8,128)(2,1)S(1)} %fusion.4), channel_id=1, source_target_pairs={{0,23},{1,16},{2,17},{3,18},{4,19},{5,20},{6,21},{7,22},{8,0},{9,1... | collective-permute-start | bytes 393224 | tf_op jit(solution)/shard_map/ppermute | solution.py:215
  8.7 6.1 %collective-permute-start.6 = (f32[8,128,128]{2,1,0:T(8,128)}, f32[8,128,128]{2,1,0:T(8,128)S(1)}, u32[]{:S(2)}, u32[]{:S(2)}) collective-permute-start(f32[8,128,128]{2,1,0:T(8,128)} %meas_ref.1), channel_id=1, source_target_pairs={{0,1},{1,0},{2,3},{3,2},{4,5},{5,4},{6,7},{7,6},{8,9},{9,8},{10,11... | collective-permute-start | bytes 1572872 | tf_op jit(solution)/shard_map/ppermute | solution.py:213
  8.7 6.1 %copy-start.1 = (bf16[2,4,128,128]{3,2,1,0:T(8,128)(2,1)S(1)}, bf16[2,4,128,128]{3,2,1,0:T(8,128)(2,1)}, u32[]{:S(2)}) copy-start(bf16[2,4,128,128]{3,2,1,0:T(8,128)(2,1)} %constant.20.clone.mats_ref) | copy-start | bytes 786436
  8.8 6.1 %copy-start.2 = (f32[2,128,128]{2,1,0:T(8,128)S(1)}, f32[2,128,128]{2,1,0:T(8,128)}, u32[]{:S(2)}) copy-start(f32[2,128,128]{2,1,0:T(8,128)} %probe_ref.1) | copy-start | bytes 393220
  12.6 0.8 %copy-start.3 = (s32[8]{0:T(128)S(1)}, s32[8]{0:T(128)}, u32[]{:S(2)}) copy-start(s32[8]{0:T(128)} %param.10) | copy-start | bytes 100
  12.6 0.8 %copy-start.4 = (s32[8]{0:T(128)S(1)}, s32[8]{0:T(128)}, u32[]{:S(2)}) copy-start(s32[8]{0:T(128)} %param.9) | copy-start | bytes 100
  12.7 2.2 %collective-permute-start.5 = (bf16[4,2,128,256]{3,2,1,0:T(8,128)(2,1)S(1)}, bf16[4,2,128,256]{3,2,1,0:T(8,128)(2,1)S(1)}, u32[]{:S(2)}, u32[]{:S(2)}) collective-permute-start(bf16[4,2,128,256]{3,2,1,0:T(8,128)(2,1)S(1)} %constant_dynamic-update-slice_fusion.own_ref), channel_id=1, source_target_pairs={{0,1},{1,0},{2,3},{3,2},{4,5},{5,4},{6,7},{7,6},{8,9},{9,8},{10,11... | collective-permute-start | bytes 1572872 | tf_op jit(solution)/shard_map/ppermute | solution.py:217
  13.5 1.3 %collective-permute-start = (s32[17]{0:T(128)S(1)}, s32[17]{0:T(128)S(1)}, u32[]{:S(2)}, u32[]{:S(2)}) collective-permute-start(s32[17]{0:T(128)S(1)} %pad_add_fusion.mine_ref), channel_id=1, source_target_pairs={{0,1},{1,0},{2,3},{3,2},{4,5},{5,4},{6,7},{7,6},{8,9},{9,8},{10,11... | collective-permute-start | bytes 212 | tf_op jit(solution)/shard_map/ppermute | solution.py:212
  21.0 2.0 %collective-permute-start.7 = (bf16[4,2,128,256]{3,2,1,0:T(8,128)(2,1)S(1)}, bf16[4,2,128,256]{3,2,1,0:T(8,128)(2,1)S(1)}, u32[]{:S(2)}, u32[]{:S(2)}) collective-permute-start(bf16[4,2,128,256]{3,2,1,0:T(8,128)(2,1)S(1)} %get-tuple-element.8), channel_id=1, source_target_pairs={{0,1},{1,0},{2,3},{3,2},{4,5},{5,4},{6,7},{7,6},{8,9},{9,8},{10,11... | collective-permute-start | bytes 1572872 | tf_op jit(solution)/shard_map/ppermute | solution.py:236
  23.2 3.0 %collective-permute-start.11 = (bf16[2,128,256]{2,1,0:T(8,128)(2,1)S(1)}, bf16[2,128,256]{2,1,0:T(8,128)(2,1)S(1)}, u32[]{:S(2)}, u32[]{:S(2)}) collective-permute-start(bf16[2,128,256]{2,1,0:T(8,128)(2,1)S(1)} %get-tuple-element.10), channel_id=1, source_target_pairs={{1,0},{0,1},{3,2},{2,3},{5,4},{4,5},{7,6},{6,7},{9,8},{8,9},{11,10... | collective-permute-start | bytes 393224 | tf_op jit(solution)/shard_map/ppermute | solution.py:238
  23.5 6.5 %collective-permute-start.10 = (bf16[2,128,256]{2,1,0:T(8,128)(2,1)S(1)}, bf16[2,128,256]{2,1,0:T(8,128)(2,1)S(1)}, u32[]{:S(2)}, u32[]{:S(2)}) collective-permute-start(bf16[2,128,256]{2,1,0:T(8,128)(2,1)S(1)} %get-tuple-element.11), channel_id=1, source_target_pairs={{8,0},{9,1},{10,2},{11,3},{12,4},{13,5},{14,6},{15,7},{0,8},{1,9},... | collective-permute-start | bytes 393224 | tf_op jit(solution)/shard_map/ppermute | solution.py:238
  26.2 8.1 %collective-permute-start.8 = (bf16[2,128,256]{2,1,0:T(8,128)(2,1)S(1)}, bf16[2,128,256]{2,1,0:T(8,128)(2,1)S(1)}, u32[]{:S(2)}, u32[]{:S(2)}) collective-permute-start(bf16[2,128,256]{2,1,0:T(8,128)(2,1)S(1)} %get-tuple-element.9), channel_id=1, source_target_pairs={{23,0},{16,1},{17,2},{18,3},{19,4},{20,5},{21,6},{22,7},{0,8},{1,9... | collective-permute-start | bytes 393224 | tf_op jit(solution)/shard_map/ppermute | solution.py:238
  26.2 8.1 %collective-permute-start.9 = (bf16[2,128,256]{2,1,0:T(8,128)(2,1)S(1)}, bf16[2,128,256]{2,1,0:T(8,128)(2,1)S(1)}, u32[]{:S(2)}, u32[]{:S(2)}) collective-permute-start(bf16[2,128,256]{2,1,0:T(8,128)(2,1)S(1)} %get-tuple-element.12), channel_id=1, source_target_pairs={{1,0},{0,1},{3,2},{2,3},{5,4},{4,5},{7,6},{6,7},{23,8},{16,9},{17,... | collective-permute-start | bytes 393224 | tf_op jit(solution)/shard_map/ppermute | solution.py:238

commit v2 on v1

v2 whole, which is shorter than its diff:
```python
import functools
import math

import jax
import jax.numpy as jnp
import ml_dtypes
import numpy as np
from jax import lax
from jax.experimental import pallas as pl
from jax.experimental.pallas import tpu as pltpu
from jax.sharding import PartitionSpec as P

AXES = ("beam", "lat")


W_SCALE = 1.1775


def matrices(order, steps):
    index = np.arange(order)
    dft = np.exp(-2j * np.pi * (index[:, None] * index[None, :] % order) / order) / math.sqrt(order)
    freq = (index + order // 2) % order - order // 2
    phase = np.exp(-1j * np.pi * (freq * freq % (4 * order)) / (2 * order))
    prop = (dft.conj() * phase) @ dft

    def pair(matrix):
        return np.stack([matrix.real, matrix.imag]).astype(ml_dtypes.bfloat16)

    def value(parts):
        parts = parts.astype(np.float64)
        return parts[0] + 1j * parts[1]

    out, ahead = [], np.zeros_like(prop)
    for step in range(steps):
        out.append(pair(prop - ahead))
        if step == steps - 1:
            out.append(pair(prop - ahead - value(out[-1])))
        else:
            ahead = ahead + value(out[-1]) - prop
    out.append(pair(W_SCALE * dft))
    return np.stack(out)


def place(n, lats, slice_index, short):
    first, second = n // 2 - 1, n // 2
    mirror = n - 1 - slice_index
    goals = {slice_index: first, mirror: second}
    outer = slice_index not in (first, second)
    if outer:
        goals[first] = min(slice_index, mirror)
        goals[second] = max(slice_index, mirror)
    to = {}
    for b in range(n):
        for l in range(lats):
            goal = goals.get(b, b)
            if goal == second:
                to[b, l] = (goal, (l - 1) % lats)
            else:
                to[b, l] = (goal, l ^ 1 if goal == b else l)
    if outer and short:
        via, middle = (first if goals[first] == mirror else second), lats // 4
        to[mirror, 0] = (mirror, middle)
        to[via, middle] = (second, lats - 1)
    return [(b * lats + l, c * lats + m) for (b, l), (c, m) in to.items()]


def swap(n, lats):
    return [(b * lats + l, b * lats + (l ^ 1)) for b in range(n) for l in range(lats)]


def turns(n, back):
    ends = [0, n - 1] if back else [n - 1, 0]
    return ends + list(range(1, n - 1))


def kernel(
    n, lats, slots, mine_ref, near_ref, mats_ref, own_ref, other_ref, probe_ref, meas_ref, near_meas_ref,
    keep_ref, send_ref, full_ref, trn_ref, psi_ref, ext_ref,
):
    order = probe_ref.shape[-1]
    tile = own_ref.shape[2]
    half = slots // 2
    first, second = n // 2 - 1, n // 2
    group = lax.axis_index("beam")
    lat = lax.axis_index("lat")
    side = lax.rem(lat, 2)
    at_first = group == first
    at_second = group == second
    base = jnp.where(at_first, lat - side, lat + 1 - side)
    local = base == lat
    beyond = base + 1 >= lats

    def scalar(i):
        return jnp.where(local, mine_ref[i], near_ref[i])

    slot_of = [side * half + s for s in range(half)]
    xs = [scalar(slot_of[s]) for s in range(half)]
    ys = [scalar(slots + slot_of[s]) for s in range(half)]
    count = scalar(2 * slots)

    for m in range(n + 1):
        re, im = mats_ref[m, 0], mats_ref[m, 1]
        for h, (upper, lower) in enumerate(((-im, im), (im, -im))):
            full_ref[m, h, :order, :order] = re
            full_ref[m, h, :order, order:] = upper
            full_ref[m, h, order:, :order] = lower
            full_ref[m, h, order:, order:] = re

    lane = lax.broadcasted_iota(jnp.int32, (order, order), 1)

    def spot(k, back):
        order = turns(n, back)
        return jnp.where(at_second, order.index(n - 1 - k), order.index(k))

    def column(axis, shape):
        index = lax.broadcasted_iota(jnp.int32, shape, axis)
        other_side = jnp.where(index >= tile, 1 - side, side)
        return jnp.where(index >= tile, index - tile, index) + other_side * tile

    tall = (2 * tile, order)
    put_at = column(0, tall) - lax.broadcasted_iota(jnp.int32, tall, 1)
    puts = jnp.concatenate([jnp.where(put_at == x, 1.0, 0.0) for x in xs], axis=1).astype(jnp.bfloat16)

    def dot(a, b):
        return jnp.dot(a, b, preferred_element_type=jnp.float32)

    for k in range(n):
        i = spot(k, False)
        row = jnp.where(at_first & (k == first), 1 - side, side)
        for ref, r in ((own_ref, row), (other_ref, 1 - row)):
            value = ref[i].astype(jnp.float32) * jnp.where(beyond & (r == 1), 0.0, 1.0)
            ext_ref[k, :, pl.ds(pl.multiple_of(r * tile, tile), tile), :] = value

    sub = lax.broadcasted_iota(jnp.int32, (order // 8, 8, order), 1)
    longer = lax.broadcasted_iota(jnp.int32, (order + 8, order), 1)

    def cut(k, c):
        out = []
        for s in range(half):
            turn = lax.rem(order - ys[s], order)
            start = pl.ds(pl.multiple_of(xs[s] // 8 * 8, 8), order + 8)
            left = pltpu.roll(ext_ref[k, c, start, :order], turn, 1)
            right = pltpu.roll(ext_ref[k, c, start, order:], turn, 1)
            w = jnp.where(longer < order - ys[s], left, right).reshape(order // 8 + 1, 8, order)
            r = lax.rem(xs[s], 8)
            w = pltpu.roll(w, lax.rem(8 - r, 8), 1)
            out.append(jnp.where(sub < 8 - r, w[:-1], w[1:]).reshape(order, order))
        return out

    def put(k, c, values):
        rows = []
        for s, value in enumerate(values):
            value = pltpu.roll(value, lax.rem(ys[s], order), 1)
            rows.append(
                jnp.concatenate(
                    [jnp.where(lane >= ys[s], value, 0.0), jnp.where(lane < ys[s], value, 0.0)], axis=1
                ).astype(jnp.bfloat16)
            )
        total = dot(puts, jnp.concatenate(rows, axis=0))
        i = spot(k, True)
        keep_ref[i, c] = total[:tile]
        send_ref[i, c] = total[tile:].astype(jnp.bfloat16)

    def sandwich(pairs, ms, conj):
        right, left = (0, 1) if conj else (1, 0)
        rows = [jnp.concatenate([jnp.concatenate(w, axis=1) for w in p], axis=0).astype(jnp.bfloat16) for p in pairs]
        ys = [sum(dot(r, full_ref[m, right]) for m in ms).astype(jnp.bfloat16) for r in rows]
        cols = [
            jnp.concatenate(
                [
                    jnp.concatenate([y[q * order : (q + 1) * order, c * order : (c + 1) * order] for q in range(1)], axis=1)
                    for c in range(2)
                ],
                axis=0,
            )
            for y in ys
        ]
        zs = [sum(dot(full_ref[m, left], c) for m in ms) for c in cols]
        return [[(z[:order, q * order : (q + 1) * order], z[order:, q * order : (q + 1) * order]) for q in range(1)] for z in zs]

    def step(i):
        return (n - 2, n - 1) if i == n - 2 else (i,)

    transform = (n,)
    pairs = [tuple(range(s, s + 1)) for s in range(0, half, 1)]
    waves = [[(probe_ref[0], probe_ref[1])] * 1 for _ in pairs]
    for k in range(n):
        cut_re, cut_im = cut(k, 0), cut(k, 1)
        mults = []
        for j, pair in enumerate(pairs):
            mult = []
            for q, s in enumerate(pair):
                re, im = waves[j][q]
                psi_ref[k, s, 0] = re
                psi_ref[k, s, 1] = im
                t_re, t_im = 1.0 + cut_re[s], cut_im[s]
                trn_ref[k, s, 0] = t_re
                trn_ref[k, s, 1] = t_im
                mult.append((t_re * re - t_im * im, t_re * im + t_im * re))
            mults.append(mult)
        waves = sandwich(mults, step(k) if k < n - 1 else transform, False)

    mults = []
    for j, pair in enumerate(pairs):
        scaled = []
        for q, s in enumerate(pair):
            re, im = waves[j][q]
            slot = slot_of[s]
            seen = jnp.where(local, meas_ref[slot], near_meas_ref[slot])
            misfit = jnp.where(slot < count, (re * re + im * im) * W_SCALE**-8 - seen * W_SCALE**-4, 0.0)
            scaled.append((misfit * re, misfit * im))
        mults.append(scaled)
    back = sandwich(mults, transform, True)
    for k in reversed(range(n)):
        grad_re, grad_im, mults = [], [], []
        for j, pair in enumerate(pairs):
            mult = []
            for q, s in enumerate(pair):
                re, im = back[j][q]
                p_re, p_im = psi_ref[k, s, 0], psi_ref[k, s, 1]
                grad_re.append(p_re * re + p_im * im)
                grad_im.append(p_re * im - p_im * re)
                if k > 0:
                    t_re, t_im = trn_ref[k, s, 0], trn_ref[k, s, 1]
                    mult.append((t_re * re + t_im * im, t_re * im - t_im * re))
            mults.append(mult)
        if k > 0:
            back = sandwich(mults, step(n - 1 - k), True)
        put(k, 0, grad_re)
        put(k, 1, grad_im)


def on_device(contrast, probe, offset_x, offset_y, probe_count, measured):
    n, lats = lax.axis_size("beam"), lax.axis_size("lat")
    order, tile, height = probe.shape[1], contrast.shape[2], contrast.shape[3]
    slots = offset_x.shape[0]
    half = slots // 2
    first = n // 2 - 1
    lat, group = lax.axis_index("lat"), lax.axis_index("beam")
    routes = [place(n, lats, a, False) for a in range(n)]
    back_routes = [place(n, lats, a, True) for a in range(n)]
    turn, back_turn = turns(n, False), turns(n, True)
    partner = swap(n, lats)

    mine = jnp.concatenate([offset_x, offset_y, probe_count])
    own_tile = contrast[:, 0].astype(jnp.bfloat16)[None]
    near = lax.ppermute(mine, AXES, partner)
    near_measured = lax.ppermute(measured, AXES, partner)
    own = jnp.concatenate([lax.ppermute(own_tile, AXES, routes[a]) for a in turn], axis=0)
    own, near, near_measured = lax.optimization_barrier((own, near, near_measured))
    other = lax.ppermute(own, AXES, partner)

    smem = pl.BlockSpec(memory_space=pltpu.SMEM)
    vmem = pl.BlockSpec(memory_space=pltpu.VMEM)
    mats = jnp.asarray(matrices(order, n - 1))
    tiles = (n, 2, tile, height)
    keep, send = pl.pallas_call(
        functools.partial(kernel, n, lats, slots),
        out_shape=(jax.ShapeDtypeStruct(tiles, jnp.float32), jax.ShapeDtypeStruct(tiles, jnp.bfloat16)),
        in_specs=[smem, smem] + [vmem] * 6,
        out_specs=(vmem, vmem),
        scratch_shapes=[
            pltpu.VMEM((n + 1, 2, 2 * order, 2 * order), jnp.bfloat16),
            pltpu.VMEM((n, half, 2, order, order), jnp.float32),
            pltpu.VMEM((n, half, 2, order, order), jnp.float32),
            pltpu.VMEM((n, 2, 2 * tile, height), jnp.float32),
        ],
        compiler_params=pltpu.CompilerParams(vmem_limit_bytes=(16 + 3 * n) << 20),
    )(mine, near, mats, own, other, probe, measured, near_measured)

    from_partner = lax.ppermute(send, AXES, partner)
    totals = [(keep[i] + from_partner[i].astype(jnp.float32)).astype(jnp.bfloat16) for i in range(n)]
    returned = [lax.ppermute(totals[i], AXES, [(d, s) for s, d in back_routes[a]]) for i, a in enumerate(back_turn)]
    returned = jnp.concatenate([r[None] for r in returned], axis=0)
    spot_first, spot_second = jnp.int32(0), jnp.int32(0)
    for i, a in enumerate(back_turn):
        spot_first = jnp.where(group == a, i, spot_first)
        spot_second = jnp.where(group == n - 1 - a, i, spot_second)
    from_first = lax.dynamic_index_in_dim(returned, spot_first, 0, False)
    from_first = jnp.where(group == first, totals[back_turn.index(first)], from_first)
    from_second = lax.dynamic_index_in_dim(returned, spot_second, 0, False).astype(jnp.float32)
    from_second = jnp.where(lat == 0, 0.0, from_second)
    return (from_first.astype(jnp.float32) + from_second)[:, None]


def solution(mesh):
    in_specs = (
        P(None, "beam", "lat", None),
        P(),
        P("lat"),
        P("lat"),
        P("lat"),
        P("lat", None, None),
    )
    out_specs = P(None, "beam", "lat", None)
    return jax.shard_map(
        on_device, mesh=mesh, in_specs=in_specs, out_specs=out_specs, check_vma=False
    )
```

time: 35.2 us -> 31.7 us (0.901)
  the two profiles are of different devices: /device:TPU:0 before, /device:TPU:9 now
where the time goes in v2:
time: 31.7 us; the launch traced here: 31.6 us
  waiting for transfers between devices  12.4 us (39%)
  starting transfers between devices  11.7 us (37%)
  Pallas kernels  4.59 us (14%)
  other arithmetic  2.08 us (7%)
  between operations  0.75 us (2%)
    ppermute x4, waiting for transfers between devices, on_device(): lax.ppermute(totals[i], AXES, [(d, s) for s, d in back_routes[a]])  6.2 us
    ppermute x4, starting transfers between devices, on_device(): lax.ppermute(own_tile, AXES, routes[a])  5.19 us
    pallas_call x1, Pallas kernels, on_device(): pl.pallas_call(functools.partial(kernel, n, lats, slots), out_shape=(jax....  4.59 us
    ppermute x4, starting transfers between devices, on_device(): lax.ppermute(totals[i], AXES, [(d, s) for s, d in back_routes[a]])  3.44 us
    ppermute x4, waiting for transfers between devices, on_device(): lax.ppermute(own_tile, AXES, routes[a])  3.1 us
    ppermute x1, waiting for transfers between devices, on_device(): from_partner = lax.ppermute(send, AXES, partner)  1.58 us
    ppermute x1, waiting for transfers between devices, on_device(): other = lax.ppermute(own, AXES, partner)  1.54 us
    ppermute x1, starting transfers between devices, on_device(): near = lax.ppermute(mine, AXES, partner)  1.17 us
  transfers between devices with their start and end apart: 12, of which 7 were waited for; matrix products, arithmetic and copies ran while one was open for 4% of the time, Pallas kernels for 0%

profile of v2, /device:TPU:9, one launch (start us, length us, event | category | flops | bytes accessed | tf_op | source)
XLA Modules:
  0.0 31.6 jit_solution(3619529375971670253)
XLA Ops:
  0.0 0.7 %collective-permute-start.5 = (f32[8,128,128]{2,1,0:T(8,128)}, f32[8,128,128]{2,1,0:T(8,128)S(1)}, u32[]{:S(2)}, u32[]{:S(2)}) collective-permute-start(f32[8,128,128]{2,1,0:T(8,128)} %meas_ref.1), channel_id=1, source_target_pairs={{0,1},{1,0},{2,3},{3,2},{4,5},{5,4},{6,7},{7,6},{8,9},{9,8},{10,11... | collective-permute-start | bytes 1572872 | tf_op jit(solution)/shard_map/ppermute | solution.py:248
  0.7 1.0 %fusion.3 = bf16[1,2,128,256]{3,2,1,0:T(8,128)(2,1)S(1)} fusion(f32[2,1,128,256]{3,2,1,0:T(8,128)} %param.7), kind=kLoop, calls=%fused_computation.11 | loop fusion | flops 65536 | bytes 393216 | tf_op jit(solution)/shard_map/convert_element_type | solution.py:246
  1.6 0.0 copy-start.3
  1.7 0.0 copy-start.4
  1.7 0.1 collective-permute-start
  1.7 2.4 %collective-permute-start.1 = (bf16[1,2,128,256]{3,2,1,0:T(8,128)(2,1)S(1)}, bf16[1,2,128,256]{3,2,1,0:T(8,128)(2,1)S(1)}, u32[]{:S(2)}, u32[]{:S(2)}) collective-permute-start(bf16[1,2,128,256]{3,2,1,0:T(8,128)(2,1)S(1)} %fusion.3), channel_id=1, source_target_pairs={{0,8},{1,9},{2,10},{3,11},{4,12},{5,13},{6,14},{7,15},{8,0},{9,1},... | collective-permute-start | bytes 393224 | tf_op jit(solution)/shard_map/ppermute | solution.py:249
  4.1 2.7 %collective-permute-start.2 = (bf16[1,2,128,256]{3,2,1,0:T(8,128)(2,1)S(1)}, bf16[1,2,128,256]{3,2,1,0:T(8,128)(2,1)S(1)}, u32[]{:S(2)}, u32[]{:S(2)}) collective-permute-start(bf16[1,2,128,256]{3,2,1,0:T(8,128)(2,1)S(1)} %fusion.3), channel_id=1, source_target_pairs={{0,1},{1,0},{2,3},{3,2},{4,5},{5,4},{6,7},{7,6},{8,9},{9,8},{10,11... | collective-permute-start | bytes 393224 | tf_op jit(solution)/shard_map/ppermute | solution.py:249
  6.8 0.1 collective-permute-start.3
  7.5 0.1 pad_add_fusion.mine_ref
  7.6 0.1 collective-permute-done
  7.8 1.2 %collective-permute-start.4 = (s32[17]{0:T(128)S(1)}, s32[17]{0:T(128)S(1)}, u32[]{:S(2)}, u32[]{:S(2)}) collective-permute-start(s32[17]{0:T(128)S(1)} %pad_add_fusion.mine_ref), channel_id=1, source_target_pairs={{0,1},{1,0},{2,3},{3,2},{4,5},{5,4},{6,7},{7,6},{8,9},{9,8},{10,11... | collective-permute-start | bytes 212 | tf_op jit(solution)/shard_map/ppermute | solution.py:247
  8.9 0.0 collective-permute-done.1
  8.9 0.0 collective-permute-done.2
  8.9 3.0 %collective-permute-done.3 = bf16[1,2,128,256]{3,2,1,0:T(8,128)(2,1)S(1)} collective-permute-done((bf16[1,2,128,256]{3,2,1,0:T(8,128)(2,1)S(1)}, bf16[1,2,128,256]{3,2,1,0:T(8,128)(2,1)S(1)}, u32[]{:S(2)}, u32[]{:S(2)}) %collective-permute-start.3) | collective-permute-done | bytes 131104 | tf_op jit(solution)/shard_map/ppermute | solution.py:249
  11.9 0.1 pad_maximum_fusion.own_ref
  12.0 0.0 collective-permute-done.4.near_ref
  12.0 0.8 %collective-permute-start.6 = (bf16[4,2,128,256]{3,2,1,0:T(8,128)(2,1)S(1)}, bf16[4,2,128,256]{3,2,1,0:T(8,128)(2,1)S(1)}, u32[]{:S(2)}, u32[]{:S(2)}) collective-permute-start(bf16[4,2,128,256]{3,2,1,0:T(8,128)(2,1)S(1)} %pad_maximum_fusion.own_ref), channel_id=1, source_target_pairs={{0,1},{1,0},{2,3},{3,2},{4,5},{5,4},{6,7},{7,6},{8,9},{9,8},{10,11... | collective-permute-start | bytes 1572872 | tf_op jit(solution)/shard_map/ppermute | solution.py:251
  12.8 1.5 %collective-permute-done.6.other_ref = bf16[4,2,128,256]{3,2,1,0:T(8,128)(2,1)S(1)} collective-permute-done((bf16[4,2,128,256]{3,2,1,0:T(8,128)(2,1)S(1)}, bf16[4,2,128,256]{3,2,1,0:T(8,128)(2,1)S(1)}, u32[]{:S(2)}, u32[]{:S(2)}) %collective-permute-start.6) | collective-permute-done | bytes 524320 | tf_op jit(solution)/shard_map/ppermute | solution.py:251
  14.4 4.6 %shard_map.73 = (f32[4,2,128,256]{3,2,1,0:T(8,128)S(1)}, bf16[4,2,128,256]{3,2,1,0:T(8,128)(2,1)S(1)}) custom-call(s32[17]{0:T(128)S(1)} %pad_add_fusion.mine_ref, s32[17]{0:T(128)S(1)} %collective-permute-done.4.near_ref, bf16[5,2,128,128]{3,2,1,0:T(8,128)(2,1)S(1)} %copy-done.1, bf16[4,2,128,256]{3,2,1,0:T(8,128)(2,1)S(1)} %pad_maximum_fusion.own_ref, ...), custom_call_target="tpu_custom_call" | custom-call | tf_op jit(solution)/shard_map/pallas_call | solution.py:257
  19.0 0.4 %collective-permute-start.7 = (bf16[4,2,128,256]{3,2,1,0:T(8,128)(2,1)S(1)}, bf16[4,2,128,256]{3,2,1,0:T(8,128)(2,1)S(1)}, u32[]{:S(2)}, u32[]{:S(2)}) collective-permute-start(bf16[4,2,128,256]{3,2,1,0:T(8,128)(2,1)S(1)} %get-tuple-element.14), channel_id=1, source_target_pairs={{0,1},{1,0},{2,3},{3,2},{4,5},{5,4},{6,7},{7,6},{8,9},{9,8},{10,11... | collective-permute-start | bytes 1572872 | tf_op jit(solution)/shard_map/ppermute | solution.py:271
  19.4 1.6 %collective-permute-done.7 = bf16[4,2,128,256]{3,2,1,0:T(8,128)(2,1)S(1)} collective-permute-done((bf16[4,2,128,256]{3,2,1,0:T(8,128)(2,1)S(1)}, bf16[4,2,128,256]{3,2,1,0:T(8,128)(2,1)S(1)}, u32[]{:S(2)}, u32[]{:S(2)}) %collective-permute-start.7) | collective-permute-done | bytes 524320 | tf_op jit(solution)/shard_map/ppermute | solution.py:271
  21.0 0.1 fusion
  21.1 0.0 collective-permute-start.8
  21.1 2.5 %collective-permute-start.9 = (bf16[2,128,256]{2,1,0:T(8,128)(2,1)S(1)}, bf16[2,128,256]{2,1,0:T(8,128)(2,1)S(1)}, u32[]{:S(2)}, u32[]{:S(2)}) collective-permute-start(bf16[2,128,256]{2,1,0:T(8,128)(2,1)S(1)} %get-tuple-element.17), channel_id=1, source_target_pairs={{2,0},{16,1},{17,2},{18,3},{19,4},{20,5},{21,6},{22,7},{0,8},{1,9}... | collective-permute-start | bytes 393224 | tf_op jit(solution)/shard_map/ppermute | solution.py:273
  23.6 0.9 %collective-permute-start.10 = (bf16[2,128,256]{2,1,0:T(8,128)(2,1)S(1)}, bf16[2,128,256]{2,1,0:T(8,128)(2,1)S(1)}, u32[]{:S(2)}, u32[]{:S(2)}) collective-permute-start(bf16[2,128,256]{2,1,0:T(8,128)(2,1)S(1)} %get-tuple-element.18), channel_id=1, source_target_pairs={{1,0},{0,1},{3,2},{2,3},{5,4},{4,5},{7,6},{6,7},{9,8},{8,9},{11,10... | collective-permute-start | bytes 393224 | tf_op jit(solution)/shard_map/ppermute | solution.py:273
  24.5 0.0 collective-permute-start.11
  24.5 1.3 %collective-permute-done.8 = bf16[2,128,256]{2,1,0:T(8,128)(2,1)S(1)} collective-permute-done((bf16[2,128,256]{2,1,0:T(8,128)(2,1)S(1)}, bf16[2,128,256]{2,1,0:T(8,128)(2,1)S(1)}, u32[]{:S(2)}, u32[]{:S(2)}) %collective-permute-start.8) | collective-permute-done | bytes 131104 | tf_op jit(solution)/shard_map/ppermute | solution.py:273
  25.9 2.8 %collective-permute-done.9 = bf16[2,128,256]{2,1,0:T(8,128)(2,1)S(1)} collective-permute-done((bf16[2,128,256]{2,1,0:T(8,128)(2,1)S(1)}, bf16[2,128,256]{2,1,0:T(8,128)(2,1)S(1)}, u32[]{:S(2)}, u32[]{:S(2)}) %collective-permute-start.9) | collective-permute-done | bytes 131104 | tf_op jit(solution)/shard_map/ppermute | solution.py:273
  28.7 0.0 collective-permute-done.10
  28.7 2.0 %collective-permute-done.11 = bf16[2,128,256]{2,1,0:T(8,128)(2,1)S(1)} collective-permute-done((bf16[2,128,256]{2,1,0:T(8,128)(2,1)S(1)}, bf16[2,128,256]{2,1,0:T(8,128)(2,1)S(1)}, u32[]{:S(2)}, u32[]{:S(2)}) %collective-permute-start.11) | collective-permute-done | bytes 131104 | tf_op jit(solution)/shard_map/ppermute | solution.py:273
  30.7 0.1 pad_maximum_fusion.1
  30.8 0.8 %add_bitcast_fusion = f32[2,1,128,256]{3,2,1,0:T(8,128)} fusion(bf16[4,2,128,256]{3,2,1,0:T(8,128)(2,1)S(1)} %pad_maximum_fusion.1, s32[]{:T(128)S(6)} %select_n.69, s32[]{:T(128)S(6)} %select_n.63, pred[]{:T(512)S(6)} %eq.23, pred[]{:T(512)S(6)} %eq.20, bf16[4,2,128,256]{3,2,1,0:T(8,128)(2,1)S(1)} %collective-permute-done.7, ...), kind=kLoop, calls=%fused_computation.3 | loop fusion | flops 524288 | bytes 917514 | tf_op jit(solution)/shard_map/add | solution.py:283
  (9 shorter events, 0.0 us)
Async XLA Ops:
  0.0 12.0 %collective-permute-start.5 = (f32[8,128,128]{2,1,0:T(8,128)}, f32[8,128,128]{2,1,0:T(8,128)S(1)}, u32[]{:S(2)}, u32[]{:S(2)}) collective-permute-start(f32[8,128,128]{2,1,0:T(8,128)} %meas_ref.1), channel_id=1, source_target_pairs={{0,1},{1,0},{2,3},{3,2},{4,5},{5,4},{6,7},{7,6},{8,9},{9,8},{10,11... | collective-permute-start | bytes 1572872 | tf_op jit(solution)/shard_map/ppermute | solution.py:248
  1.6 5.9 %copy-start.3 = (s32[8]{0:T(128)S(1)}, s32[8]{0:T(128)}, u32[]{:S(2)}) copy-start(s32[8]{0:T(128)} %param.10) | copy-start | bytes 100
  1.7 5.9 %copy-start.4 = (s32[8]{0:T(128)S(1)}, s32[8]{0:T(128)}, u32[]{:S(2)}) copy-start(s32[8]{0:T(128)} %param.9) | copy-start | bytes 100
  1.7 6.1 %collective-permute-start = (bf16[1,2,128,256]{3,2,1,0:T(8,128)(2,1)S(1)}, bf16[1,2,128,256]{3,2,1,0:T(8,128)(2,1)S(1)}, u32[]{:S(2)}, u32[]{:S(2)}) collective-permute-start(bf16[1,2,128,256]{3,2,1,0:T(8,128)(2,1)S(1)} %fusion.3), channel_id=1, source_target_pairs={{0,23},{1,16},{2,17},{3,18},{4,19},{5,20},{6,21},{7,22},{8,0},{9,1... | collective-permute-start | bytes 393224 | tf_op jit(solution)/shard_map/ppermute | solution.py:249
  1.7 7.2 %collective-permute-start.1 = (bf16[1,2,128,256]{3,2,1,0:T(8,128)(2,1)S(1)}, bf16[1,2,128,256]{3,2,1,0:T(8,128)(2,1)S(1)}, u32[]{:S(2)}, u32[]{:S(2)}) collective-permute-start(bf16[1,2,128,256]{3,2,1,0:T(8,128)(2,1)S(1)} %fusion.3), channel_id=1, source_target_pairs={{0,8},{1,9},{2,10},{3,11},{4,12},{5,13},{6,14},{7,15},{8,0},{9,1},... | collective-permute-start | bytes 393224 | tf_op jit(solution)/shard_map/ppermute | solution.py:249
  4.1 4.8 %collective-permute-start.2 = (bf16[1,2,128,256]{3,2,1,0:T(8,128)(2,1)S(1)}, bf16[1,2,128,256]{3,2,1,0:T(8,128)(2,1)S(1)}, u32[]{:S(2)}, u32[]{:S(2)}) collective-permute-start(bf16[1,2,128,256]{3,2,1,0:T(8,128)(2,1)S(1)} %fusion.3), channel_id=1, source_target_pairs={{0,1},{1,0},{2,3},{3,2},{4,5},{5,4},{6,7},{7,6},{8,9},{9,8},{10,11... | collective-permute-start | bytes 393224 | tf_op jit(solution)/shard_map/ppermute | solution.py:249
  6.8 5.1 %collective-permute-start.3 = (bf16[1,2,128,256]{3,2,1,0:T(8,128)(2,1)S(1)}, bf16[1,2,128,256]{3,2,1,0:T(8,128)(2,1)S(1)}, u32[]{:S(2)}, u32[]{:S(2)}) collective-permute-start(bf16[1,2,128,256]{3,2,1,0:T(8,128)(2,1)S(1)} %fusion.3), channel_id=1, source_target_pairs={{0,1},{1,0},{2,3},{3,2},{4,5},{5,4},{6,7},{7,6},{8,23},{9,16},{10,... | collective-permute-start | bytes 393224 | tf_op jit(solution)/shard_map/ppermute | solution.py:249
  7.6 6.8 %copy-start = (f32[8,128,128]{2,1,0:T(8,128)S(1)}, f32[8,128,128]{2,1,0:T(8,128)}, u32[]{:S(2)}) copy-start(f32[8,128,128]{2,1,0:T(8,128)} %meas_ref.1) | copy-start | bytes 1572868
  7.6 6.8 %copy-start.1 = (bf16[5,2,128,128]{3,2,1,0:T(8,128)(2,1)S(1)}, bf16[5,2,128,128]{3,2,1,0:T(8,128)(2,1)}, u32[]{:S(2)}) copy-start(bf16[5,2,128,128]{3,2,1,0:T(8,128)(2,1)} %constant.28.clone.mats_ref) | copy-start | bytes 983044
  7.6 6.8 %copy-start.2 = (f32[2,128,128]{2,1,0:T(8,128)S(1)}, f32[2,128,128]{2,1,0:T(8,128)}, u32[]{:S(2)}) copy-start(f32[2,128,128]{2,1,0:T(8,128)} %probe_ref.1) | copy-start | bytes 393220
  7.8 4.2 %collective-permute-start.4 = (s32[17]{0:T(128)S(1)}, s32[17]{0:T(128)S(1)}, u32[]{:S(2)}, u32[]{:S(2)}) collective-permute-start(s32[17]{0:T(128)S(1)} %pad_add_fusion.mine_ref), channel_id=1, source_target_pairs={{0,1},{1,0},{2,3},{3,2},{4,5},{5,4},{6,7},{7,6},{8,9},{9,8},{10,11... | collective-permute-start | bytes 212 | tf_op jit(solution)/shard_map/ppermute | solution.py:247
  12.0 2.4 %collective-permute-start.6 = (bf16[4,2,128,256]{3,2,1,0:T(8,128)(2,1)S(1)}, bf16[4,2,128,256]{3,2,1,0:T(8,128)(2,1)S(1)}, u32[]{:S(2)}, u32[]{:S(2)}) collective-permute-start(bf16[4,2,128,256]{3,2,1,0:T(8,128)(2,1)S(1)} %pad_maximum_fusion.own_ref), channel_id=1, source_target_pairs={{0,1},{1,0},{2,3},{3,2},{4,5},{5,4},{6,7},{7,6},{8,9},{9,8},{10,11... | collective-permute-start | bytes 1572872 | tf_op jit(solution)/shard_map/ppermute | solution.py:251
  19.0 2.0 %collective-permute-start.7 = (bf16[4,2,128,256]{3,2,1,0:T(8,128)(2,1)S(1)}, bf16[4,2,128,256]{3,2,1,0:T(8,128)(2,1)S(1)}, u32[]{:S(2)}, u32[]{:S(2)}) collective-permute-start(bf16[4,2,128,256]{3,2,1,0:T(8,128)(2,1)S(1)} %get-tuple-element.14), channel_id=1, source_target_pairs={{0,1},{1,0},{2,3},{3,2},{4,5},{5,4},{6,7},{7,6},{8,9},{9,8},{10,11... | collective-permute-start | bytes 1572872 | tf_op jit(solution)/shard_map/ppermute | solution.py:271
  21.1 4.8 %collective-permute-start.8 = (bf16[2,128,256]{2,1,0:T(8,128)(2,1)S(1)}, bf16[2,128,256]{2,1,0:T(8,128)(2,1)S(1)}, u32[]{:S(2)}, u32[]{:S(2)}) collective-permute-start(bf16[2,128,256]{2,1,0:T(8,128)(2,1)S(1)} %get-tuple-element.15), channel_id=1, source_target_pairs={{8,0},{9,1},{10,2},{11,3},{12,4},{13,5},{14,6},{15,7},{0,8},{1,9},... | collective-permute-start | bytes 393224 | tf_op jit(solution)/shard_map/ppermute | solution.py:273
  21.1 7.5 %collective-permute-start.9 = (bf16[2,128,256]{2,1,0:T(8,128)(2,1)S(1)}, bf16[2,128,256]{2,1,0:T(8,128)(2,1)S(1)}, u32[]{:S(2)}, u32[]{:S(2)}) collective-permute-start(bf16[2,128,256]{2,1,0:T(8,128)(2,1)S(1)} %get-tuple-element.17), channel_id=1, source_target_pairs={{2,0},{16,1},{17,2},{18,3},{19,4},{20,5},{21,6},{22,7},{0,8},{1,9}... | collective-permute-start | bytes 393224 | tf_op jit(solution)/shard_map/ppermute | solution.py:273
  23.6 5.0 %collective-permute-start.10 = (bf16[2,128,256]{2,1,0:T(8,128)(2,1)S(1)}, bf16[2,128,256]{2,1,0:T(8,128)(2,1)S(1)}, u32[]{:S(2)}, u32[]{:S(2)}) collective-permute-start(bf16[2,128,256]{2,1,0:T(8,128)(2,1)S(1)} %get-tuple-element.18), channel_id=1, source_target_pairs={{1,0},{0,1},{3,2},{2,3},{5,4},{4,5},{7,6},{6,7},{9,8},{8,9},{11,10... | collective-permute-start | bytes 393224 | tf_op jit(solution)/shard_map/ppermute | solution.py:273
  24.5 6.2 %collective-permute-start.11 = (bf16[2,128,256]{2,1,0:T(8,128)(2,1)S(1)}, bf16[2,128,256]{2,1,0:T(8,128)(2,1)S(1)}, u32[]{:S(2)}, u32[]{:S(2)}) collective-permute-start(bf16[2,128,256]{2,1,0:T(8,128)(2,1)S(1)} %get-tuple-element.16), channel_id=1, source_target_pairs={{1,0},{0,1},{3,2},{2,3},{5,4},{4,5},{7,6},{6,7},{23,8},{16,9},{17,... | collective-permute-start | bytes 393224 | tf_op jit(solution)/shard_map/ppermute | solution.py:273

commit v3 on v2

v3 whole, which is shorter than its diff:
```python
import functools
import math

import jax
import jax.numpy as jnp
import ml_dtypes
import numpy as np
from jax import lax
from jax.experimental import pallas as pl
from jax.experimental.pallas import tpu as pltpu
from jax.sharding import PartitionSpec as P

AXES = ("beam", "lat")


W_SCALE = 1.1775
LANES = 128


def matrices(order, steps):
    index = np.arange(order)
    dft = np.exp(-2j * np.pi * (index[:, None] * index[None, :] % order) / order) / math.sqrt(order)
    freq = (index + order // 2) % order - order // 2
    phase = np.exp(-1j * np.pi * (freq * freq % (4 * order)) / (2 * order))
    prop = (dft.conj() * phase) @ dft

    def pair(matrix):
        return np.stack([matrix.real, matrix.imag]).astype(ml_dtypes.bfloat16)

    def value(parts):
        parts = parts.astype(np.float64)
        return parts[0] + 1j * parts[1]

    out, ahead = [], np.zeros_like(prop)
    for step in range(steps):
        out.append(pair(prop - ahead))
        if step == steps - 1:
            out.append(pair(prop - ahead - value(out[-1])))
        else:
            ahead = ahead + value(out[-1]) - prop
    out.append(pair(W_SCALE * dft))
    return np.stack(out)


def place(n, lats, slice_index, short):
    first, second = n // 2 - 1, n // 2
    mirror = n - 1 - slice_index
    goals = {slice_index: first, mirror: second}
    outer = slice_index not in (first, second)
    if outer:
        goals[first] = min(slice_index, mirror)
        goals[second] = max(slice_index, mirror)
    to = {}
    for b in range(n):
        for l in range(lats):
            goal = goals.get(b, b)
            if goal == second:
                to[b, l] = (goal, (l - 1) % lats)
            else:
                to[b, l] = (goal, l ^ 1 if goal == b else l)
    if outer and short:
        via, middle = (first if goals[first] == mirror else second), lats // 4
        to[mirror, 0] = (mirror, middle)
        to[via, middle] = (second, lats - 1)
    return [(b * lats + l, c * lats + m) for (b, l), (c, m) in to.items()]


def swap(n, lats):
    return [(b * lats + l, b * lats + (l ^ 1)) for b in range(n) for l in range(lats)]


def turns(n, back):
    ends = [0, n - 1] if back else [n - 1, 0]
    return ends + list(range(1, n - 1))


def position(n, lats):
    group, lat = lax.axis_index("beam"), lax.axis_index("lat")
    side = lax.rem(lat, 2)
    at_first, at_second = group == n // 2 - 1, group == n // 2
    base = jnp.where(at_first, lat - side, lat + 1 - side)
    return lat, side, at_first, at_second, base


def corners(slots, local, side, mine_ref, near_ref):
    half = slots // 2
    values = jnp.where(local, mine_ref[...], near_ref[...])

    def scalar(i):
        return jnp.where(side == 0, values[0, i], values[0, i + half])

    return [scalar(s) for s in range(half)], [scalar(slots + s) for s in range(half)], values[0, 2 * slots]


def lay(ext_ref, k, own, other, row, beyond, tile):
    for value, r in ((own, row), (other, 1 - row)):
        value = value.astype(jnp.float32) * jnp.where(beyond & (r == 1), 0.0, 1.0)
        ext_ref[k, :, pl.ds(pl.multiple_of(r * tile, tile), tile), :] = value


def cut(ext_ref, k, c, xs, ys, order):
    sub = lax.broadcasted_iota(jnp.int32, (order // 8, 8, order), 1)
    lane = lax.broadcasted_iota(jnp.int32, (order + 8, order), 1)
    out = []
    for x, y in zip(xs, ys):
        turn = lax.rem(order - y, order)
        start = pl.ds(pl.multiple_of(x // 8 * 8, 8), order + 8)
        left = pltpu.roll(ext_ref[k, c, start, :order], turn, 1)
        right = pltpu.roll(ext_ref[k, c, start, order:], turn, 1)
        w = jnp.where(lane < order - y, left, right).reshape(order // 8 + 1, 8, order)
        r = lax.rem(x, 8)
        w = pltpu.roll(w, lax.rem(8 - r, 8), 1)
        out.append(jnp.where(sub < 8 - r, w[:-1], w[1:]).reshape(order, order))
    return out


def dot(a, b):
    return jnp.dot(a, b, preferred_element_type=jnp.float32)


def sandwich(full_ref, waves, ms, conj):
    order = waves[0][0].shape[0]
    right, left = (0, 1) if conj else (1, 0)
    rows = [jnp.concatenate(w, axis=1).astype(jnp.bfloat16) for w in waves]
    ys = [sum(dot(r, full_ref[m, right]) for m in ms).astype(jnp.bfloat16) for r in rows]
    cols = [jnp.concatenate([y[:, :order], y[:, order:]], axis=0) for y in ys]
    zs = [sum(dot(full_ref[m, left], c) for m in ms) for c in cols]
    return [(z[:order], z[order:]) for z in zs]


def step(n, i):
    return (n - 2, n - 1) if i == n - 2 else (i,)


def early_kernel(
    n, lats, slots, mine_ref, near_ref, mats_ref, own_ref, other_ref, probe_ref, full_ref, psi_ref, trn_ref, ext_ref
):
    order, tile = probe_ref.shape[-1], own_ref.shape[2]
    lat, side, at_first, at_second, base = position(n, lats)
    xs, ys, count = corners(slots, base == lat, side, mine_ref, near_ref)
    for m in range(n + 1):
        re, im = mats_ref[m, 0], mats_ref[m, 1]
        for h, (upper, lower) in enumerate(((-im, im), (im, -im))):
            full_ref[m, h, :order, :order] = re
            full_ref[m, h, :order, order:] = upper
            full_ref[m, h, order:, :order] = lower
            full_ref[m, h, order:, order:] = re
    for k in range(2):
        i = jnp.where(at_second, k, 1 - k)
        lay(ext_ref, k, own_ref[i], other_ref[i], side, base + 1 >= lats, tile)
    first = [cut(ext_ref, 0, c, xs, ys, order) for c in range(2)]
    re, im = probe_ref[0], probe_ref[1]
    waves = []
    for c_re, c_im in zip(*first):
        t_re = 1.0 + c_re
        waves.append((t_re * re - c_im * im, t_re * im + c_im * re))
    waves = sandwich(full_ref, waves, step(n, 0), False)
    for s, wave in enumerate(waves):
        for c in range(2):
            psi_ref[s, c] = wave[c]
    for c in range(2):
        for s, value in enumerate(cut(ext_ref, 1, c, xs, ys, order)):
            trn_ref[s, c] = value


def main_kernel(
    n, lats, slots, mine_ref, near_ref, full_ref, own_ref, other_ref, probe_ref, one_ref, last_ref, meas_ref,
    near_meas_ref, keep_ref, send_ref, trn_ref, psi_ref, ext_ref,
):
    order, tile = probe_ref.shape[-1], own_ref.shape[2]
    half = slots // 2
    first = n // 2 - 1
    lat, side, at_first, at_second, base = position(n, lats)
    local = base == lat
    xs, ys, count = corners(slots, local, side, mine_ref, near_ref)
    lane = lax.broadcasted_iota(jnp.int32, (order, order), 1)

    tall = (2 * tile, order)
    index = lax.broadcasted_iota(jnp.int32, tall, 0)
    column = jnp.where(index >= tile, index - tile + (1 - side) * tile, index + side * tile)
    put_at = column - lax.broadcasted_iota(jnp.int32, tall, 1)
    puts = jnp.concatenate([jnp.where(put_at == x, 1.0, 0.0) for x in xs], axis=1).astype(jnp.bfloat16)

    def put(k, c, values):
        rows = []
        for s, value in enumerate(values):
            value = pltpu.roll(value, lax.rem(ys[s], order), 1)
            rows.append(
                jnp.concatenate(
                    [jnp.where(lane >= ys[s], value, 0.0), jnp.where(lane < ys[s], value, 0.0)], axis=1
                ).astype(jnp.bfloat16)
            )
        total = dot(puts, jnp.concatenate(rows, axis=0))
        order_back = turns(n, True)
        i = jnp.where(at_second, order_back.index(n - 1 - k), order_back.index(k))
        keep_ref[i, c] = total[:tile]
        send_ref[i, c] = total[tile:].astype(jnp.bfloat16)

    for k in range(1, n - 1):
        i = jnp.where(at_second, n - 2 - k, k - 1)
        row = jnp.where(at_first & (k == first), 1 - side, side)
        lay(ext_ref, k - 1, own_ref[i], other_ref[i], row, base + 1 >= lats, tile)

    waves = [(one_ref[s, 0], one_ref[s, 1]) for s in range(half)]
    for k in range(1, n):
        if k < n - 1:
            cuts = [cut(ext_ref, k - 1, c, xs, ys, order) for c in range(2)]
        else:
            cuts = [[last_ref[s, c] for s in range(half)] for c in range(2)]
        mult = []
        for s, (re, im) in enumerate(waves):
            psi_ref[k, s, 0] = re
            psi_ref[k, s, 1] = im
            t_re, t_im = 1.0 + cuts[0][s], cuts[1][s]
            trn_ref[k, s, 0] = t_re
            trn_ref[k, s, 1] = t_im
            mult.append((t_re * re - t_im * im, t_re * im + t_im * re))
        waves = sandwich(full_ref, mult, step(n, k) if k < n - 1 else (n,), False)

    mult = []
    for s, (re, im) in enumerate(waves):
        slot = side * half + s
        seen = jnp.where(local, meas_ref[slot], near_meas_ref[slot])
        misfit = jnp.where(slot < count, (re * re + im * im) * W_SCALE**-8 - seen * W_SCALE**-4, 0.0)
        mult.append((misfit * re, misfit * im))
    waves = sandwich(full_ref, mult, (n,), True)
    for k in reversed(range(n)):
        grad_re, grad_im, mult = [], [], []
        for s, (re, im) in enumerate(waves):
            p_re, p_im = (psi_ref[k, s, 0], psi_ref[k, s, 1]) if k else (probe_ref[0], probe_ref[1])
            grad_re.append(p_re * re + p_im * im)
            grad_im.append(p_re * im - p_im * re)
            if k > 0:
                t_re, t_im = trn_ref[k, s, 0], trn_ref[k, s, 1]
                mult.append((t_re * re + t_im * im, t_re * im - t_im * re))
        if k > 0:
            waves = sandwich(full_ref, mult, step(n, n - 1 - k), True)
        put(k, 0, grad_re)
        put(k, 1, grad_im)


def on_device(contrast, probe, offset_x, offset_y, probe_count, measured):
    n, lats = lax.axis_size("beam"), lax.axis_size("lat")
    order, tile, height = probe.shape[1], contrast.shape[2], contrast.shape[3]
    slots = offset_x.shape[0]
    half = slots // 2
    first = n // 2 - 1
    lat, group = lax.axis_index("lat"), lax.axis_index("beam")
    routes = [place(n, lats, a, False) for a in range(n)]
    back_routes = [place(n, lats, a, True) for a in range(n)]
    turn, back_turn = turns(n, False), turns(n, True)
    partner = swap(n, lats)

    own_tile = contrast[:, 0].astype(jnp.bfloat16)[None]
    arrived = [lax.ppermute(own_tile, AXES, routes[a]) for a in turn]
    own_early = jnp.concatenate(arrived[:2], axis=0)
    own_late = jnp.concatenate(arrived[2:], axis=0)
    mine = jnp.concatenate([offset_x, offset_y, probe_count])
    mine = jnp.pad(mine, (0, LANES - mine.shape[0]))[None]
    near = lax.ppermute(mine, AXES, partner)
    near_measured = lax.ppermute(measured, AXES, partner)
    own_early, near = lax.optimization_barrier((own_early, near))
    other_early = lax.ppermute(own_early, AXES, partner)
    other_late = lax.ppermute(own_late, AXES, partner)

    vmem = pl.BlockSpec(memory_space=pltpu.VMEM)
    params = pltpu.CompilerParams(vmem_limit_bytes=(16 + 3 * n) << 20)
    mats = jnp.asarray(matrices(order, n - 1))
    tiles = (n, 2, tile, height)
    fields = jax.ShapeDtypeStruct((half, 2, order, order), jnp.float32)
    full = jax.ShapeDtypeStruct((n + 1, 2, 2 * order, 2 * order), jnp.bfloat16)
    full, one, last = pl.pallas_call(
        functools.partial(early_kernel, n, lats, slots),
        out_shape=(full, fields, fields),
        in_specs=[vmem] * 6,
        out_specs=(vmem,) * 3,
        scratch_shapes=[pltpu.VMEM((2, 2, 2 * tile, height), jnp.float32)],
        compiler_params=params,
        cost_estimate=pl.CostEstimate(flops=10**9, bytes_accessed=2 << 20, transcendentals=0),
    )(mine, near, mats, own_early, other_early, probe)
    keep, send = pl.pallas_call(
        functools.partial(main_kernel, n, lats, slots),
        out_shape=(jax.ShapeDtypeStruct(tiles, jnp.float32), jax.ShapeDtypeStruct(tiles, jnp.bfloat16)),
        in_specs=[vmem] * 10,
        out_specs=(vmem, vmem),
        scratch_shapes=[
            pltpu.VMEM((n, half, 2, order, order), jnp.float32),
            pltpu.VMEM((n, half, 2, order, order), jnp.float32),
            pltpu.VMEM((n - 2, 2, 2 * tile, height), jnp.float32),
        ],
        compiler_params=params,
        cost_estimate=pl.CostEstimate(flops=4 * 10**9, bytes_accessed=8 << 20, transcendentals=0),
    )(mine, near, full, own_late, other_late, probe, one, last, measured, near_measured)

    from_partner = lax.ppermute(send, AXES, partner)
    totals = [(keep[i] + from_partner[i].astype(jnp.float32)).astype(jnp.bfloat16) for i in range(n)]
    returned = [lax.ppermute(totals[i], AXES, [(d, s) for s, d in back_routes[a]]) for i, a in enumerate(back_turn)]
    returned = jnp.concatenate([r[None] for r in returned], axis=0)
    spot_first, spot_second = jnp.int32(0), jnp.int32(0)
    for i, a in enumerate(back_turn):
        spot_first = jnp.where(group == a, i, spot_first)
        spot_second = jnp.where(group == n - 1 - a, i, spot_second)
    from_first = lax.dynamic_index_in_dim(returned, spot_first, 0, False)
    from_first = jnp.where(group == first, totals[back_turn.index(first)], from_first)
    from_second = lax.dynamic_index_in_dim(returned, spot_second, 0, False).astype(jnp.float32)
    from_second = jnp.where(lat == 0, 0.0, from_second)
    return (from_first.astype(jnp.float32) + from_second)[:, None]


def solution(mesh):
    in_specs = (
        P(None, "beam", "lat", None),
        P(),
        P("lat"),
        P("lat"),
        P("lat"),
        P("lat", None, None),
    )
    out_specs = P(None, "beam", "lat", None)
    return jax.shard_map(
        on_device, mesh=mesh, in_specs=in_specs, out_specs=out_specs, check_vma=False
    )
```

time: 31.7 us -> 31 us (0.978)
  the two profiles are of different devices: /device:TPU:9 before, /device:TPU:4 now
where the time goes in v3:
time: 31 us; the launch traced here: 30.9 us
  waiting for transfers between devices  14.8 us (48%)
  starting transfers between devices  7.79 us (25%)
  Pallas kernels  4.64 us (15%)
  other arithmetic  2.76 us (9%)
  between operations  0.78 us (3%)
    ppermute x4, waiting for transfers between devices, on_device(): lax.ppermute(totals[i], AXES, [(d, s) for s, d in back_routes[a]])  8.28 us
    ppermute x4, waiting for transfers between devices, on_device(): arrived = [lax.ppermute(own_tile, AXES, routes[a]) for a in turn]  3.87 us
    pallas_call x1, Pallas kernels, on_device(): pl.pallas_call(functools.partial(main_kernel, n, lats, slots), out_shape=...  3.67 us
    ppermute x4, starting transfers between devices, on_device(): lax.ppermute(totals[i], AXES, [(d, s) for s, d in back_routes[a]])  3.48 us
    ppermute x4, starting transfers between devices, on_device(): arrived = [lax.ppermute(own_tile, AXES, routes[a]) for a in turn]  3.47 us
    ppermute x1, waiting for transfers between devices, on_device(): from_partner = lax.ppermute(send, AXES, partner)  1.77 us
    convert_element_type x1, other arithmetic, on_device(): own_tile = contrast[:, 0].astype(jnp.bfloat16)[None]  1.02 us
    pallas_call x1, Pallas kernels, on_device(): pl.pallas_call(functools.partial(early_kernel, n, lats, slots), out_shape...  0.97 us
  transfers between devices with their start and end apart: 13, of which 6 were waited for; matrix products, arithmetic and copies ran while one was open for 3% of the time, Pallas kernels for 3%

profile of v3, /device:TPU:4, one launch (start us, length us, event | category | flops | bytes accessed | tf_op | source)
XLA Modules:
  0.0 30.9 jit_solution(5449709721420117302)
XLA Ops:
  0.0 1.0 %fusion.3 = bf16[1,2,128,256]{3,2,1,0:T(8,128)(2,1)S(1)} fusion(f32[2,1,128,256]{3,2,1,0:T(8,128)} %param.7), kind=kLoop, calls=%fused_computation.11 | loop fusion | flops 65536 | bytes 393216 | tf_op jit(solution)/shard_map/convert_element_type | solution.py:254
  1.0 3.0 %collective-permute-start = (bf16[1,2,128,256]{3,2,1,0:T(8,128)(2,1)S(1)}, bf16[1,2,128,256]{3,2,1,0:T(8,128)(2,1)S(1)}, u32[]{:S(2)}, u32[]{:S(2)}) collective-permute-start(bf16[1,2,128,256]{3,2,1,0:T(8,128)(2,1)S(1)} %fusion.3), channel_id=1, source_target_pairs={{0,23},{1,16},{2,17},{3,18},{4,19},{5,20},{6,21},{7,22},{8,0},{9,1... | collective-permute-start | bytes 393224 | tf_op jit(solution)/shard_map/ppermute | solution.py:255
  4.0 0.0 collective-permute-start.1
  4.0 0.0 collective-permute-start.4
  4.0 0.5 %collective-permute-start.5 = (bf16[1,2,128,256]{3,2,1,0:T(8,128)(2,1)S(1)}, bf16[1,2,128,256]{3,2,1,0:T(8,128)(2,1)S(1)}, u32[]{:S(2)}, u32[]{:S(2)}) collective-permute-start(bf16[1,2,128,256]{3,2,1,0:T(8,128)(2,1)S(1)} %fusion.3), channel_id=1, source_target_pairs={{0,1},{1,0},{2,3},{3,2},{4,5},{5,4},{6,7},{7,6},{8,23},{9,16},{10,... | collective-permute-start | bytes 393224 | tf_op jit(solution)/shard_map/ppermute | solution.py:255
  5.1 0.7 %pad_add_fusion = s32[17]{0:T(128)S(1)} fusion(s32[1]{0:T(128)S(6)} %copy.11, s32[8]{0:T(128)} %param.10, s32[8]{0:T(128)} %param.9), kind=kLoop, calls=%fused_computation.14 | loop fusion | flops 34 | bytes 136 | tf_op jit(solution)/shard_map/concatenate | solution.py:258
  5.9 0.0 collective-permute-start.2
  5.9 1.9 %collective-permute-done = bf16[1,2,128,256]{3,2,1,0:T(8,128)(2,1)S(1)} collective-permute-done((bf16[1,2,128,256]{3,2,1,0:T(8,128)(2,1)S(1)}, bf16[1,2,128,256]{3,2,1,0:T(8,128)(2,1)S(1)}, u32[]{:S(2)}, u32[]{:S(2)}) %collective-permute-start) | collective-permute-done | bytes 131104 | tf_op jit(solution)/shard_map/ppermute | solution.py:255
  7.9 0.0 collective-permute-start.7
  7.9 1.9 %collective-permute-done.1 = bf16[1,2,128,256]{3,2,1,0:T(8,128)(2,1)S(1)} collective-permute-done((bf16[1,2,128,256]{3,2,1,0:T(8,128)(2,1)S(1)}, bf16[1,2,128,256]{3,2,1,0:T(8,128)(2,1)S(1)}, u32[]{:S(2)}, u32[]{:S(2)}) %collective-permute-start.1) | collective-permute-done | bytes 131104 | tf_op jit(solution)/shard_map/ppermute | solution.py:255
  9.8 0.0 collective-permute-done.2.near_ref
  9.8 0.1 collective-permute-start.3
  9.9 0.0 collective-permute-done.4
  9.9 0.0 collective-permute-done.5
  10.0 0.0 copy-start
  10.0 0.6 %collective-permute-start.6 = (bf16[2,2,128,256]{3,2,1,0:T(8,128)(2,1)S(1)}, bf16[2,2,128,256]{3,2,1,0:T(8,128)(2,1)S(1)}, u32[]{:S(2)}, u32[]{:S(2)}) collective-permute-start(bf16[2,2,128,256]{3,2,1,0:T(8,128)(2,1)S(1)} %constant_dynamic-update-slice_fusion.own_ref), channel_id=1, source_target_pairs={{0,1},{1,0},{2,3},{3,2},{4,5},{5,4},{6,7},{7,6},{8,9},{9,8},{10,11... | collective-permute-start | bytes 786440 | tf_op jit(solution)/shard_map/ppermute | solution.py:264
  10.5 0.9 %collective-permute-done.3.other_ref = bf16[2,2,128,256]{3,2,1,0:T(8,128)(2,1)S(1)} collective-permute-done((bf16[2,2,128,256]{3,2,1,0:T(8,128)(2,1)S(1)}, bf16[2,2,128,256]{3,2,1,0:T(8,128)(2,1)S(1)}, u32[]{:S(2)}, u32[]{:S(2)}) %collective-permute-start.3) | collective-permute-done | bytes 262176 | tf_op jit(solution)/shard_map/ppermute | solution.py:263
  11.4 1.0 %shard_map.73 = (bf16[5,2,256,256]{3,2,1,0:T(8,128)(2,1)S(1)}, f32[4,2,128,128]{3,2,1,0:T(8,128)S(1)}, f32[4,2,128,128]{3,2,1,0:T(8,128)S(1)}) custom-call(s32[1,128]{1,0:T(1,128)S(1)} %pad_bitcast_fusion.mine_ref, s32[1,128]{1,0:T(1,128)S(1)} %collective-permute-done.2.near_ref, bf16[5,2,128,128]{3,2,1,0:T(8,128)(2,1)S(1)} %copy-done.2, ...), custom_call_target="tpu_custom_call" | custom-call | flops 1000000000 | bytes 2097152 | tf_op jit(solution)/shard_map/pallas_call | solution.py:272
  12.4 0.0 collective-permute-done.6.other_ref
  12.4 0.0 collective-permute-done.7.near_meas_ref
  12.4 3.7 %shard_map.74 = (f32[4,2,128,256]{3,2,1,0:T(8,128)S(1)}, bf16[4,2,128,256]{3,2,1,0:T(8,128)(2,1)S(1)}) custom-call(s32[1,128]{1,0:T(1,128)S(1)} %pad_bitcast_fusion.mine_ref, s32[1,128]{1,0:T(1,128)S(1)} %collective-permute-done.2.near_ref, bf16[5,2,256,256]{3,2,1,0:T(8,128)(2,1)S(1)} %get-tuple-element.14.full_ref, ...), custom_call_target="tpu_custom_call" | custom-call | flops 4000000000 | bytes 8388608 | tf_op jit(solution)/shard_map/pallas_call | solution.py:281
  16.1 0.2 collective-permute-start.8
  16.3 1.8 %collective-permute-done.8 = bf16[4,2,128,256]{3,2,1,0:T(8,128)(2,1)S(1)} collective-permute-done((bf16[4,2,128,256]{3,2,1,0:T(8,128)(2,1)S(1)}, bf16[4,2,128,256]{3,2,1,0:T(8,128)(2,1)S(1)}, u32[]{:S(2)}, u32[]{:S(2)}) %collective-permute-start.8) | collective-permute-done | bytes 524320 | tf_op jit(solution)/shard_map/ppermute | solution.py:295
  18.1 0.1 fusion
  18.2 0.2 collective-permute-start.12
  18.4 3.3 %collective-permute-start.9 = (bf16[2,128,256]{2,1,0:T(8,128)(2,1)S(1)}, bf16[2,128,256]{2,1,0:T(8,128)(2,1)S(1)}, u32[]{:S(2)}, u32[]{:S(2)}) collective-permute-start(bf16[2,128,256]{2,1,0:T(8,128)(2,1)S(1)} %get-tuple-element.19), channel_id=1, source_target_pairs={{8,0},{9,1},{10,2},{11,3},{12,4},{13,5},{14,6},{15,7},{0,8},{1,9},... | collective-permute-start | bytes 393224 | tf_op jit(solution)/shard_map/ppermute | solution.py:297
  21.7 0.0 collective-permute-start.10
  21.7 0.0 collective-permute-done.12
  21.7 3.8 %collective-permute-done.9 = bf16[2,128,256]{2,1,0:T(8,128)(2,1)S(1)} collective-permute-done((bf16[2,128,256]{2,1,0:T(8,128)(2,1)S(1)}, bf16[2,128,256]{2,1,0:T(8,128)(2,1)S(1)}, u32[]{:S(2)}, u32[]{:S(2)}) %collective-permute-start.9) | collective-permute-done | bytes 131104 | tf_op jit(solution)/shard_map/ppermute | solution.py:297
  25.5 4.4 %collective-permute-done.10 = bf16[2,128,256]{2,1,0:T(8,128)(2,1)S(1)} collective-permute-done((bf16[2,128,256]{2,1,0:T(8,128)(2,1)S(1)}, bf16[2,128,256]{2,1,0:T(8,128)(2,1)S(1)}, u32[]{:S(2)}, u32[]{:S(2)}) %collective-permute-start.10) | collective-permute-done | bytes 131104 | tf_op jit(solution)/shard_map/ppermute | solution.py:297
  30.0 0.1 pad_maximum_fusion
  30.1 0.8 %add_bitcast_fusion = f32[2,1,128,256]{3,2,1,0:T(8,128)} fusion(bf16[4,2,128,256]{3,2,1,0:T(8,128)(2,1)S(1)} %pad_maximum_fusion, s32[]{:T(128)S(6)} %select_n.69, s32[]{:T(128)S(6)} %select_n.63, pred[]{:T(512)S(6)} %eq.23, pred[]{:T(512)S(6)} %eq.20, bf16[4,2,128,256]{3,2,1,0:T(8,128)(2,1)S(1)} %collective-permute-done.8, ...), kind=kLoop, calls=%fused_computation.3 | loop fusion | flops 524288 | bytes 917514 | tf_op jit(solution)/shard_map/add | solution.py:307
  (11 shorter events, 0.1 us)
Async XLA Ops:
  0.0 11.4 %copy-start.2 = (bf16[5,2,128,128]{3,2,1,0:T(8,128)(2,1)S(1)}, bf16[5,2,128,128]{3,2,1,0:T(8,128)(2,1)}, u32[]{:S(2)}) copy-start(bf16[5,2,128,128]{3,2,1,0:T(8,128)(2,1)} %constant.28.clone.mats_ref) | copy-start | bytes 983044
  0.0 11.4 %copy-start.1 = (f32[2,128,128]{2,1,0:T(8,128)S(1)}, f32[2,128,128]{2,1,0:T(8,128)}, u32[]{:S(2)}) copy-start(f32[2,128,128]{2,1,0:T(8,128)} %probe_ref.3) | copy-start | bytes 393220
  1.0 6.8 %collective-permute-start = (bf16[1,2,128,256]{3,2,1,0:T(8,128)(2,1)S(1)}, bf16[1,2,128,256]{3,2,1,0:T(8,128)(2,1)S(1)}, u32[]{:S(2)}, u32[]{:S(2)}) collective-permute-start(bf16[1,2,128,256]{3,2,1,0:T(8,128)(2,1)S(1)} %fusion.3), channel_id=1, source_target_pairs={{0,23},{1,16},{2,17},{3,18},{4,19},{5,20},{6,21},{7,22},{8,0},{9,1... | collective-permute-start | bytes 393224 | tf_op jit(solution)/shard_map/ppermute | solution.py:255
  4.0 5.8 %collective-permute-start.1 = (bf16[1,2,128,256]{3,2,1,0:T(8,128)(2,1)S(1)}, bf16[1,2,128,256]{3,2,1,0:T(8,128)(2,1)S(1)}, u32[]{:S(2)}, u32[]{:S(2)}) collective-permute-start(bf16[1,2,128,256]{3,2,1,0:T(8,128)(2,1)S(1)} %fusion.3), channel_id=1, source_target_pairs={{0,8},{1,9},{2,10},{3,11},{4,12},{5,13},{6,14},{7,15},{8,0},{9,1},... | collective-permute-start | bytes 393224 | tf_op jit(solution)/shard_map/ppermute | solution.py:255
  4.0 5.9 %collective-permute-start.4 = (bf16[1,2,128,256]{3,2,1,0:T(8,128)(2,1)S(1)}, bf16[1,2,128,256]{3,2,1,0:T(8,128)(2,1)S(1)}, u32[]{:S(2)}, u32[]{:S(2)}) collective-permute-start(bf16[1,2,128,256]{3,2,1,0:T(8,128)(2,1)S(1)} %fusion.3), channel_id=1, source_target_pairs={{0,1},{1,0},{2,3},{3,2},{4,5},{5,4},{6,7},{7,6},{8,9},{9,8},{10,11... | collective-permute-start | bytes 393224 | tf_op jit(solution)/shard_map/ppermute | solution.py:255
  4.0 6.0 %collective-permute-start.5 = (bf16[1,2,128,256]{3,2,1,0:T(8,128)(2,1)S(1)}, bf16[1,2,128,256]{3,2,1,0:T(8,128)(2,1)S(1)}, u32[]{:S(2)}, u32[]{:S(2)}) collective-permute-start(bf16[1,2,128,256]{3,2,1,0:T(8,128)(2,1)S(1)} %fusion.3), channel_id=1, source_target_pairs={{0,1},{1,0},{2,3},{3,2},{4,5},{5,4},{6,7},{7,6},{8,23},{9,16},{10,... | collective-permute-start | bytes 393224 | tf_op jit(solution)/shard_map/ppermute | solution.py:255
  5.9 3.9 %collective-permute-start.2 = (s32[1,128]{1,0:T(1,128)S(1)}, s32[1,128]{1,0:T(1,128)S(1)}, u32[]{:S(2)}, u32[]{:S(2)}) collective-permute-start(s32[1,128]{1,0:T(1,128)S(1)} %pad_bitcast_fusion.mine_ref), channel_id=1, source_target_pairs={{0,1},{1,0},{2,3},{3,2},{4,5},{5,4},{6,7},{7,6},{8,9},{9,8},{10,11... | collective-permute-start | bytes 1544 | tf_op jit(solution)/shard_map/ppermute | solution.py:260
  7.9 4.6 %collective-permute-start.7 = (f32[8,128,128]{2,1,0:T(8,128)}, f32[8,128,128]{2,1,0:T(8,128)S(1)}, u32[]{:S(2)}, u32[]{:S(2)}) collective-permute-start(f32[8,128,128]{2,1,0:T(8,128)} %meas_ref.1), channel_id=1, source_target_pairs={{0,1},{1,0},{2,3},{3,2},{4,5},{5,4},{6,7},{7,6},{8,9},{9,8},{10,11... | collective-permute-start | bytes 1572872 | tf_op jit(solution)/shard_map/ppermute | solution.py:261
  9.8 1.6 %collective-permute-start.3 = (bf16[2,2,128,256]{3,2,1,0:T(8,128)(2,1)S(1)}, bf16[2,2,128,256]{3,2,1,0:T(8,128)(2,1)S(1)}, u32[]{:S(2)}, u32[]{:S(2)}) collective-permute-start(bf16[2,2,128,256]{3,2,1,0:T(8,128)(2,1)S(1)} %pad_maximum_fusion.1.own_ref), channel_id=1, source_target_pairs={{0,1},{1,0},{2,3},{3,2},{4,5},{5,4},{6,7},{7,6},{8,9},{9,8},{10,11... | collective-permute-start | bytes 786440 | tf_op jit(solution)/shard_map/ppermute | solution.py:263
  10.0 2.5 %copy-start = (f32[8,128,128]{2,1,0:T(8,128)S(1)}, f32[8,128,128]{2,1,0:T(8,128)}, u32[]{:S(2)}) copy-start(f32[8,128,128]{2,1,0:T(8,128)} %meas_ref.1) | copy-start | bytes 1572868
  10.0 2.4 %collective-permute-start.6 = (bf16[2,2,128,256]{3,2,1,0:T(8,128)(2,1)S(1)}, bf16[2,2,128,256]{3,2,1,0:T(8,128)(2,1)S(1)}, u32[]{:S(2)}, u32[]{:S(2)}) collective-permute-start(bf16[2,2,128,256]{3,2,1,0:T(8,128)(2,1)S(1)} %constant_dynamic-update-slice_fusion.own_ref), channel_id=1, source_target_pairs={{0,1},{1,0},{2,3},{3,2},{4,5},{5,4},{6,7},{7,6},{8,9},{9,8},{10,11... | collective-permute-start | bytes 786440 | tf_op jit(solution)/shard_map/ppermute | solution.py:264
  16.1 2.0 %collective-permute-start.8 = (bf16[4,2,128,256]{3,2,1,0:T(8,128)(2,1)S(1)}, bf16[4,2,128,256]{3,2,1,0:T(8,128)(2,1)S(1)}, u32[]{:S(2)}, u32[]{:S(2)}) collective-permute-start(bf16[4,2,128,256]{3,2,1,0:T(8,128)(2,1)S(1)} %get-tuple-element.18), channel_id=1, source_target_pairs={{0,1},{1,0},{2,3},{3,2},{4,5},{5,4},{6,7},{7,6},{8,9},{9,8},{10,11... | collective-permute-start | bytes 1572872 | tf_op jit(solution)/shard_map/ppermute | solution.py:295
  18.2 3.5 %collective-permute-start.12 = (bf16[2,128,256]{2,1,0:T(8,128)(2,1)S(1)}, bf16[2,128,256]{2,1,0:T(8,128)(2,1)S(1)}, u32[]{:S(2)}, u32[]{:S(2)}) collective-permute-start(bf16[2,128,256]{2,1,0:T(8,128)(2,1)S(1)} %get-tuple-element.20), channel_id=1, source_target_pairs={{1,0},{0,1},{3,2},{2,3},{5,4},{4,5},{7,6},{6,7},{23,8},{16,9},{17,... | collective-permute-start | bytes 393224 | tf_op jit(solution)/shard_map/ppermute | solution.py:297
  18.4 7.1 %collective-permute-start.9 = (bf16[2,128,256]{2,1,0:T(8,128)(2,1)S(1)}, bf16[2,128,256]{2,1,0:T(8,128)(2,1)S(1)}, u32[]{:S(2)}, u32[]{:S(2)}) collective-permute-start(bf16[2,128,256]{2,1,0:T(8,128)(2,1)S(1)} %get-tuple-element.19), channel_id=1, source_target_pairs={{8,0},{9,1},{10,2},{11,3},{12,4},{13,5},{14,6},{15,7},{0,8},{1,9},... | collective-permute-start | bytes 393224 | tf_op jit(solution)/shard_map/ppermute | solution.py:297
  21.7 8.3 %collective-permute-start.10 = (bf16[2,128,256]{2,1,0:T(8,128)(2,1)S(1)}, bf16[2,128,256]{2,1,0:T(8,128)(2,1)S(1)}, u32[]{:S(2)}, u32[]{:S(2)}) collective-permute-start(bf16[2,128,256]{2,1,0:T(8,128)(2,1)S(1)} %get-tuple-element.21), channel_id=1, source_target_pairs={{2,0},{16,1},{17,2},{18,3},{19,4},{20,5},{21,6},{22,7},{0,8},{1,9}... | collective-permute-start | bytes 393224 | tf_op jit(solution)/shard_map/ppermute | solution.py:297
  21.7 8.3 %collective-permute-start.11 = (bf16[2,128,256]{2,1,0:T(8,128)(2,1)S(1)}, bf16[2,128,256]{2,1,0:T(8,128)(2,1)S(1)}, u32[]{:S(2)}, u32[]{:S(2)}) collective-permute-start(bf16[2,128,256]{2,1,0:T(8,128)(2,1)S(1)} %get-tuple-element.22), channel_id=1, source_target_pairs={{1,0},{0,1},{3,2},{2,3},{5,4},{4,5},{7,6},{6,7},{9,8},{8,9},{11,10... | collective-permute-start | bytes 393224 | tf_op jit(solution)/shard_map/ppermute | solution.py:297

commit v4 on v3

--- a/solution.py
+++ b/solution.py
@@ -70,8 +70,8 @@
 
 
 def turns(n, back):
-    ends = [0, n - 1] if back else [n - 1, 0]
-    return ends + list(range(1, n - 1))
+    inner = list(range(1, n - 1))
+    return [0] + inner[::-1] + [n - 1] if back else [n - 1, 0] + inner
 
 
 def position(n, lats):
@@ -132,12 +132,41 @@
     return (n - 2, n - 1) if i == n - 2 else (i,)
 
 
+def one_hot(order, tile, side, xs):
+    tall = (2 * tile, order)
+    index = lax.broadcasted_iota(jnp.int32, tall, 0)
+    column = jnp.where(index >= tile, index - tile + (1 - side) * tile, index + side * tile)
+    put_at = column - lax.broadcasted_iota(jnp.int32, tall, 1)
+    return jnp.concatenate([jnp.where(put_at == x, 1.0, 0.0) for x in xs], axis=1).astype(jnp.bfloat16)
+
+
+def placer(order, tile, puts_ref, ys):
+    lane = lax.broadcasted_iota(jnp.int32, (order, order), 1)
+
+    def put(values, keep_ref, send_ref, at):
+        rows = []
+        for y, value in zip(ys, values):
+            value = pltpu.roll(value, lax.rem(y, order), 1)
+            rows.append(
+                jnp.concatenate(
+                    [jnp.where(lane >= y, value, 0.0), jnp.where(lane < y, value, 0.0)], axis=1
+                ).astype(jnp.bfloat16)
+            )
+        total = dot(puts_ref[...], jnp.concatenate(rows, axis=0))
+        keep_ref[at] = total[:tile]
+        send_ref[at] = total[tile:].astype(jnp.bfloat16)
+
+    return put
+
+
 def early_kernel(
-    n, lats, slots, mine_ref, near_ref, mats_ref, own_ref, other_ref, probe_ref, full_ref, psi_ref, trn_ref, ext_ref
+    n, lats, slots, mine_ref, near_ref, mats_ref, own_ref, other_ref, probe_ref, full_ref, psi_ref, trn_ref, puts_ref,
+    ext_ref,
 ):
     order, tile = probe_ref.shape[-1], own_ref.shape[2]
     lat, side, at_first, at_second, base = position(n, lats)
     xs, ys, count = corners(slots, base == lat, side, mine_ref, near_ref)
+    puts_ref[...] = one_hot(order, tile, side, xs)
     for m in range(n + 1):
         re, im = mats_ref[m, 0], mats_ref[m, 1]
         for h, (upper, lower) in enumerate(((-im, im), (im, -im))):
@@ -164,8 +193,8 @@
 
 
 def main_kernel(
-    n, lats, slots, mine_ref, near_ref, full_ref, own_ref, other_ref, probe_ref, one_ref, last_ref, meas_ref,
-    near_meas_ref, keep_ref, send_ref, trn_ref, psi_ref, ext_ref,
+    n, lats, slots, mine_ref, near_ref, full_ref, own_ref, other_ref, probe_ref, one_ref, last_ref, puts_ref,
+    meas_ref, near_meas_ref, keep_ref, send_ref, rows_ref, trn_ref, psi_ref, ext_ref,
 ):
     order, tile = probe_ref.shape[-1], own_ref.shape[2]
     half = slots // 2
@@ -173,28 +202,7 @@
     lat, side, at_first, at_second, base = position(n, lats)
     local = base == lat
     xs, ys, count = corners(slots, local, side, mine_ref, near_ref)
-    lane = lax.broadcasted_iota(jnp.int32, (order, order), 1)
-
-    tall = (2 * tile, order)
-    index = lax.broadcasted_iota(jnp.int32, tall, 0)
-    column = jnp.where(index >= tile, index - tile + (1 - side) * tile, index + side * tile)
-    put_at = column - lax.broadcasted_iota(jnp.int32, tall, 1)
-    puts = jnp.concatenate([jnp.where(put_at == x, 1.0, 0.0) for x in xs], axis=1).astype(jnp.bfloat16)
-
-    def put(k, c, values):
-        rows = []
-        for s, value in enumerate(values):
-            value = pltpu.roll(value, lax.rem(ys[s], order), 1)
-            rows.append(
-                jnp.concatenate(
-                    [jnp.where(lane >= ys[s], value, 0.0), jnp.where(lane < ys[s], value, 0.0)], axis=1
-                ).astype(jnp.bfloat16)
-            )
-        total = dot(puts, jnp.concatenate(rows, axis=0))
-        order_back = turns(n, True)
-        i = jnp.where(at_second, order_back.index(n - 1 - k), order_back.index(k))
-        keep_ref[i, c] = total[:tile]
-        send_ref[i, c] = total[tile:].astype(jnp.bfloat16)
+    put = placer(order, tile, puts_ref, ys)
 
     for k in range(1, n - 1):
         i = jnp.where(at_second, n - 2 - k, k - 1)
@@ -224,19 +232,34 @@
         misfit = jnp.where(slot < count, (re * re + im * im) * W_SCALE**-8 - seen * W_SCALE**-4, 0.0)
         mult.append((misfit * re, misfit * im))
     waves = sandwich(full_ref, mult, (n,), True)
-    for k in reversed(range(n)):
+    for k in reversed(range(1, n)):
         grad_re, grad_im, mult = [], [], []
         for s, (re, im) in enumerate(waves):
-            p_re, p_im = (psi_ref[k, s, 0], psi_ref[k, s, 1]) if k else (probe_ref[0], probe_ref[1])
+            p_re, p_im = psi_ref[k, s, 0], psi_ref[k, s, 1]
             grad_re.append(p_re * re + p_im * im)
             grad_im.append(p_re * im - p_im * re)
-            if k > 0:
-                t_re, t_im = trn_ref[k, s, 0], trn_ref[k, s, 1]
-                mult.append((t_re * re + t_im * im, t_re * im - t_im * re))
-        if k > 0:
+            t_re, t_im = trn_ref[k, s, 0], trn_ref[k, s, 1]
+            mult.append((t_re * re + t_im * im, t_re * im - t_im * re))
+        if k > 1:
             waves = sandwich(full_ref, mult, step(n, n - 1 - k), True)
-        put(k, 0, grad_re)
-        put(k, 1, grad_im)
+        i = k - 1 if k == n - 1 else jnp.where(at_second, n - 2 - k, k - 1)
+        put(grad_re, keep_ref, send_ref, (i, 0))
+        put(grad_im, keep_ref, send_ref, (i, 1))
+    for s, wave in enumerate(mult):
+        for c in range(2):
+            rows_ref[s, c] = wave[c].astype(jnp.bfloat16)
+
+
+def first_slice_kernel(n, lats, slots, mine_ref, near_ref, full_ref, probe_ref, puts_ref, rows_ref, keep_ref, send_ref):
+    order, tile = probe_ref.shape[-1], keep_ref.shape[1]
+    lat, side, at_first, at_second, base = position(n, lats)
+    xs, ys, count = corners(slots, base == lat, side, mine_ref, near_ref)
+    put = placer(order, tile, puts_ref, ys)
+    waves = [(rows_ref[s, 0], rows_ref[s, 1]) for s in range(slots // 2)]
+    waves = sandwich(full_ref, waves, step(n, n - 2), True)
+    p_re, p_im = probe_ref[0], probe_ref[1]
+    put([p_re * re + p_im * im for re, im in waves], keep_ref, send_ref, 0)
+    put([p_re * im - p_im * re for re, im in waves], keep_ref, send_ref, 1)
 
 
 def on_device(contrast, probe, offset_x, offset_y, probe_count, measured):
@@ -266,23 +289,27 @@
     vmem = pl.BlockSpec(memory_space=pltpu.VMEM)
     params = pltpu.CompilerParams(vmem_limit_bytes=(16 + 3 * n) << 20)
     mats = jnp.asarray(matrices(order, n - 1))
-    tiles = (n, 2, tile, height)
+    tiles = (2, tile, height)
     fields = jax.ShapeDtypeStruct((half, 2, order, order), jnp.float32)
     full = jax.ShapeDtypeStruct((n + 1, 2, 2 * order, 2 * order), jnp.bfloat16)
-    full, one, last = pl.pallas_call(
+    full, one, last, puts = pl.pallas_call(
         functools.partial(early_kernel, n, lats, slots),
-        out_shape=(full, fields, fields),
+        out_shape=(full, fields, fields, jax.ShapeDtypeStruct((2 * tile, half * order), jnp.bfloat16)),
         in_specs=[vmem] * 6,
-        out_specs=(vmem,) * 3,
+        out_specs=(vmem,) * 4,
         scratch_shapes=[pltpu.VMEM((2, 2, 2 * tile, height), jnp.float32)],
         compiler_params=params,
         cost_estimate=pl.CostEstimate(flops=10**9, bytes_accessed=2 << 20, transcendentals=0),
     )(mine, near, mats, own_early, other_early, probe)
-    keep, send = pl.pallas_call(
+    keep, send, rows = pl.pallas_call(
         functools.partial(main_kernel, n, lats, slots),
-        out_shape=(jax.ShapeDtypeStruct(tiles, jnp.float32), jax.ShapeDtypeStruct(tiles, jnp.bfloat16)),
-        in_specs=[vmem] * 10,
-        out_specs=(vmem, vmem),
+        out_shape=(
+            jax.ShapeDtypeStruct((n - 1,) + tiles, jnp.float32),
+            jax.ShapeDtypeStruct((n - 1,) + tiles, jnp.bfloat16),
+            jax.ShapeDtypeStruct((half, 2, order, order), jnp.bfloat16),
+        ),
+        in_specs=[vmem] * 11,
+        out_specs=(vmem,) * 3,
         scratch_shapes=[
             pltpu.VMEM((n, half, 2, order, order), jnp.float32),
             pltpu.VMEM((n, half, 2, order, order), jnp.float32),
@@ -290,18 +317,31 @@
         ],
         compiler_params=params,
         cost_estimate=pl.CostEstimate(flops=4 * 10**9, bytes_accessed=8 << 20, transcendentals=0),
-    )(mine, near, full, own_late, other_late, probe, one, last, measured, near_measured)
+    )(mine, near, full, own_late, other_late, probe, one, last, puts, measured, near_measured)
 
     from_partner = lax.ppermute(send, AXES, partner)
-    totals = [(keep[i] + from_partner[i].astype(jnp.float32)).astype(jnp.bfloat16) for i in range(n)]
-    returned = [lax.ppermute(totals[i], AXES, [(d, s) for s, d in back_routes[a]]) for i, a in enumerate(back_turn)]
+    keep_first, send_first = pl.pallas_call(
+        functools.partial(first_slice_kernel, n, lats, slots),
+        out_shape=(jax.ShapeDtypeStruct(tiles, jnp.float32), jax.ShapeDtypeStruct(tiles, jnp.bfloat16)),
+        in_specs=[vmem] * 6,
+        out_specs=(vmem, vmem),
+        compiler_params=params,
+        cost_estimate=pl.CostEstimate(flops=10**9, bytes_accessed=2 << 20, transcendentals=0),
+    )(mine, near, full, probe, puts, rows)
+    from_partner_first = lax.ppermute(send_first, AXES, partner)
+    totals = [(keep[i] + from_partner[i].astype(jnp.float32)).astype(jnp.bfloat16) for i in range(n - 1)]
+    of_last = totals.pop()
+    of_first = (keep_first + from_partner_first.astype(jnp.float32)).astype(jnp.bfloat16)
+    at_second = group == n // 2
+    totals = [jnp.where(at_second, of_last, of_first)] + totals + [jnp.where(at_second, of_first, of_last)]
+    returned = [lax.ppermute(totals[a], AXES, [(d, s) for s, d in back_routes[a]]) for a in back_turn]
     returned = jnp.concatenate([r[None] for r in returned], axis=0)
     spot_first, spot_second = jnp.int32(0), jnp.int32(0)
     for i, a in enumerate(back_turn):
         spot_first = jnp.where(group == a, i, spot_first)
         spot_second = jnp.where(group == n - 1 - a, i, spot_second)
     from_first = lax.dynamic_index_in_dim(returned, spot_first, 0, False)
-    from_first = jnp.where(group == first, totals[back_turn.index(first)], from_first)
+    from_first = jnp.where(group == first, totals[first], from_first)
     from_second = lax.dynamic_index_in_dim(returned, spot_second, 0, False).astype(jnp.float32)
     from_second = jnp.where(lat == 0, 0.0, from_second)
     return (from_first.astype(jnp.float32) + from_second)[:, None]

time: 31 us -> 30.5 us (0.984)
  waiting for transfers between devices: 14.8 us -> 13.4 us
  Pallas kernels: 4.64 us -> 5.18 us
  starting transfers between devices: 7.79 us -> 8.15 us
    ppermute x1, waiting for transfers between devices: 1.77 us -> 0.19 us  [on_device(): from_partner = lax.ppermute(send, AXES, partner)]
    pallas_call x0 -> x1, Pallas kernels: none -> 0.95 us  [on_device(): pl.pallas_call(functools.partial(first_slice_kernel, n, lats, slots), out...]
    pallas_call x1, Pallas kernels: 3.67 us -> 3.17 us  [on_device(): pl.pallas_call(functools.partial(main_kernel, n, lats, slots), out_shape=...]
    ppermute x4 -> x5, starting transfers between devices: 3.48 us -> 3.85 us  [the longest x4 3.4 us: on_device(): lax.ppermute(totals[a], AXES, [(d, s) for s, d in back_routes[a]])]
    ppermute x4 -> x5, waiting for transfers between devices: 8.28 us -> 8.41 us  [the longest x4 8.26 us: on_device(): lax.ppermute(totals[a], AXES, [(d, s) for s, d in back_routes[a]])]
  transfers between devices with their start and end apart: 13 -> 14, of which waited for: 6 -> 7; matrix products, arithmetic and copies ran while one was open for 3% -> 3% of each run, Pallas kernels for 3% -> 7%
where the time goes in v4:
time: 30.5 us; the launch traced here: 30.4 us
  waiting for transfers between devices  13.4 us (44%)
  starting transfers between devices  8.15 us (27%)
  Pallas kernels  5.18 us (17%)
  other arithmetic  2.82 us (9%)
  between operations  0.79 us (3%)
    ppermute x4, waiting for transfers between devices, on_device(): lax.ppermute(totals[a], AXES, [(d, s) for s, d in back_routes[a]])  8.26 us
    ppermute x4, waiting for transfers between devices, on_device(): arrived = [lax.ppermute(own_tile, AXES, routes[a]) for a in turn]  3.87 us
    ppermute x4, starting transfers between devices, on_device(): arrived = [lax.ppermute(own_tile, AXES, routes[a]) for a in turn]  3.47 us
    ppermute x4, starting transfers between devices, on_device(): lax.ppermute(totals[a], AXES, [(d, s) for s, d in back_routes[a]])  3.4 us
    pallas_call x1, Pallas kernels, on_device(): pl.pallas_call(functools.partial(main_kernel, n, lats, slots), out_shape=...  3.17 us
    pallas_call x1, Pallas kernels, on_device(): pl.pallas_call(functools.partial(early_kernel, n, lats, slots), out_shape...  1.06 us
    convert_element_type x1, other arithmetic, on_device(): own_tile = contrast[:, 0].astype(jnp.bfloat16)[None]  1.02 us
    pallas_call x1, Pallas kernels, on_device(): pl.pallas_call(functools.partial(first_slice_kernel, n, lats, slots), out...  0.95 us
  transfers between devices with their start and end apart: 14, of which 7 were waited for; matrix products, arithmetic and copies ran while one was open for 3% of the time, Pallas kernels for 7%

profile of v4, /device:TPU:4, one launch (start us, length us, event | category | flops | bytes accessed | tf_op | source)
XLA Modules:
  0.0 30.4 jit_solution(14606587751591820814)
XLA Ops:
  0.0 1.0 %fusion.2 = bf16[1,2,128,256]{3,2,1,0:T(8,128)(2,1)S(1)} fusion(f32[2,1,128,256]{3,2,1,0:T(8,128)} %param.7), kind=kLoop, calls=%fused_computation.10 | loop fusion | flops 65536 | bytes 393216 | tf_op jit(solution)/shard_map/convert_element_type | solution.py:277
  1.0 3.0 %collective-permute-start = (bf16[1,2,128,256]{3,2,1,0:T(8,128)(2,1)S(1)}, bf16[1,2,128,256]{3,2,1,0:T(8,128)(2,1)S(1)}, u32[]{:S(2)}, u32[]{:S(2)}) collective-permute-start(bf16[1,2,128,256]{3,2,1,0:T(8,128)(2,1)S(1)} %fusion.2), channel_id=1, source_target_pairs={{0,23},{1,16},{2,17},{3,18},{4,19},{5,20},{6,21},{7,22},{8,0},{9,1... | collective-permute-start | bytes 393224 | tf_op jit(solution)/shard_map/ppermute | solution.py:278
  4.0 0.0 collective-permute-start.1
  4.0 0.0 collective-permute-start.4
  4.0 0.5 %collective-permute-start.5 = (bf16[1,2,128,256]{3,2,1,0:T(8,128)(2,1)S(1)}, bf16[1,2,128,256]{3,2,1,0:T(8,128)(2,1)S(1)}, u32[]{:S(2)}, u32[]{:S(2)}) collective-permute-start(bf16[1,2,128,256]{3,2,1,0:T(8,128)(2,1)S(1)} %fusion.2), channel_id=1, source_target_pairs={{0,1},{1,0},{2,3},{3,2},{4,5},{5,4},{6,7},{7,6},{8,23},{9,16},{10,... | collective-permute-start | bytes 393224 | tf_op jit(solution)/shard_map/ppermute | solution.py:278
  5.1 0.7 %pad_add_fusion = s32[17]{0:T(128)S(1)} fusion(s32[1]{0:T(128)S(6)} %copy.11, s32[8]{0:T(128)} %param.10, s32[8]{0:T(128)} %param.9), kind=kLoop, calls=%fused_computation.15 | loop fusion | flops 34 | bytes 136 | tf_op jit(solution)/shard_map/concatenate | solution.py:281
  5.9 0.0 collective-permute-start.2
  5.9 1.9 %collective-permute-done = bf16[1,2,128,256]{3,2,1,0:T(8,128)(2,1)S(1)} collective-permute-done((bf16[1,2,128,256]{3,2,1,0:T(8,128)(2,1)S(1)}, bf16[1,2,128,256]{3,2,1,0:T(8,128)(2,1)S(1)}, u32[]{:S(2)}, u32[]{:S(2)}) %collective-permute-start) | collective-permute-done | bytes 131104 | tf_op jit(solution)/shard_map/ppermute | solution.py:278
  7.9 0.0 collective-permute-start.7
  7.9 1.9 %collective-permute-done.1 = bf16[1,2,128,256]{3,2,1,0:T(8,128)(2,1)S(1)} collective-permute-done((bf16[1,2,128,256]{3,2,1,0:T(8,128)(2,1)S(1)}, bf16[1,2,128,256]{3,2,1,0:T(8,128)(2,1)S(1)}, u32[]{:S(2)}, u32[]{:S(2)}) %collective-permute-start.1) | collective-permute-done | bytes 131104 | tf_op jit(solution)/shard_map/ppermute | solution.py:278
  9.8 0.1 collective-permute-start.3
  9.9 0.0 collective-permute-done.4
  10.0 0.0 copy-start
  10.0 0.6 %collective-permute-start.6 = (bf16[2,2,128,256]{3,2,1,0:T(8,128)(2,1)S(1)}, bf16[2,2,128,256]{3,2,1,0:T(8,128)(2,1)S(1)}, u32[]{:S(2)}, u32[]{:S(2)}) collective-permute-start(bf16[2,2,128,256]{3,2,1,0:T(8,128)(2,1)S(1)} %constant_dynamic-update-slice_fusion.own_ref), channel_id=1, source_target_pairs={{0,1},{1,0},{2,3},{3,2},{4,5},{5,4},{6,7},{7,6},{8,9},{9,8},{10,11... | collective-permute-start | bytes 786440 | tf_op jit(solution)/shard_map/ppermute | solution.py:287
  10.5 0.9 %collective-permute-done.3.other_ref = bf16[2,2,128,256]{3,2,1,0:T(8,128)(2,1)S(1)} collective-permute-done((bf16[2,2,128,256]{3,2,1,0:T(8,128)(2,1)S(1)}, bf16[2,2,128,256]{3,2,1,0:T(8,128)(2,1)S(1)}, u32[]{:S(2)}, u32[]{:S(2)}) %collective-permute-start.3) | collective-permute-done | bytes 262176 | tf_op jit(solution)/shard_map/ppermute | solution.py:286
  11.4 1.1 %shard_map.73 = (bf16[5,2,256,256]{3,2,1,0:T(8,128)(2,1)S(1)}, f32[4,2,128,128]{3,2,1,0:T(8,128)S(1)}, f32[4,2,128,128]{3,2,1,0:T(8,128)S(1)}, bf16[256,512]{1,0:T(8,128)(2,1)S(1)}) custom-call(s32[1,128]{1,0:T(1,128)S(1)} %pad_bitcast_fusion.mine_ref, s32[1,128]{1,0:T(1,128)S(1)} %collective-permute-done.2.near_ref, bf16[5,2,128,128]{3,2,1,0:T(8,128)(2,1)S(1)} %copy-done.2, ...), custom_call_target="tpu_custom_call" | custom-call | flops 1000000000 | bytes 2097152 | tf_op jit(solution)/shard_map/pallas_call | solution.py:295
  12.5 3.2 %shard_map.74 = (f32[3,2,128,256]{3,2,1,0:T(8,128)S(1)}, bf16[3,2,128,256]{3,2,1,0:T(8,128)(2,1)S(1)}, bf16[4,2,128,128]{3,2,1,0:T(8,128)(2,1)S(1)}) custom-call(s32[1,128]{1,0:T(1,128)S(1)} %pad_bitcast_fusion.mine_ref, s32[1,128]{1,0:T(1,128)S(1)} %collective-permute-done.2.near_ref, bf16[5,2,256,256]{3,2,1,0:T(8,128)(2,1)S(1)} %get-tuple-element.18.full_ref, ...), custom_call_target="tpu_custom_call" | custom-call | flops 4000000000 | bytes 8388608 | tf_op jit(solution)/shard_map/pallas_call | solution.py:304
  15.7 0.2 collective-permute-start.8
  15.9 1.0 %shard_map.75 = (f32[2,128,256]{2,1,0:T(8,128)S(1)}, bf16[2,128,256]{2,1,0:T(8,128)(2,1)S(1)}) custom-call(s32[1,128]{1,0:T(1,128)S(1)} %pad_bitcast_fusion.mine_ref, s32[1,128]{1,0:T(1,128)S(1)} %collective-permute-done.2.near_ref, bf16[5,2,256,256]{3,2,1,0:T(8,128)(2,1)S(1)} %get-tuple-element.18.full_ref, f32[2,128,128]{2,1,0:T(8,128)S(1)} %copy-done.1, ...), custom_call_target="tpu_custom_call" | custom-call | flops 1000000000 | bytes 2097152 | tf_op jit(solution)/shard_map/pallas_call | solution.py:323
  16.9 0.4 %collective-permute-start.9 = (bf16[2,128,256]{2,1,0:T(8,128)(2,1)S(1)}, bf16[2,128,256]{2,1,0:T(8,128)(2,1)S(1)}, u32[]{:S(2)}, u32[]{:S(2)}) collective-permute-start(bf16[2,128,256]{2,1,0:T(8,128)(2,1)S(1)} %get-tuple-element.26), channel_id=1, source_target_pairs={{0,1},{1,0},{2,3},{3,2},{4,5},{5,4},{6,7},{7,6},{8,9},{9,8},{10,11... | collective-permute-start | bytes 393224 | tf_op jit(solution)/shard_map/ppermute | solution.py:331
  17.3 0.2 collective-permute-done.8
  17.5 0.1 fusion.1
  17.6 0.2 collective-permute-start.11
  17.8 0.4 %collective-permute-start.12 = (bf16[2,128,256]{2,1,0:T(8,128)(2,1)S(1)}, bf16[2,128,256]{2,1,0:T(8,128)(2,1)S(1)}, u32[]{:S(2)}, u32[]{:S(2)}) collective-permute-start(bf16[2,128,256]{2,1,0:T(8,128)(2,1)S(1)} %get-tuple-element.30), channel_id=1, source_target_pairs={{1,0},{0,1},{3,2},{2,3},{5,4},{4,5},{7,6},{6,7},{9,8},{8,9},{11,10... | collective-permute-start | bytes 393224 | tf_op jit(solution)/shard_map/ppermute | solution.py:337
  18.1 0.1 collective-permute-done.9
  18.3 0.1 broadcast_select_fusion.1
  18.4 2.8 %collective-permute-start.10 = (bf16[2,128,256]{2,1,0:T(8,128)(2,1)S(1)}, bf16[2,128,256]{2,1,0:T(8,128)(2,1)S(1)}, u32[]{:S(2)}, u32[]{:S(2)}) collective-permute-start(bf16[2,128,256]{2,1,0:T(8,128)(2,1)S(1)} %get-tuple-element.27), channel_id=1, source_target_pairs={{8,0},{9,1},{10,2},{11,3},{12,4},{13,5},{14,6},{15,7},{0,8},{1,9},... | collective-permute-start | bytes 393224 | tf_op jit(solution)/shard_map/ppermute | solution.py:337
  21.1 0.1 collective-permute-start.13
  21.2 4.0 %collective-permute-done.10 = bf16[2,128,256]{2,1,0:T(8,128)(2,1)S(1)} collective-permute-done((bf16[2,128,256]{2,1,0:T(8,128)(2,1)S(1)}, bf16[2,128,256]{2,1,0:T(8,128)(2,1)S(1)}, u32[]{:S(2)}, u32[]{:S(2)}) %collective-permute-start.10) | collective-permute-done | bytes 131104 | tf_op jit(solution)/shard_map/ppermute | solution.py:337
  25.2 4.3 %collective-permute-done.13 = bf16[2,128,256]{2,1,0:T(8,128)(2,1)S(1)} collective-permute-done((bf16[2,128,256]{2,1,0:T(8,128)(2,1)S(1)}, bf16[2,128,256]{2,1,0:T(8,128)(2,1)S(1)}, u32[]{:S(2)}, u32[]{:S(2)}) %collective-permute-start.13) | collective-permute-done | bytes 131104 | tf_op jit(solution)/shard_map/ppermute | solution.py:337
  29.5 0.1 pad_maximum_fusion
  29.6 0.8 %add_bitcast_fusion = f32[2,1,128,256]{3,2,1,0:T(8,128)} fusion(bf16[4,2,128,256]{3,2,1,0:T(8,128)(2,1)S(1)} %pad_maximum_fusion, s32[]{:T(128)S(6)} %select_n.82, s32[]{:T(128)S(6)} %select_n.76, pred[]{:T(512)S(6)} %eq.24, pred[]{:T(512)S(6)} %eq.10, bf16[3,2,128,256]{3,2,1,0:T(8,128)(2,1)S(1)} %collective-permute-done.8, ...), kind=kLoop, calls=%fused_computation.3 | loop fusion | flops 524288 | bytes 917514 | tf_op jit(solution)/shard_map/add | solution.py:347
  (15 shorter events, 0.1 us)
Async XLA Ops:
  0.0 11.4 %copy-start.2 = (bf16[5,2,128,128]{3,2,1,0:T(8,128)(2,1)S(1)}, bf16[5,2,128,128]{3,2,1,0:T(8,128)(2,1)}, u32[]{:S(2)}) copy-start(bf16[5,2,128,128]{3,2,1,0:T(8,128)(2,1)} %constant.28.clone.mats_ref) | copy-start | bytes 983044
  0.0 11.4 %copy-start.1 = (f32[2,128,128]{2,1,0:T(8,128)S(1)}, f32[2,128,128]{2,1,0:T(8,128)}, u32[]{:S(2)}) copy-start(f32[2,128,128]{2,1,0:T(8,128)} %probe_ref.5) | copy-start | bytes 393220
  1.0 6.8 %collective-permute-start = (bf16[1,2,128,256]{3,2,1,0:T(8,128)(2,1)S(1)}, bf16[1,2,128,256]{3,2,1,0:T(8,128)(2,1)S(1)}, u32[]{:S(2)}, u32[]{:S(2)}) collective-permute-start(bf16[1,2,128,256]{3,2,1,0:T(8,128)(2,1)S(1)} %fusion.2), channel_id=1, source_target_pairs={{0,23},{1,16},{2,17},{3,18},{4,19},{5,20},{6,21},{7,22},{8,0},{9,1... | collective-permute-start | bytes 393224 | tf_op jit(solution)/shard_map/ppermute | solution.py:278
  4.0 5.8 %collective-permute-start.1 = (bf16[1,2,128,256]{3,2,1,0:T(8,128)(2,1)S(1)}, bf16[1,2,128,256]{3,2,1,0:T(8,128)(2,1)S(1)}, u32[]{:S(2)}, u32[]{:S(2)}) collective-permute-start(bf16[1,2,128,256]{3,2,1,0:T(8,128)(2,1)S(1)} %fusion.2), channel_id=1, source_target_pairs={{0,8},{1,9},{2,10},{3,11},{4,12},{5,13},{6,14},{7,15},{8,0},{9,1},... | collective-permute-start | bytes 393224 | tf_op jit(solution)/shard_map/ppermute | solution.py:278
  4.0 5.9 %collective-permute-start.4 = (bf16[1,2,128,256]{3,2,1,0:T(8,128)(2,1)S(1)}, bf16[1,2,128,256]{3,2,1,0:T(8,128)(2,1)S(1)}, u32[]{:S(2)}, u32[]{:S(2)}) collective-permute-start(bf16[1,2,128,256]{3,2,1,0:T(8,128)(2,1)S(1)} %fusion.2), channel_id=1, source_target_pairs={{0,1},{1,0},{2,3},{3,2},{4,5},{5,4},{6,7},{7,6},{8,9},{9,8},{10,11... | collective-permute-start | bytes 393224 | tf_op jit(solution)/shard_map/ppermute | solution.py:278
  4.0 6.0 %collective-permute-start.5 = (bf16[1,2,128,256]{3,2,1,0:T(8,128)(2,1)S(1)}, bf16[1,2,128,256]{3,2,1,0:T(8,128)(2,1)S(1)}, u32[]{:S(2)}, u32[]{:S(2)}) collective-permute-start(bf16[1,2,128,256]{3,2,1,0:T(8,128)(2,1)S(1)} %fusion.2), channel_id=1, source_target_pairs={{0,1},{1,0},{2,3},{3,2},{4,5},{5,4},{6,7},{7,6},{8,23},{9,16},{10,... | collective-permute-start | bytes 393224 | tf_op jit(solution)/shard_map/ppermute | solution.py:278
  5.9 3.9 %collective-permute-start.2 = (s32[1,128]{1,0:T(1,128)S(1)}, s32[1,128]{1,0:T(1,128)S(1)}, u32[]{:S(2)}, u32[]{:S(2)}) collective-permute-start(s32[1,128]{1,0:T(1,128)S(1)} %pad_bitcast_fusion.mine_ref), channel_id=1, source_target_pairs={{0,1},{1,0},{2,3},{3,2},{4,5},{5,4},{6,7},{7,6},{8,9},{9,8},{10,11... | collective-permute-start | bytes 1544 | tf_op jit(solution)/shard_map/ppermute | solution.py:283
  7.9 4.7 %collective-permute-start.7 = (f32[8,128,128]{2,1,0:T(8,128)}, f32[8,128,128]{2,1,0:T(8,128)S(1)}, u32[]{:S(2)}, u32[]{:S(2)}) collective-permute-start(f32[8,128,128]{2,1,0:T(8,128)} %meas_ref.1), channel_id=1, source_target_pairs={{0,1},{1,0},{2,3},{3,2},{4,5},{5,4},{6,7},{7,6},{8,9},{9,8},{10,11... | collective-permute-start | bytes 1572872 | tf_op jit(solution)/shard_map/ppermute | solution.py:284
  9.8 1.6 %collective-permute-start.3 = (bf16[2,2,128,256]{3,2,1,0:T(8,128)(2,1)S(1)}, bf16[2,2,128,256]{3,2,1,0:T(8,128)(2,1)S(1)}, u32[]{:S(2)}, u32[]{:S(2)}) collective-permute-start(bf16[2,2,128,256]{3,2,1,0:T(8,128)(2,1)S(1)} %pad_maximum_fusion.1.own_ref), channel_id=1, source_target_pairs={{0,1},{1,0},{2,3},{3,2},{4,5},{5,4},{6,7},{7,6},{8,9},{9,8},{10,11... | collective-permute-start | bytes 786440 | tf_op jit(solution)/shard_map/ppermute | solution.py:286
  10.0 2.6 %copy-start = (f32[8,128,128]{2,1,0:T(8,128)S(1)}, f32[8,128,128]{2,1,0:T(8,128)}, u32[]{:S(2)}) copy-start(f32[8,128,128]{2,1,0:T(8,128)} %meas_ref.1) | copy-start | bytes 1572868
  10.0 2.5 %collective-permute-start.6 = (bf16[2,2,128,256]{3,2,1,0:T(8,128)(2,1)S(1)}, bf16[2,2,128,256]{3,2,1,0:T(8,128)(2,1)S(1)}, u32[]{:S(2)}, u32[]{:S(2)}) collective-permute-start(bf16[2,2,128,256]{3,2,1,0:T(8,128)(2,1)S(1)} %constant_dynamic-update-slice_fusion.own_ref), channel_id=1, source_target_pairs={{0,1},{1,0},{2,3},{3,2},{4,5},{5,4},{6,7},{7,6},{8,9},{9,8},{10,11... | collective-permute-start | bytes 786440 | tf_op jit(solution)/shard_map/ppermute | solution.py:287
  15.7 1.8 %collective-permute-start.8 = (bf16[3,2,128,256]{3,2,1,0:T(8,128)(2,1)S(1)}, bf16[3,2,128,256]{3,2,1,0:T(8,128)(2,1)S(1)}, u32[]{:S(2)}, u32[]{:S(2)}) collective-permute-start(bf16[3,2,128,256]{3,2,1,0:T(8,128)(2,1)S(1)} %get-tuple-element.23), channel_id=1, source_target_pairs={{0,1},{1,0},{2,3},{3,2},{4,5},{5,4},{6,7},{7,6},{8,9},{9,8},{10,11... | collective-permute-start | bytes 1179656 | tf_op jit(solution)/shard_map/ppermute | solution.py:322
  16.9 1.4 %collective-permute-start.9 = (bf16[2,128,256]{2,1,0:T(8,128)(2,1)S(1)}, bf16[2,128,256]{2,1,0:T(8,128)(2,1)S(1)}, u32[]{:S(2)}, u32[]{:S(2)}) collective-permute-start(bf16[2,128,256]{2,1,0:T(8,128)(2,1)S(1)} %get-tuple-element.26), channel_id=1, source_target_pairs={{0,1},{1,0},{2,3},{3,2},{4,5},{5,4},{6,7},{7,6},{8,9},{9,8},{10,11... | collective-permute-start | bytes 393224 | tf_op jit(solution)/shard_map/ppermute | solution.py:331
  17.6 3.6 %collective-permute-start.11 = (bf16[2,128,256]{2,1,0:T(8,128)(2,1)S(1)}, bf16[2,128,256]{2,1,0:T(8,128)(2,1)S(1)}, u32[]{:S(2)}, u32[]{:S(2)}) collective-permute-start(bf16[2,128,256]{2,1,0:T(8,128)(2,1)S(1)} %get-tuple-element.29), channel_id=1, source_target_pairs={{1,0},{0,1},{3,2},{2,3},{5,4},{4,5},{7,6},{6,7},{23,8},{16,9},{17,... | collective-permute-start | bytes 393224 | tf_op jit(solution)/shard_map/ppermute | solution.py:337
  17.8 3.5 %collective-permute-start.12 = (bf16[2,128,256]{2,1,0:T(8,128)(2,1)S(1)}, bf16[2,128,256]{2,1,0:T(8,128)(2,1)S(1)}, u32[]{:S(2)}, u32[]{:S(2)}) collective-permute-start(bf16[2,128,256]{2,1,0:T(8,128)(2,1)S(1)} %get-tuple-element.30), channel_id=1, source_target_pairs={{1,0},{0,1},{3,2},{2,3},{5,4},{4,5},{7,6},{6,7},{9,8},{8,9},{11,10... | collective-permute-start | bytes 393224 | tf_op jit(solution)/shard_map/ppermute | solution.py:337
  18.4 6.8 %collective-permute-start.10 = (bf16[2,128,256]{2,1,0:T(8,128)(2,1)S(1)}, bf16[2,128,256]{2,1,0:T(8,128)(2,1)S(1)}, u32[]{:S(2)}, u32[]{:S(2)}) collective-permute-start(bf16[2,128,256]{2,1,0:T(8,128)(2,1)S(1)} %get-tuple-element.27), channel_id=1, source_target_pairs={{8,0},{9,1},{10,2},{11,3},{12,4},{13,5},{14,6},{15,7},{0,8},{1,9},... | collective-permute-start | bytes 393224 | tf_op jit(solution)/shard_map/ppermute | solution.py:337
  21.1 8.4 %collective-permute-start.13 = (bf16[2,128,256]{2,1,0:T(8,128)(2,1)S(1)}, bf16[2,128,256]{2,1,0:T(8,128)(2,1)S(1)}, u32[]{:S(2)}, u32[]{:S(2)}) collective-permute-start(bf16[2,128,256]{2,1,0:T(8,128)(2,1)S(1)} %get-tuple-element.28), channel_id=1, source_target_pairs={{2,0},{16,1},{17,2},{18,3},{19,4},{20,5},{21,6},{22,7},{0,8},{1,9}... | collective-permute-start | bytes 393224 | tf_op jit(solution)/shard_map/ppermute | solution.py:337

commit v5 on v4

--- a/solution.py
+++ b/solution.py
@@ -166,17 +166,20 @@
     order, tile = probe_ref.shape[-1], own_ref.shape[2]
     lat, side, at_first, at_second, base = position(n, lats)
     xs, ys, count = corners(slots, base == lat, side, mine_ref, near_ref)
-    puts_ref[...] = one_hot(order, tile, side, xs)
-    for m in range(n + 1):
+    def matrix(m):
         re, im = mats_ref[m, 0], mats_ref[m, 1]
         for h, (upper, lower) in enumerate(((-im, im), (im, -im))):
             full_ref[m, h, :order, :order] = re
             full_ref[m, h, :order, order:] = upper
             full_ref[m, h, order:, :order] = lower
             full_ref[m, h, order:, order:] = re
-    for k in range(2):
+
+    def tiles(k):
         i = jnp.where(at_second, k, 1 - k)
         lay(ext_ref, k, own_ref[i], other_ref[i], side, base + 1 >= lats, tile)
+
+    matrix(0)
+    tiles(0)
     first = [cut(ext_ref, 0, c, xs, ys, order) for c in range(2)]
     re, im = probe_ref[0], probe_ref[1]
     waves = []
@@ -184,12 +187,16 @@
         t_re = 1.0 + c_re
         waves.append((t_re * re - c_im * im, t_re * im + c_im * re))
     waves = sandwich(full_ref, waves, step(n, 0), False)
+    tiles(1)
+    for c in range(2):
+        for s, value in enumerate(cut(ext_ref, 1, c, xs, ys, order)):
+            trn_ref[s, c] = value
+    for m in range(1, n + 1):
+        matrix(m)
+    puts_ref[...] = one_hot(order, tile, side, xs)
     for s, wave in enumerate(waves):
         for c in range(2):
             psi_ref[s, c] = wave[c]
-    for c in range(2):
-        for s, value in enumerate(cut(ext_ref, 1, c, xs, ys, order)):
-            trn_ref[s, c] = value
 
 
 def main_kernel(

time: 30.5 us -> 30.5 us (level)
  no operation moved by 1% of the time
where the time goes in v5:
time: 30.5 us; the launch traced here: 30.4 us
  waiting for transfers between devices  13.4 us (44%)
  starting transfers between devices  8.15 us (27%)
  Pallas kernels  5.18 us (17%)
  other arithmetic  2.82 us (9%)
  between operations  0.79 us (3%)
    ppermute x4, waiting for transfers between devices, on_device(): lax.ppermute(totals[a], AXES, [(d, s) for s, d in back_routes[a]])  8.26 us
    ppermute x4, waiting for transfers between devices, on_device(): arrived = [lax.ppermute(own_tile, AXES, routes[a]) for a in turn]  3.87 us
    ppermute x4, starting transfers between devices, on_device(): arrived = [lax.ppermute(own_tile, AXES, routes[a]) for a in turn]  3.47 us
    ppermute x4, starting transfers between devices, on_device(): lax.ppermute(totals[a], AXES, [(d, s) for s, d in back_routes[a]])  3.4 us
    pallas_call x1, Pallas kernels, on_device(): pl.pallas_call(functools.partial(main_kernel, n, lats, slots), out_shape=...  3.17 us
    pallas_call x1, Pallas kernels, on_device(): pl.pallas_call(functools.partial(early_kernel, n, lats, slots), out_shape...  1.05 us
    convert_element_type x1, other arithmetic, on_device(): own_tile = contrast[:, 0].astype(jnp.bfloat16)[None]  1.02 us
    pallas_call x1, Pallas kernels, on_device(): pl.pallas_call(functools.partial(first_slice_kernel, n, lats, slots), out...  0.95 us
  transfers between devices with their start and end apart: 14, of which 7 were waited for; matrix products, arithmetic and copies ran while one was open for 3% of the time, Pallas kernels for 7%

profile of v5, /device:TPU:4, one launch (start us, length us, event | category | flops | bytes accessed | tf_op | source)
XLA Modules:
  0.0 30.4 jit_solution(11130768841772131408)
XLA Ops:
  0.0 1.0 %fusion.2 = bf16[1,2,128,256]{3,2,1,0:T(8,128)(2,1)S(1)} fusion(f32[2,1,128,256]{3,2,1,0:T(8,128)} %param.7), kind=kLoop, calls=%fused_computation.10 | loop fusion | flops 65536 | bytes 393216 | tf_op jit(solution)/shard_map/convert_element_type | solution.py:284
  1.0 3.0 %collective-permute-start = (bf16[1,2,128,256]{3,2,1,0:T(8,128)(2,1)S(1)}, bf16[1,2,128,256]{3,2,1,0:T(8,128)(2,1)S(1)}, u32[]{:S(2)}, u32[]{:S(2)}) collective-permute-start(bf16[1,2,128,256]{3,2,1,0:T(8,128)(2,1)S(1)} %fusion.2), channel_id=1, source_target_pairs={{0,23},{1,16},{2,17},{3,18},{4,19},{5,20},{6,21},{7,22},{8,0},{9,1... | collective-permute-start | bytes 393224 | tf_op jit(solution)/shard_map/ppermute | solution.py:285
  4.0 0.0 collective-permute-start.1
  4.0 0.0 collective-permute-start.4
  4.0 0.5 %collective-permute-start.5 = (bf16[1,2,128,256]{3,2,1,0:T(8,128)(2,1)S(1)}, bf16[1,2,128,256]{3,2,1,0:T(8,128)(2,1)S(1)}, u32[]{:S(2)}, u32[]{:S(2)}) collective-permute-start(bf16[1,2,128,256]{3,2,1,0:T(8,128)(2,1)S(1)} %fusion.2), channel_id=1, source_target_pairs={{0,1},{1,0},{2,3},{3,2},{4,5},{5,4},{6,7},{7,6},{8,23},{9,16},{10,... | collective-permute-start | bytes 393224 | tf_op jit(solution)/shard_map/ppermute | solution.py:285
  5.1 0.7 %pad_add_fusion = s32[17]{0:T(128)S(1)} fusion(s32[1]{0:T(128)S(6)} %copy.11, s32[8]{0:T(128)} %param.10, s32[8]{0:T(128)} %param.9), kind=kLoop, calls=%fused_computation.15 | loop fusion | flops 34 | bytes 136 | tf_op jit(solution)/shard_map/concatenate | solution.py:288
  5.9 0.0 collective-permute-start.2
  5.9 1.9 %collective-permute-done = bf16[1,2,128,256]{3,2,1,0:T(8,128)(2,1)S(1)} collective-permute-done((bf16[1,2,128,256]{3,2,1,0:T(8,128)(2,1)S(1)}, bf16[1,2,128,256]{3,2,1,0:T(8,128)(2,1)S(1)}, u32[]{:S(2)}, u32[]{:S(2)}) %collective-permute-start) | collective-permute-done | bytes 131104 | tf_op jit(solution)/shard_map/ppermute | solution.py:285
  7.9 0.0 collective-permute-start.7
  7.9 1.9 %collective-permute-done.1 = bf16[1,2,128,256]{3,2,1,0:T(8,128)(2,1)S(1)} collective-permute-done((bf16[1,2,128,256]{3,2,1,0:T(8,128)(2,1)S(1)}, bf16[1,2,128,256]{3,2,1,0:T(8,128)(2,1)S(1)}, u32[]{:S(2)}, u32[]{:S(2)}) %collective-permute-start.1) | collective-permute-done | bytes 131104 | tf_op jit(solution)/shard_map/ppermute | solution.py:285
  9.8 0.1 collective-permute-start.3
  10.0 0.0 copy-start
  10.0 0.6 %collective-permute-start.6 = (bf16[2,2,128,256]{3,2,1,0:T(8,128)(2,1)S(1)}, bf16[2,2,128,256]{3,2,1,0:T(8,128)(2,1)S(1)}, u32[]{:S(2)}, u32[]{:S(2)}) collective-permute-start(bf16[2,2,128,256]{3,2,1,0:T(8,128)(2,1)S(1)} %constant_dynamic-update-slice_fusion.own_ref), channel_id=1, source_target_pairs={{0,1},{1,0},{2,3},{3,2},{4,5},{5,4},{6,7},{7,6},{8,9},{9,8},{10,11... | collective-permute-start | bytes 786440 | tf_op jit(solution)/shard_map/ppermute | solution.py:294
  10.5 0.9 %collective-permute-done.3.other_ref = bf16[2,2,128,256]{3,2,1,0:T(8,128)(2,1)S(1)} collective-permute-done((bf16[2,2,128,256]{3,2,1,0:T(8,128)(2,1)S(1)}, bf16[2,2,128,256]{3,2,1,0:T(8,128)(2,1)S(1)}, u32[]{:S(2)}, u32[]{:S(2)}) %collective-permute-start.3) | collective-permute-done | bytes 262176 | tf_op jit(solution)/shard_map/ppermute | solution.py:293
  11.4 1.1 %shard_map.73 = (bf16[5,2,256,256]{3,2,1,0:T(8,128)(2,1)S(1)}, f32[4,2,128,128]{3,2,1,0:T(8,128)S(1)}, f32[4,2,128,128]{3,2,1,0:T(8,128)S(1)}, bf16[256,512]{1,0:T(8,128)(2,1)S(1)}) custom-call(s32[1,128]{1,0:T(1,128)S(1)} %pad_bitcast_fusion.mine_ref, s32[1,128]{1,0:T(1,128)S(1)} %collective-permute-done.2.near_ref, bf16[5,2,128,128]{3,2,1,0:T(8,128)(2,1)S(1)} %copy-done.2, ...), custom_call_target="tpu_custom_call" | custom-call | flops 1000000000 | bytes 2097152 | tf_op jit(solution)/shard_map/pallas_call | solution.py:302
  12.5 0.0 collective-permute-done.6.other_ref
  12.5 3.2 %shard_map.74 = (f32[3,2,128,256]{3,2,1,0:T(8,128)S(1)}, bf16[3,2,128,256]{3,2,1,0:T(8,128)(2,1)S(1)}, bf16[4,2,128,128]{3,2,1,0:T(8,128)(2,1)S(1)}) custom-call(s32[1,128]{1,0:T(1,128)S(1)} %pad_bitcast_fusion.mine_ref, s32[1,128]{1,0:T(1,128)S(1)} %collective-permute-done.2.near_ref, bf16[5,2,256,256]{3,2,1,0:T(8,128)(2,1)S(1)} %get-tuple-element.18.full_ref, ...), custom_call_target="tpu_custom_call" | custom-call | flops 4000000000 | bytes 8388608 | tf_op jit(solution)/shard_map/pallas_call | solution.py:311
  15.7 0.2 collective-permute-start.8
  15.9 1.0 %shard_map.75 = (f32[2,128,256]{2,1,0:T(8,128)S(1)}, bf16[2,128,256]{2,1,0:T(8,128)(2,1)S(1)}) custom-call(s32[1,128]{1,0:T(1,128)S(1)} %pad_bitcast_fusion.mine_ref, s32[1,128]{1,0:T(1,128)S(1)} %collective-permute-done.2.near_ref, bf16[5,2,256,256]{3,2,1,0:T(8,128)(2,1)S(1)} %get-tuple-element.18.full_ref, f32[2,128,128]{2,1,0:T(8,128)S(1)} %copy-done.1, ...), custom_call_target="tpu_custom_call" | custom-call | flops 1000000000 | bytes 2097152 | tf_op jit(solution)/shard_map/pallas_call | solution.py:330
  16.9 0.4 %collective-permute-start.9 = (bf16[2,128,256]{2,1,0:T(8,128)(2,1)S(1)}, bf16[2,128,256]{2,1,0:T(8,128)(2,1)S(1)}, u32[]{:S(2)}, u32[]{:S(2)}) collective-permute-start(bf16[2,128,256]{2,1,0:T(8,128)(2,1)S(1)} %get-tuple-element.26), channel_id=1, source_target_pairs={{0,1},{1,0},{2,3},{3,2},{4,5},{5,4},{6,7},{7,6},{8,9},{9,8},{10,11... | collective-permute-start | bytes 393224 | tf_op jit(solution)/shard_map/ppermute | solution.py:338
  17.3 0.2 collective-permute-done.8
  17.5 0.1 fusion.1
  17.6 0.2 collective-permute-start.11
  17.8 0.4 %collective-permute-start.12 = (bf16[2,128,256]{2,1,0:T(8,128)(2,1)S(1)}, bf16[2,128,256]{2,1,0:T(8,128)(2,1)S(1)}, u32[]{:S(2)}, u32[]{:S(2)}) collective-permute-start(bf16[2,128,256]{2,1,0:T(8,128)(2,1)S(1)} %get-tuple-element.30), channel_id=1, source_target_pairs={{1,0},{0,1},{3,2},{2,3},{5,4},{4,5},{7,6},{6,7},{9,8},{8,9},{11,10... | collective-permute-start | bytes 393224 | tf_op jit(solution)/shard_map/ppermute | solution.py:344
  18.2 0.2 collective-permute-done.9
  18.3 0.1 broadcast_select_fusion.1
  18.4 2.8 %collective-permute-start.10 = (bf16[2,128,256]{2,1,0:T(8,128)(2,1)S(1)}, bf16[2,128,256]{2,1,0:T(8,128)(2,1)S(1)}, u32[]{:S(2)}, u32[]{:S(2)}) collective-permute-start(bf16[2,128,256]{2,1,0:T(8,128)(2,1)S(1)} %get-tuple-element.27), channel_id=1, source_target_pairs={{8,0},{9,1},{10,2},{11,3},{12,4},{13,5},{14,6},{15,7},{0,8},{1,9},... | collective-permute-start | bytes 393224 | tf_op jit(solution)/shard_map/ppermute | solution.py:344
  21.2 0.1 collective-permute-start.13
  21.2 4.0 %collective-permute-done.10 = bf16[2,128,256]{2,1,0:T(8,128)(2,1)S(1)} collective-permute-done((bf16[2,128,256]{2,1,0:T(8,128)(2,1)S(1)}, bf16[2,128,256]{2,1,0:T(8,128)(2,1)S(1)}, u32[]{:S(2)}, u32[]{:S(2)}) %collective-permute-start.10) | collective-permute-done | bytes 131104 | tf_op jit(solution)/shard_map/ppermute | solution.py:344
  25.2 4.3 %collective-permute-done.13 = bf16[2,128,256]{2,1,0:T(8,128)(2,1)S(1)} collective-permute-done((bf16[2,128,256]{2,1,0:T(8,128)(2,1)S(1)}, bf16[2,128,256]{2,1,0:T(8,128)(2,1)S(1)}, u32[]{:S(2)}, u32[]{:S(2)}) %collective-permute-start.13) | collective-permute-done | bytes 131104 | tf_op jit(solution)/shard_map/ppermute | solution.py:344
  29.5 0.1 pad_maximum_fusion
  29.6 0.8 %add_bitcast_fusion = f32[2,1,128,256]{3,2,1,0:T(8,128)} fusion(bf16[4,2,128,256]{3,2,1,0:T(8,128)(2,1)S(1)} %pad_maximum_fusion, s32[]{:T(128)S(6)} %select_n.82, s32[]{:T(128)S(6)} %select_n.76, pred[]{:T(512)S(6)} %eq.24, pred[]{:T(512)S(6)} %eq.10, bf16[3,2,128,256]{3,2,1,0:T(8,128)(2,1)S(1)} %collective-permute-done.8, ...), kind=kLoop, calls=%fused_computation.3 | loop fusion | flops 524288 | bytes 917514 | tf_op jit(solution)/shard_map/add | solution.py:354
  (15 shorter events, 0.1 us)
Async XLA Ops:
  0.0 11.4 %copy-start.2 = (bf16[5,2,128,128]{3,2,1,0:T(8,128)(2,1)S(1)}, bf16[5,2,128,128]{3,2,1,0:T(8,128)(2,1)}, u32[]{:S(2)}) copy-start(bf16[5,2,128,128]{3,2,1,0:T(8,128)(2,1)} %constant.28.clone.mats_ref) | copy-start | bytes 983044
  0.0 11.4 %copy-start.1 = (f32[2,128,128]{2,1,0:T(8,128)S(1)}, f32[2,128,128]{2,1,0:T(8,128)}, u32[]{:S(2)}) copy-start(f32[2,128,128]{2,1,0:T(8,128)} %probe_ref.5) | copy-start | bytes 393220
  1.0 6.8 %collective-permute-start = (bf16[1,2,128,256]{3,2,1,0:T(8,128)(2,1)S(1)}, bf16[1,2,128,256]{3,2,1,0:T(8,128)(2,1)S(1)}, u32[]{:S(2)}, u32[]{:S(2)}) collective-permute-start(bf16[1,2,128,256]{3,2,1,0:T(8,128)(2,1)S(1)} %fusion.2), channel_id=1, source_target_pairs={{0,23},{1,16},{2,17},{3,18},{4,19},{5,20},{6,21},{7,22},{8,0},{9,1... | collective-permute-start | bytes 393224 | tf_op jit(solution)/shard_map/ppermute | solution.py:285
  4.0 5.8 %collective-permute-start.1 = (bf16[1,2,128,256]{3,2,1,0:T(8,128)(2,1)S(1)}, bf16[1,2,128,256]{3,2,1,0:T(8,128)(2,1)S(1)}, u32[]{:S(2)}, u32[]{:S(2)}) collective-permute-start(bf16[1,2,128,256]{3,2,1,0:T(8,128)(2,1)S(1)} %fusion.2), channel_id=1, source_target_pairs={{0,8},{1,9},{2,10},{3,11},{4,12},{5,13},{6,14},{7,15},{8,0},{9,1},... | collective-permute-start | bytes 393224 | tf_op jit(solution)/shard_map/ppermute | solution.py:285
  4.0 5.9 %collective-permute-start.4 = (bf16[1,2,128,256]{3,2,1,0:T(8,128)(2,1)S(1)}, bf16[1,2,128,256]{3,2,1,0:T(8,128)(2,1)S(1)}, u32[]{:S(2)}, u32[]{:S(2)}) collective-permute-start(bf16[1,2,128,256]{3,2,1,0:T(8,128)(2,1)S(1)} %fusion.2), channel_id=1, source_target_pairs={{0,1},{1,0},{2,3},{3,2},{4,5},{5,4},{6,7},{7,6},{8,9},{9,8},{10,11... | collective-permute-start | bytes 393224 | tf_op jit(solution)/shard_map/ppermute | solution.py:285
  4.0 6.0 %collective-permute-start.5 = (bf16[1,2,128,256]{3,2,1,0:T(8,128)(2,1)S(1)}, bf16[1,2,128,256]{3,2,1,0:T(8,128)(2,1)S(1)}, u32[]{:S(2)}, u32[]{:S(2)}) collective-permute-start(bf16[1,2,128,256]{3,2,1,0:T(8,128)(2,1)S(1)} %fusion.2), channel_id=1, source_target_pairs={{0,1},{1,0},{2,3},{3,2},{4,5},{5,4},{6,7},{7,6},{8,23},{9,16},{10,... | collective-permute-start | bytes 393224 | tf_op jit(solution)/shard_map/ppermute | solution.py:285
  5.9 3.9 %collective-permute-start.2 = (s32[1,128]{1,0:T(1,128)S(1)}, s32[1,128]{1,0:T(1,128)S(1)}, u32[]{:S(2)}, u32[]{:S(2)}) collective-permute-start(s32[1,128]{1,0:T(1,128)S(1)} %pad_bitcast_fusion.mine_ref), channel_id=1, source_target_pairs={{0,1},{1,0},{2,3},{3,2},{4,5},{5,4},{6,7},{7,6},{8,9},{9,8},{10,11... | collective-permute-start | bytes 1544 | tf_op jit(solution)/shard_map/ppermute | solution.py:290
  7.9 4.7 %collective-permute-start.7 = (f32[8,128,128]{2,1,0:T(8,128)}, f32[8,128,128]{2,1,0:T(8,128)S(1)}, u32[]{:S(2)}, u32[]{:S(2)}) collective-permute-start(f32[8,128,128]{2,1,0:T(8,128)} %meas_ref.1), channel_id=1, source_target_pairs={{0,1},{1,0},{2,3},{3,2},{4,5},{5,4},{6,7},{7,6},{8,9},{9,8},{10,11... | collective-permute-start | bytes 1572872 | tf_op jit(solution)/shard_map/ppermute | solution.py:291
  9.8 1.6 %collective-permute-start.3 = (bf16[2,2,128,256]{3,2,1,0:T(8,128)(2,1)S(1)}, bf16[2,2,128,256]{3,2,1,0:T(8,128)(2,1)S(1)}, u32[]{:S(2)}, u32[]{:S(2)}) collective-permute-start(bf16[2,2,128,256]{3,2,1,0:T(8,128)(2,1)S(1)} %pad_maximum_fusion.1.own_ref), channel_id=1, source_target_pairs={{0,1},{1,0},{2,3},{3,2},{4,5},{5,4},{6,7},{7,6},{8,9},{9,8},{10,11... | collective-permute-start | bytes 786440 | tf_op jit(solution)/shard_map/ppermute | solution.py:293
  10.0 2.6 %copy-start = (f32[8,128,128]{2,1,0:T(8,128)S(1)}, f32[8,128,128]{2,1,0:T(8,128)}, u32[]{:S(2)}) copy-start(f32[8,128,128]{2,1,0:T(8,128)} %meas_ref.1) | copy-start | bytes 1572868
  10.0 2.5 %collective-permute-start.6 = (bf16[2,2,128,256]{3,2,1,0:T(8,128)(2,1)S(1)}, bf16[2,2,128,256]{3,2,1,0:T(8,128)(2,1)S(1)}, u32[]{:S(2)}, u32[]{:S(2)}) collective-permute-start(bf16[2,2,128,256]{3,2,1,0:T(8,128)(2,1)S(1)} %constant_dynamic-update-slice_fusion.own_ref), channel_id=1, source_target_pairs={{0,1},{1,0},{2,3},{3,2},{4,5},{5,4},{6,7},{7,6},{8,9},{9,8},{10,11... | collective-permute-start | bytes 786440 | tf_op jit(solution)/shard_map/ppermute | solution.py:294
  15.7 1.8 %collective-permute-start.8 = (bf16[3,2,128,256]{3,2,1,0:T(8,128)(2,1)S(1)}, bf16[3,2,128,256]{3,2,1,0:T(8,128)(2,1)S(1)}, u32[]{:S(2)}, u32[]{:S(2)}) collective-permute-start(bf16[3,2,128,256]{3,2,1,0:T(8,128)(2,1)S(1)} %get-tuple-element.23), channel_id=1, source_target_pairs={{0,1},{1,0},{2,3},{3,2},{4,5},{5,4},{6,7},{7,6},{8,9},{9,8},{10,11... | collective-permute-start | bytes 1179656 | tf_op jit(solution)/shard_map/ppermute | solution.py:329
  16.9 1.4 %collective-permute-start.9 = (bf16[2,128,256]{2,1,0:T(8,128)(2,1)S(1)}, bf16[2,128,256]{2,1,0:T(8,128)(2,1)S(1)}, u32[]{:S(2)}, u32[]{:S(2)}) collective-permute-start(bf16[2,128,256]{2,1,0:T(8,128)(2,1)S(1)} %get-tuple-element.26), channel_id=1, source_target_pairs={{0,1},{1,0},{2,3},{3,2},{4,5},{5,4},{6,7},{7,6},{8,9},{9,8},{10,11... | collective-permute-start | bytes 393224 | tf_op jit(solution)/shard_map/ppermute | solution.py:338
  17.6 3.7 %collective-permute-start.11 = (bf16[2,128,256]{2,1,0:T(8,128)(2,1)S(1)}, bf16[2,128,256]{2,1,0:T(8,128)(2,1)S(1)}, u32[]{:S(2)}, u32[]{:S(2)}) collective-permute-start(bf16[2,128,256]{2,1,0:T(8,128)(2,1)S(1)} %get-tuple-element.29), channel_id=1, source_target_pairs={{1,0},{0,1},{3,2},{2,3},{5,4},{4,5},{7,6},{6,7},{23,8},{16,9},{17,... | collective-permute-start | bytes 393224 | tf_op jit(solution)/shard_map/ppermute | solution.py:344
  17.8 3.5 %collective-permute-start.12 = (bf16[2,128,256]{2,1,0:T(8,128)(2,1)S(1)}, bf16[2,128,256]{2,1,0:T(8,128)(2,1)S(1)}, u32[]{:S(2)}, u32[]{:S(2)}) collective-permute-start(bf16[2,128,256]{2,1,0:T(8,128)(2,1)S(1)} %get-tuple-element.30), channel_id=1, source_target_pairs={{1,0},{0,1},{3,2},{2,3},{5,4},{4,5},{7,6},{6,7},{9,8},{8,9},{11,10... | collective-permute-start | bytes 393224 | tf_op jit(solution)/shard_map/ppermute | solution.py:344
  18.4 6.8 %collective-permute-start.10 = (bf16[2,128,256]{2,1,0:T(8,128)(2,1)S(1)}, bf16[2,128,256]{2,1,0:T(8,128)(2,1)S(1)}, u32[]{:S(2)}, u32[]{:S(2)}) collective-permute-start(bf16[2,128,256]{2,1,0:T(8,128)(2,1)S(1)} %get-tuple-element.27), channel_id=1, source_target_pairs={{8,0},{9,1},{10,2},{11,3},{12,4},{13,5},{14,6},{15,7},{0,8},{1,9},... | collective-permute-start | bytes 393224 | tf_op jit(solution)/shard_map/ppermute | solution.py:344
  21.2 8.3 %collective-permute-start.13 = (bf16[2,128,256]{2,1,0:T(8,128)(2,1)S(1)}, bf16[2,128,256]{2,1,0:T(8,128)(2,1)S(1)}, u32[]{:S(2)}, u32[]{:S(2)}) collective-permute-start(bf16[2,128,256]{2,1,0:T(8,128)(2,1)S(1)} %get-tuple-element.28), channel_id=1, source_target_pairs={{2,0},{16,1},{17,2},{18,3},{19,4},{20,5},{21,6},{22,7},{0,8},{1,9}... | collective-permute-start | bytes 393224 | tf_op jit(solution)/shard_map/ppermute | solution.py:344

commit v6 on v5

--- a/solution.py
+++ b/solution.py
@@ -224,11 +224,13 @@
             cuts = [[last_ref[s, c] for s in range(half)] for c in range(2)]
         mult = []
         for s, (re, im) in enumerate(waves):
-            psi_ref[k, s, 0] = re
-            psi_ref[k, s, 1] = im
             t_re, t_im = 1.0 + cuts[0][s], cuts[1][s]
-            trn_ref[k, s, 0] = t_re
-            trn_ref[k, s, 1] = t_im
+            if k > 1:
+                psi_ref[k, s, 0] = re
+                psi_ref[k, s, 1] = im
+            if k < n - 1:
+                trn_ref[k, s, 0] = t_re
+                trn_ref[k, s, 1] = t_im
             mult.append((t_re * re - t_im * im, t_re * im + t_im * re))
         waves = sandwich(full_ref, mult, step(n, k) if k < n - 1 else (n,), False)
 
@@ -242,10 +244,13 @@
     for k in reversed(range(1, n)):
         grad_re, grad_im, mult = [], [], []
         for s, (re, im) in enumerate(waves):
-            p_re, p_im = psi_ref[k, s, 0], psi_ref[k, s, 1]
+            p_re, p_im = (psi_ref[k, s, 0], psi_ref[k, s, 1]) if k > 1 else (one_ref[s, 0], one_ref[s, 1])
             grad_re.append(p_re * re + p_im * im)
             grad_im.append(p_re * im - p_im * re)
-            t_re, t_im = trn_ref[k, s, 0], trn_ref[k, s, 1]
+            if k < n - 1:
+                t_re, t_im = trn_ref[k, s, 0], trn_ref[k, s, 1]
+            else:
+                t_re, t_im = 1.0 + last_ref[s, 0], last_ref[s, 1]
             mult.append((t_re * re + t_im * im, t_re * im - t_im * re))
         if k > 1:
             waves = sandwich(full_ref, mult, step(n, n - 1 - k), True)

time: 30.5 us -> 30.5 us (level)
  no operation moved by 1% of the time
where the time goes in v6:
time: 30.5 us; the launch traced here: 30.3 us
  waiting for transfers between devices  13.4 us (44%)
  starting transfers between devices  8.15 us (27%)
  Pallas kernels  5.17 us (17%)
  other arithmetic  2.82 us (9%)
  between operations  0.79 us (3%)
    ppermute x4, waiting for transfers between devices, on_device(): lax.ppermute(totals[a], AXES, [(d, s) for s, d in back_routes[a]])  8.25 us
    ppermute x4, waiting for transfers between devices, on_device(): arrived = [lax.ppermute(own_tile, AXES, routes[a]) for a in turn]  3.87 us
    ppermute x4, starting transfers between devices, on_device(): arrived = [lax.ppermute(own_tile, AXES, routes[a]) for a in turn]  3.47 us
    ppermute x4, starting transfers between devices, on_device(): lax.ppermute(totals[a], AXES, [(d, s) for s, d in back_routes[a]])  3.38 us
    pallas_call x1, Pallas kernels, on_device(): pl.pallas_call(functools.partial(main_kernel, n, lats, slots), out_shape=...  3.16 us
    pallas_call x1, Pallas kernels, on_device(): pl.pallas_call(functools.partial(early_kernel, n, lats, slots), out_shape...  1.06 us
    convert_element_type x1, other arithmetic, on_device(): own_tile = contrast[:, 0].astype(jnp.bfloat16)[None]  1.02 us
    pallas_call x1, Pallas kernels, on_device(): pl.pallas_call(functools.partial(first_slice_kernel, n, lats, slots), out...  0.95 us
  transfers between devices with their start and end apart: 14, of which 7 were waited for; matrix products, arithmetic and copies ran while one was open for 3% of the time, Pallas kernels for 7%

profile of v6, /device:TPU:4, one launch (start us, length us, event | category | flops | bytes accessed | tf_op | source)
XLA Modules:
  0.0 30.3 jit_solution(14254724445853083876)
XLA Ops:
  0.0 1.0 %fusion.2 = bf16[1,2,128,256]{3,2,1,0:T(8,128)(2,1)S(1)} fusion(f32[2,1,128,256]{3,2,1,0:T(8,128)} %param.7), kind=kLoop, calls=%fused_computation.10 | loop fusion | flops 65536 | bytes 393216 | tf_op jit(solution)/shard_map/convert_element_type | solution.py:289
  1.0 3.0 %collective-permute-start = (bf16[1,2,128,256]{3,2,1,0:T(8,128)(2,1)S(1)}, bf16[1,2,128,256]{3,2,1,0:T(8,128)(2,1)S(1)}, u32[]{:S(2)}, u32[]{:S(2)}) collective-permute-start(bf16[1,2,128,256]{3,2,1,0:T(8,128)(2,1)S(1)} %fusion.2), channel_id=1, source_target_pairs={{0,23},{1,16},{2,17},{3,18},{4,19},{5,20},{6,21},{7,22},{8,0},{9,1... | collective-permute-start | bytes 393224 | tf_op jit(solution)/shard_map/ppermute | solution.py:290
  4.0 0.0 collective-permute-start.1
  4.0 0.0 collective-permute-start.4
  4.0 0.5 %collective-permute-start.5 = (bf16[1,2,128,256]{3,2,1,0:T(8,128)(2,1)S(1)}, bf16[1,2,128,256]{3,2,1,0:T(8,128)(2,1)S(1)}, u32[]{:S(2)}, u32[]{:S(2)}) collective-permute-start(bf16[1,2,128,256]{3,2,1,0:T(8,128)(2,1)S(1)} %fusion.2), channel_id=1, source_target_pairs={{0,1},{1,0},{2,3},{3,2},{4,5},{5,4},{6,7},{7,6},{8,23},{9,16},{10,... | collective-permute-start | bytes 393224 | tf_op jit(solution)/shard_map/ppermute | solution.py:290
  5.1 0.7 %pad_add_fusion = s32[17]{0:T(128)S(1)} fusion(s32[1]{0:T(128)S(6)} %copy.11, s32[8]{0:T(128)} %param.10, s32[8]{0:T(128)} %param.9), kind=kLoop, calls=%fused_computation.15 | loop fusion | flops 34 | bytes 136 | tf_op jit(solution)/shard_map/concatenate | solution.py:293
  5.9 0.0 collective-permute-start.2
  5.9 1.9 %collective-permute-done = bf16[1,2,128,256]{3,2,1,0:T(8,128)(2,1)S(1)} collective-permute-done((bf16[1,2,128,256]{3,2,1,0:T(8,128)(2,1)S(1)}, bf16[1,2,128,256]{3,2,1,0:T(8,128)(2,1)S(1)}, u32[]{:S(2)}, u32[]{:S(2)}) %collective-permute-start) | collective-permute-done | bytes 131104 | tf_op jit(solution)/shard_map/ppermute | solution.py:290
  7.9 0.0 collective-permute-start.7
  7.9 1.9 %collective-permute-done.1 = bf16[1,2,128,256]{3,2,1,0:T(8,128)(2,1)S(1)} collective-permute-done((bf16[1,2,128,256]{3,2,1,0:T(8,128)(2,1)S(1)}, bf16[1,2,128,256]{3,2,1,0:T(8,128)(2,1)S(1)}, u32[]{:S(2)}, u32[]{:S(2)}) %collective-permute-start.1) | collective-permute-done | bytes 131104 | tf_op jit(solution)/shard_map/ppermute | solution.py:290
  9.8 0.1 collective-permute-start.3
  9.9 0.0 collective-permute-done.4
  10.0 0.0 copy-start
  10.0 0.6 %collective-permute-start.6 = (bf16[2,2,128,256]{3,2,1,0:T(8,128)(2,1)S(1)}, bf16[2,2,128,256]{3,2,1,0:T(8,128)(2,1)S(1)}, u32[]{:S(2)}, u32[]{:S(2)}) collective-permute-start(bf16[2,2,128,256]{3,2,1,0:T(8,128)(2,1)S(1)} %constant_dynamic-update-slice_fusion.own_ref), channel_id=1, source_target_pairs={{0,1},{1,0},{2,3},{3,2},{4,5},{5,4},{6,7},{7,6},{8,9},{9,8},{10,11... | collective-permute-start | bytes 786440 | tf_op jit(solution)/shard_map/ppermute | solution.py:299
  10.5 0.9 %collective-permute-done.3.other_ref = bf16[2,2,128,256]{3,2,1,0:T(8,128)(2,1)S(1)} collective-permute-done((bf16[2,2,128,256]{3,2,1,0:T(8,128)(2,1)S(1)}, bf16[2,2,128,256]{3,2,1,0:T(8,128)(2,1)S(1)}, u32[]{:S(2)}, u32[]{:S(2)}) %collective-permute-start.3) | collective-permute-done | bytes 262176 | tf_op jit(solution)/shard_map/ppermute | solution.py:298
  11.4 1.1 %shard_map.73 = (bf16[5,2,256,256]{3,2,1,0:T(8,128)(2,1)S(1)}, f32[4,2,128,128]{3,2,1,0:T(8,128)S(1)}, f32[4,2,128,128]{3,2,1,0:T(8,128)S(1)}, bf16[256,512]{1,0:T(8,128)(2,1)S(1)}) custom-call(s32[1,128]{1,0:T(1,128)S(1)} %pad_bitcast_fusion.mine_ref, s32[1,128]{1,0:T(1,128)S(1)} %collective-permute-done.2.near_ref, bf16[5,2,128,128]{3,2,1,0:T(8,128)(2,1)S(1)} %copy-done.2, ...), custom_call_target="tpu_custom_call" | custom-call | flops 1000000000 | bytes 2097152 | tf_op jit(solution)/shard_map/pallas_call | solution.py:307
  12.5 3.2 %shard_map.74 = (f32[3,2,128,256]{3,2,1,0:T(8,128)S(1)}, bf16[3,2,128,256]{3,2,1,0:T(8,128)(2,1)S(1)}, bf16[4,2,128,128]{3,2,1,0:T(8,128)(2,1)S(1)}) custom-call(s32[1,128]{1,0:T(1,128)S(1)} %pad_bitcast_fusion.mine_ref, s32[1,128]{1,0:T(1,128)S(1)} %collective-permute-done.2.near_ref, bf16[5,2,256,256]{3,2,1,0:T(8,128)(2,1)S(1)} %get-tuple-element.18.full_ref, ...), custom_call_target="tpu_custom_call" | custom-call | flops 4000000000 | bytes 8388608 | tf_op jit(solution)/shard_map/pallas_call | solution.py:316
  15.7 0.2 collective-permute-start.8
  15.9 1.0 %shard_map.75 = (f32[2,128,256]{2,1,0:T(8,128)S(1)}, bf16[2,128,256]{2,1,0:T(8,128)(2,1)S(1)}) custom-call(s32[1,128]{1,0:T(1,128)S(1)} %pad_bitcast_fusion.mine_ref, s32[1,128]{1,0:T(1,128)S(1)} %collective-permute-done.2.near_ref, bf16[5,2,256,256]{3,2,1,0:T(8,128)(2,1)S(1)} %get-tuple-element.18.full_ref, f32[2,128,128]{2,1,0:T(8,128)S(1)} %copy-done.1, ...), custom_call_target="tpu_custom_call" | custom-call | flops 1000000000 | bytes 2097152 | tf_op jit(solution)/shard_map/pallas_call | solution.py:335
  16.9 0.5 %collective-permute-start.9 = (bf16[2,128,256]{2,1,0:T(8,128)(2,1)S(1)}, bf16[2,128,256]{2,1,0:T(8,128)(2,1)S(1)}, u32[]{:S(2)}, u32[]{:S(2)}) collective-permute-start(bf16[2,128,256]{2,1,0:T(8,128)(2,1)S(1)} %get-tuple-element.26), channel_id=1, source_target_pairs={{0,1},{1,0},{2,3},{3,2},{4,5},{5,4},{6,7},{7,6},{8,9},{9,8},{10,11... | collective-permute-start | bytes 393224 | tf_op jit(solution)/shard_map/ppermute | solution.py:343
  17.3 0.2 collective-permute-done.8
  17.5 0.1 fusion.1
  17.6 0.2 collective-permute-start.11
  17.8 0.4 %collective-permute-start.12 = (bf16[2,128,256]{2,1,0:T(8,128)(2,1)S(1)}, bf16[2,128,256]{2,1,0:T(8,128)(2,1)S(1)}, u32[]{:S(2)}, u32[]{:S(2)}) collective-permute-start(bf16[2,128,256]{2,1,0:T(8,128)(2,1)S(1)} %get-tuple-element.30), channel_id=1, source_target_pairs={{1,0},{0,1},{3,2},{2,3},{5,4},{4,5},{7,6},{6,7},{9,8},{8,9},{11,10... | collective-permute-start | bytes 393224 | tf_op jit(solution)/shard_map/ppermute | solution.py:349
  18.1 0.2 collective-permute-done.9
  18.3 0.1 broadcast_select_fusion.1
  18.4 2.7 %collective-permute-start.10 = (bf16[2,128,256]{2,1,0:T(8,128)(2,1)S(1)}, bf16[2,128,256]{2,1,0:T(8,128)(2,1)S(1)}, u32[]{:S(2)}, u32[]{:S(2)}) collective-permute-start(bf16[2,128,256]{2,1,0:T(8,128)(2,1)S(1)} %get-tuple-element.27), channel_id=1, source_target_pairs={{8,0},{9,1},{10,2},{11,3},{12,4},{13,5},{14,6},{15,7},{0,8},{1,9},... | collective-permute-start | bytes 393224 | tf_op jit(solution)/shard_map/ppermute | solution.py:349
  21.1 0.1 collective-permute-start.13
  21.2 4.0 %collective-permute-done.10 = bf16[2,128,256]{2,1,0:T(8,128)(2,1)S(1)} collective-permute-done((bf16[2,128,256]{2,1,0:T(8,128)(2,1)S(1)}, bf16[2,128,256]{2,1,0:T(8,128)(2,1)S(1)}, u32[]{:S(2)}, u32[]{:S(2)}) %collective-permute-start.10) | collective-permute-done | bytes 131104 | tf_op jit(solution)/shard_map/ppermute | solution.py:349
  25.2 4.2 %collective-permute-done.13 = bf16[2,128,256]{2,1,0:T(8,128)(2,1)S(1)} collective-permute-done((bf16[2,128,256]{2,1,0:T(8,128)(2,1)S(1)}, bf16[2,128,256]{2,1,0:T(8,128)(2,1)S(1)}, u32[]{:S(2)}, u32[]{:S(2)}) %collective-permute-start.13) | collective-permute-done | bytes 131104 | tf_op jit(solution)/shard_map/ppermute | solution.py:349
  29.5 0.1 pad_maximum_fusion
  29.6 0.8 %add_bitcast_fusion = f32[2,1,128,256]{3,2,1,0:T(8,128)} fusion(bf16[4,2,128,256]{3,2,1,0:T(8,128)(2,1)S(1)} %pad_maximum_fusion, s32[]{:T(128)S(6)} %select_n.82, s32[]{:T(128)S(6)} %select_n.76, pred[]{:T(512)S(6)} %eq.24, pred[]{:T(512)S(6)} %eq.10, bf16[3,2,128,256]{3,2,1,0:T(8,128)(2,1)S(1)} %collective-permute-done.8, ...), kind=kLoop, calls=%fused_computation.3 | loop fusion | flops 524288 | bytes 917514 | tf_op jit(solution)/shard_map/add | solution.py:359
  (15 shorter events, 0.1 us)
Async XLA Ops:
  0.0 11.4 %copy-start.2 = (bf16[5,2,128,128]{3,2,1,0:T(8,128)(2,1)S(1)}, bf16[5,2,128,128]{3,2,1,0:T(8,128)(2,1)}, u32[]{:S(2)}) copy-start(bf16[5,2,128,128]{3,2,1,0:T(8,128)(2,1)} %constant.28.clone.mats_ref) | copy-start | bytes 983044
  0.0 11.4 %copy-start.1 = (f32[2,128,128]{2,1,0:T(8,128)S(1)}, f32[2,128,128]{2,1,0:T(8,128)}, u32[]{:S(2)}) copy-start(f32[2,128,128]{2,1,0:T(8,128)} %probe_ref.5) | copy-start | bytes 393220
  1.0 6.8 %collective-permute-start = (bf16[1,2,128,256]{3,2,1,0:T(8,128)(2,1)S(1)}, bf16[1,2,128,256]{3,2,1,0:T(8,128)(2,1)S(1)}, u32[]{:S(2)}, u32[]{:S(2)}) collective-permute-start(bf16[1,2,128,256]{3,2,1,0:T(8,128)(2,1)S(1)} %fusion.2), channel_id=1, source_target_pairs={{0,23},{1,16},{2,17},{3,18},{4,19},{5,20},{6,21},{7,22},{8,0},{9,1... | collective-permute-start | bytes 393224 | tf_op jit(solution)/shard_map/ppermute | solution.py:290
  4.0 5.8 %collective-permute-start.1 = (bf16[1,2,128,256]{3,2,1,0:T(8,128)(2,1)S(1)}, bf16[1,2,128,256]{3,2,1,0:T(8,128)(2,1)S(1)}, u32[]{:S(2)}, u32[]{:S(2)}) collective-permute-start(bf16[1,2,128,256]{3,2,1,0:T(8,128)(2,1)S(1)} %fusion.2), channel_id=1, source_target_pairs={{0,8},{1,9},{2,10},{3,11},{4,12},{5,13},{6,14},{7,15},{8,0},{9,1},... | collective-permute-start | bytes 393224 | tf_op jit(solution)/shard_map/ppermute | solution.py:290
  4.0 5.9 %collective-permute-start.4 = (bf16[1,2,128,256]{3,2,1,0:T(8,128)(2,1)S(1)}, bf16[1,2,128,256]{3,2,1,0:T(8,128)(2,1)S(1)}, u32[]{:S(2)}, u32[]{:S(2)}) collective-permute-start(bf16[1,2,128,256]{3,2,1,0:T(8,128)(2,1)S(1)} %fusion.2), channel_id=1, source_target_pairs={{0,1},{1,0},{2,3},{3,2},{4,5},{5,4},{6,7},{7,6},{8,9},{9,8},{10,11... | collective-permute-start | bytes 393224 | tf_op jit(solution)/shard_map/ppermute | solution.py:290
  4.0 6.0 %collective-permute-start.5 = (bf16[1,2,128,256]{3,2,1,0:T(8,128)(2,1)S(1)}, bf16[1,2,128,256]{3,2,1,0:T(8,128)(2,1)S(1)}, u32[]{:S(2)}, u32[]{:S(2)}) collective-permute-start(bf16[1,2,128,256]{3,2,1,0:T(8,128)(2,1)S(1)} %fusion.2), channel_id=1, source_target_pairs={{0,1},{1,0},{2,3},{3,2},{4,5},{5,4},{6,7},{7,6},{8,23},{9,16},{10,... | collective-permute-start | bytes 393224 | tf_op jit(solution)/shard_map/ppermute | solution.py:290
  5.9 3.9 %collective-permute-start.2 = (s32[1,128]{1,0:T(1,128)S(1)}, s32[1,128]{1,0:T(1,128)S(1)}, u32[]{:S(2)}, u32[]{:S(2)}) collective-permute-start(s32[1,128]{1,0:T(1,128)S(1)} %pad_bitcast_fusion.mine_ref), channel_id=1, source_target_pairs={{0,1},{1,0},{2,3},{3,2},{4,5},{5,4},{6,7},{7,6},{8,9},{9,8},{10,11... | collective-permute-start | bytes 1544 | tf_op jit(solution)/shard_map/ppermute | solution.py:295
  7.9 4.7 %collective-permute-start.7 = (f32[8,128,128]{2,1,0:T(8,128)}, f32[8,128,128]{2,1,0:T(8,128)S(1)}, u32[]{:S(2)}, u32[]{:S(2)}) collective-permute-start(f32[8,128,128]{2,1,0:T(8,128)} %meas_ref.1), channel_id=1, source_target_pairs={{0,1},{1,0},{2,3},{3,2},{4,5},{5,4},{6,7},{7,6},{8,9},{9,8},{10,11... | collective-permute-start | bytes 1572872 | tf_op jit(solution)/shard_map/ppermute | solution.py:296
  9.8 1.6 %collective-permute-start.3 = (bf16[2,2,128,256]{3,2,1,0:T(8,128)(2,1)S(1)}, bf16[2,2,128,256]{3,2,1,0:T(8,128)(2,1)S(1)}, u32[]{:S(2)}, u32[]{:S(2)}) collective-permute-start(bf16[2,2,128,256]{3,2,1,0:T(8,128)(2,1)S(1)} %pad_maximum_fusion.1.own_ref), channel_id=1, source_target_pairs={{0,1},{1,0},{2,3},{3,2},{4,5},{5,4},{6,7},{7,6},{8,9},{9,8},{10,11... | collective-permute-start | bytes 786440 | tf_op jit(solution)/shard_map/ppermute | solution.py:298
  10.0 2.6 %copy-start = (f32[8,128,128]{2,1,0:T(8,128)S(1)}, f32[8,128,128]{2,1,0:T(8,128)}, u32[]{:S(2)}) copy-start(f32[8,128,128]{2,1,0:T(8,128)} %meas_ref.1) | copy-start | bytes 1572868
  10.0 2.5 %collective-permute-start.6 = (bf16[2,2,128,256]{3,2,1,0:T(8,128)(2,1)S(1)}, bf16[2,2,128,256]{3,2,1,0:T(8,128)(2,1)S(1)}, u32[]{:S(2)}, u32[]{:S(2)}) collective-permute-start(bf16[2,2,128,256]{3,2,1,0:T(8,128)(2,1)S(1)} %constant_dynamic-update-slice_fusion.own_ref), channel_id=1, source_target_pairs={{0,1},{1,0},{2,3},{3,2},{4,5},{5,4},{6,7},{7,6},{8,9},{9,8},{10,11... | collective-permute-start | bytes 786440 | tf_op jit(solution)/shard_map/ppermute | solution.py:299
  15.7 1.8 %collective-permute-start.8 = (bf16[3,2,128,256]{3,2,1,0:T(8,128)(2,1)S(1)}, bf16[3,2,128,256]{3,2,1,0:T(8,128)(2,1)S(1)}, u32[]{:S(2)}, u32[]{:S(2)}) collective-permute-start(bf16[3,2,128,256]{3,2,1,0:T(8,128)(2,1)S(1)} %get-tuple-element.23), channel_id=1, source_target_pairs={{0,1},{1,0},{2,3},{3,2},{4,5},{5,4},{6,7},{7,6},{8,9},{9,8},{10,11... | collective-permute-start | bytes 1179656 | tf_op jit(solution)/shard_map/ppermute | solution.py:334
  16.9 1.4 %collective-permute-start.9 = (bf16[2,128,256]{2,1,0:T(8,128)(2,1)S(1)}, bf16[2,128,256]{2,1,0:T(8,128)(2,1)S(1)}, u32[]{:S(2)}, u32[]{:S(2)}) collective-permute-start(bf16[2,128,256]{2,1,0:T(8,128)(2,1)S(1)} %get-tuple-element.26), channel_id=1, source_target_pairs={{0,1},{1,0},{2,3},{3,2},{4,5},{5,4},{6,7},{7,6},{8,9},{9,8},{10,11... | collective-permute-start | bytes 393224 | tf_op jit(solution)/shard_map/ppermute | solution.py:343
  17.6 3.7 %collective-permute-start.11 = (bf16[2,128,256]{2,1,0:T(8,128)(2,1)S(1)}, bf16[2,128,256]{2,1,0:T(8,128)(2,1)S(1)}, u32[]{:S(2)}, u32[]{:S(2)}) collective-permute-start(bf16[2,128,256]{2,1,0:T(8,128)(2,1)S(1)} %get-tuple-element.29), channel_id=1, source_target_pairs={{1,0},{0,1},{3,2},{2,3},{5,4},{4,5},{7,6},{6,7},{23,8},{16,9},{17,... | collective-permute-start | bytes 393224 | tf_op jit(solution)/shard_map/ppermute | solution.py:349
  17.8 3.5 %collective-permute-start.12 = (bf16[2,128,256]{2,1,0:T(8,128)(2,1)S(1)}, bf16[2,128,256]{2,1,0:T(8,128)(2,1)S(1)}, u32[]{:S(2)}, u32[]{:S(2)}) collective-permute-start(bf16[2,128,256]{2,1,0:T(8,128)(2,1)S(1)} %get-tuple-element.30), channel_id=1, source_target_pairs={{1,0},{0,1},{3,2},{2,3},{5,4},{4,5},{7,6},{6,7},{9,8},{8,9},{11,10... | collective-permute-start | bytes 393224 | tf_op jit(solution)/shard_map/ppermute | solution.py:349
  18.4 6.8 %collective-permute-start.10 = (bf16[2,128,256]{2,1,0:T(8,128)(2,1)S(1)}, bf16[2,128,256]{2,1,0:T(8,128)(2,1)S(1)}, u32[]{:S(2)}, u32[]{:S(2)}) collective-permute-start(bf16[2,128,256]{2,1,0:T(8,128)(2,1)S(1)} %get-tuple-element.27), channel_id=1, source_target_pairs={{8,0},{9,1},{10,2},{11,3},{12,4},{13,5},{14,6},{15,7},{0,8},{1,9},... | collective-permute-start | bytes 393224 | tf_op jit(solution)/shard_map/ppermute | solution.py:349
  21.1 8.3 %collective-permute-start.13 = (bf16[2,128,256]{2,1,0:T(8,128)(2,1)S(1)}, bf16[2,128,256]{2,1,0:T(8,128)(2,1)S(1)}, u32[]{:S(2)}, u32[]{:S(2)}) collective-permute-start(bf16[2,128,256]{2,1,0:T(8,128)(2,1)S(1)} %get-tuple-element.28), channel_id=1, source_target_pairs={{2,0},{16,1},{17,2},{18,3},{19,4},{20,5},{21,6},{22,7},{0,8},{1,9}... | collective-permute-start | bytes 393224 | tf_op jit(solution)/shard_map/ppermute | solution.py:349

commit v7 on v5

--- a/solution.py
+++ b/solution.py
@@ -153,7 +153,7 @@
                 ).astype(jnp.bfloat16)
             )
         total = dot(puts_ref[...], jnp.concatenate(rows, axis=0))
-        keep_ref[at] = total[:tile]
+        keep_ref[at] = total[:tile].astype(jnp.bfloat16)
         send_ref[at] = total[tile:].astype(jnp.bfloat16)
 
     return put
@@ -311,7 +311,7 @@
     keep, send, rows = pl.pallas_call(
         functools.partial(main_kernel, n, lats, slots),
         out_shape=(
-            jax.ShapeDtypeStruct((n - 1,) + tiles, jnp.float32),
+            jax.ShapeDtypeStruct((n - 1,) + tiles, jnp.bfloat16),
             jax.ShapeDtypeStruct((n - 1,) + tiles, jnp.bfloat16),
             jax.ShapeDtypeStruct((half, 2, order, order), jnp.bfloat16),
         ),
@@ -329,16 +329,16 @@
     from_partner = lax.ppermute(send, AXES, partner)
     keep_first, send_first = pl.pallas_call(
         functools.partial(first_slice_kernel, n, lats, slots),
-        out_shape=(jax.ShapeDtypeStruct(tiles, jnp.float32), jax.ShapeDtypeStruct(tiles, jnp.bfloat16)),
+        out_shape=(jax.ShapeDtypeStruct(tiles, jnp.bfloat16), jax.ShapeDtypeStruct(tiles, jnp.bfloat16)),
         in_specs=[vmem] * 6,
         out_specs=(vmem, vmem),
         compiler_params=params,
         cost_estimate=pl.CostEstimate(flops=10**9, bytes_accessed=2 << 20, transcendentals=0),
     )(mine, near, full, probe, puts, rows)
     from_partner_first = lax.ppermute(send_first, AXES, partner)
-    totals = [(keep[i] + from_partner[i].astype(jnp.float32)).astype(jnp.bfloat16) for i in range(n - 1)]
+    totals = [(keep[i].astype(jnp.float32) + from_partner[i].astype(jnp.float32)).astype(jnp.bfloat16) for i in range(n - 1)]
     of_last = totals.pop()
-    of_first = (keep_first + from_partner_first.astype(jnp.float32)).astype(jnp.bfloat16)
+    of_first = (keep_first.astype(jnp.float32) + from_partner_first.astype(jnp.float32)).astype(jnp.bfloat16)
     at_second = group == n // 2
     totals = [jnp.where(at_second, of_last, of_first)] + totals + [jnp.where(at_second, of_first, of_last)]
     returned = [lax.ppermute(totals[a], AXES, [(d, s) for s, d in back_routes[a]]) for a in back_turn]

time: 30.5 us -> 30.5 us (level)
  no operation moved by 1% of the time
where the time goes in v7:
time: 30.5 us; the launch traced here: 30.3 us
  waiting for transfers between devices  13.4 us (44%)
  starting transfers between devices  8.15 us (27%)
  Pallas kernels  5.18 us (17%)
  other arithmetic  2.8 us (9%)
  between operations  0.79 us (3%)
    ppermute x4, waiting for transfers between devices, on_device(): lax.ppermute(totals[a], AXES, [(d, s) for s, d in back_routes[a]])  8.25 us
    ppermute x4, waiting for transfers between devices, on_device(): arrived = [lax.ppermute(own_tile, AXES, routes[a]) for a in turn]  3.87 us
    ppermute x4, starting transfers between devices, on_device(): arrived = [lax.ppermute(own_tile, AXES, routes[a]) for a in turn]  3.47 us
    ppermute x4, starting transfers between devices, on_device(): lax.ppermute(totals[a], AXES, [(d, s) for s, d in back_routes[a]])  3.4 us
    pallas_call x1, Pallas kernels, on_device(): pl.pallas_call(functools.partial(main_kernel, n, lats, slots), out_shape=...  3.17 us
    pallas_call x1, Pallas kernels, on_device(): pl.pallas_call(functools.partial(early_kernel, n, lats, slots), out_shape...  1.05 us
    convert_element_type x1, other arithmetic, on_device(): own_tile = contrast[:, 0].astype(jnp.bfloat16)[None]  1.02 us
    pallas_call x1, Pallas kernels, on_device(): pl.pallas_call(functools.partial(first_slice_kernel, n, lats, slots), out...  0.95 us
  transfers between devices with their start and end apart: 14, of which 7 were waited for; matrix products, arithmetic and copies ran while one was open for 3% of the time, Pallas kernels for 7%

profile of v7, /device:TPU:4, one launch (start us, length us, event | category | flops | bytes accessed | tf_op | source)
XLA Modules:
  0.0 30.3 jit_solution(12699607134361848029)
XLA Ops:
  0.0 1.0 %fusion.2 = bf16[1,2,128,256]{3,2,1,0:T(8,128)(2,1)S(1)} fusion(f32[2,1,128,256]{3,2,1,0:T(8,128)} %param.7), kind=kLoop, calls=%fused_computation.10 | loop fusion | flops 65536 | bytes 393216 | tf_op jit(solution)/shard_map/convert_element_type | solution.py:284
  1.0 3.0 %collective-permute-start = (bf16[1,2,128,256]{3,2,1,0:T(8,128)(2,1)S(1)}, bf16[1,2,128,256]{3,2,1,0:T(8,128)(2,1)S(1)}, u32[]{:S(2)}, u32[]{:S(2)}) collective-permute-start(bf16[1,2,128,256]{3,2,1,0:T(8,128)(2,1)S(1)} %fusion.2), channel_id=1, source_target_pairs={{0,23},{1,16},{2,17},{3,18},{4,19},{5,20},{6,21},{7,22},{8,0},{9,1... | collective-permute-start | bytes 393224 | tf_op jit(solution)/shard_map/ppermute | solution.py:285
  4.0 0.5 %collective-permute-start.5 = (bf16[1,2,128,256]{3,2,1,0:T(8,128)(2,1)S(1)}, bf16[1,2,128,256]{3,2,1,0:T(8,128)(2,1)S(1)}, u32[]{:S(2)}, u32[]{:S(2)}) collective-permute-start(bf16[1,2,128,256]{3,2,1,0:T(8,128)(2,1)S(1)} %fusion.2), channel_id=1, source_target_pairs={{0,1},{1,0},{2,3},{3,2},{4,5},{5,4},{6,7},{7,6},{8,23},{9,16},{10,... | collective-permute-start | bytes 393224 | tf_op jit(solution)/shard_map/ppermute | solution.py:285
  5.1 0.7 %pad_add_fusion = s32[17]{0:T(128)S(1)} fusion(s32[1]{0:T(128)S(6)} %copy.11, s32[8]{0:T(128)} %param.10, s32[8]{0:T(128)} %param.9), kind=kLoop, calls=%fused_computation.16 | loop fusion | flops 34 | bytes 136 | tf_op jit(solution)/shard_map/concatenate | solution.py:288
  5.9 0.0 collective-permute-start.2
  5.9 1.9 %collective-permute-done = bf16[1,2,128,256]{3,2,1,0:T(8,128)(2,1)S(1)} collective-permute-done((bf16[1,2,128,256]{3,2,1,0:T(8,128)(2,1)S(1)}, bf16[1,2,128,256]{3,2,1,0:T(8,128)(2,1)S(1)}, u32[]{:S(2)}, u32[]{:S(2)}) %collective-permute-start) | collective-permute-done | bytes 131104 | tf_op jit(solution)/shard_map/ppermute | solution.py:285
  7.9 1.9 %collective-permute-done.1 = bf16[1,2,128,256]{3,2,1,0:T(8,128)(2,1)S(1)} collective-permute-done((bf16[1,2,128,256]{3,2,1,0:T(8,128)(2,1)S(1)}, bf16[1,2,128,256]{3,2,1,0:T(8,128)(2,1)S(1)}, u32[]{:S(2)}, u32[]{:S(2)}) %collective-permute-start.1) | collective-permute-done | bytes 131104 | tf_op jit(solution)/shard_map/ppermute | solution.py:285
  9.8 0.0 collective-permute-done.2.near_ref
  9.8 0.1 collective-permute-start.3
  9.9 0.0 collective-permute-done.4
  9.9 0.0 collective-permute-done.5
  10.0 0.0 copy-start
  10.0 0.6 %collective-permute-start.6 = (bf16[2,2,128,256]{3,2,1,0:T(8,128)(2,1)S(1)}, bf16[2,2,128,256]{3,2,1,0:T(8,128)(2,1)S(1)}, u32[]{:S(2)}, u32[]{:S(2)}) collective-permute-start(bf16[2,2,128,256]{3,2,1,0:T(8,128)(2,1)S(1)} %constant_dynamic-update-slice_fusion.own_ref), channel_id=1, source_target_pairs={{0,1},{1,0},{2,3},{3,2},{4,5},{5,4},{6,7},{7,6},{8,9},{9,8},{10,11... | collective-permute-start | bytes 786440 | tf_op jit(solution)/shard_map/ppermute | solution.py:294
  10.5 0.9 %collective-permute-done.3.other_ref = bf16[2,2,128,256]{3,2,1,0:T(8,128)(2,1)S(1)} collective-permute-done((bf16[2,2,128,256]{3,2,1,0:T(8,128)(2,1)S(1)}, bf16[2,2,128,256]{3,2,1,0:T(8,128)(2,1)S(1)}, u32[]{:S(2)}, u32[]{:S(2)}) %collective-permute-start.3) | collective-permute-done | bytes 262176 | tf_op jit(solution)/shard_map/ppermute | solution.py:293
  11.4 1.1 %shard_map.73 = (bf16[5,2,256,256]{3,2,1,0:T(8,128)(2,1)S(1)}, f32[4,2,128,128]{3,2,1,0:T(8,128)S(1)}, f32[4,2,128,128]{3,2,1,0:T(8,128)S(1)}, bf16[256,512]{1,0:T(8,128)(2,1)S(1)}) custom-call(s32[1,128]{1,0:T(1,128)S(1)} %pad_bitcast_fusion.mine_ref, s32[1,128]{1,0:T(1,128)S(1)} %collective-permute-done.2.near_ref, bf16[5,2,128,128]{3,2,1,0:T(8,128)(2,1)S(1)} %copy-done.2, ...), custom_call_target="tpu_custom_call" | custom-call | flops 1000000000 | bytes 2097152 | tf_op jit(solution)/shard_map/pallas_call | solution.py:302
  12.5 0.0 collective-permute-done.6.other_ref
  12.5 3.2 %shard_map.74 = (bf16[3,2,128,256]{3,2,1,0:T(8,128)(2,1)S(1)}, bf16[3,2,128,256]{3,2,1,0:T(8,128)(2,1)S(1)}, bf16[4,2,128,128]{3,2,1,0:T(8,128)(2,1)S(1)}) custom-call(s32[1,128]{1,0:T(1,128)S(1)} %pad_bitcast_fusion.mine_ref, s32[1,128]{1,0:T(1,128)S(1)} %collective-permute-done.2.near_ref, bf16[5,2,256,256]{3,2,1,0:T(8,128)(2,1)S(1)} %get-tuple-element.18.full_ref, ...), custom_call_target="tpu_custom_call" | custom-call | flops 4000000000 | bytes 8388608 | tf_op jit(solution)/shard_map/pallas_call | solution.py:311
  15.7 0.2 collective-permute-start.8
  15.9 1.0 %shard_map.75 = (bf16[2,128,256]{2,1,0:T(8,128)(2,1)S(1)}, bf16[2,128,256]{2,1,0:T(8,128)(2,1)S(1)}) custom-call(s32[1,128]{1,0:T(1,128)S(1)} %pad_bitcast_fusion.mine_ref, s32[1,128]{1,0:T(1,128)S(1)} %collective-permute-done.2.near_ref, bf16[5,2,256,256]{3,2,1,0:T(8,128)(2,1)S(1)} %get-tuple-element.18.full_ref, f32[2,128,128]{2,1,0:T(8,128)S(1)} %copy-done.1, ...), custom_call_target="tpu_custom_call" | custom-call | flops 1000000000 | bytes 2097152 | tf_op jit(solution)/shard_map/pallas_call | solution.py:330
  16.9 0.4 %collective-permute-start.9 = (bf16[2,128,256]{2,1,0:T(8,128)(2,1)S(1)}, bf16[2,128,256]{2,1,0:T(8,128)(2,1)S(1)}, u32[]{:S(2)}, u32[]{:S(2)}) collective-permute-start(bf16[2,128,256]{2,1,0:T(8,128)(2,1)S(1)} %get-tuple-element.26), channel_id=1, source_target_pairs={{0,1},{1,0},{2,3},{3,2},{4,5},{5,4},{6,7},{7,6},{8,9},{9,8},{10,11... | collective-permute-start | bytes 393224 | tf_op jit(solution)/shard_map/ppermute | solution.py:338
  17.3 0.2 collective-permute-done.8
  17.5 0.1 fusion.1
  17.6 0.2 collective-permute-start.11
  17.8 0.4 %collective-permute-start.12 = (bf16[2,128,256]{2,1,0:T(8,128)(2,1)S(1)}, bf16[2,128,256]{2,1,0:T(8,128)(2,1)S(1)}, u32[]{:S(2)}, u32[]{:S(2)}) collective-permute-start(bf16[2,128,256]{2,1,0:T(8,128)(2,1)S(1)} %get-tuple-element.30), channel_id=1, source_target_pairs={{1,0},{0,1},{3,2},{2,3},{5,4},{4,5},{7,6},{6,7},{9,8},{8,9},{11,10... | collective-permute-start | bytes 393224 | tf_op jit(solution)/shard_map/ppermute | solution.py:344
  18.1 0.2 collective-permute-done.9
  18.3 0.1 broadcast_select_fusion.1
  18.4 2.8 %collective-permute-start.10 = (bf16[2,128,256]{2,1,0:T(8,128)(2,1)S(1)}, bf16[2,128,256]{2,1,0:T(8,128)(2,1)S(1)}, u32[]{:S(2)}, u32[]{:S(2)}) collective-permute-start(bf16[2,128,256]{2,1,0:T(8,128)(2,1)S(1)} %get-tuple-element.27), channel_id=1, source_target_pairs={{8,0},{9,1},{10,2},{11,3},{12,4},{13,5},{14,6},{15,7},{0,8},{1,9},... | collective-permute-start | bytes 393224 | tf_op jit(solution)/shard_map/ppermute | solution.py:344
  21.1 0.1 collective-permute-start.13
  21.2 4.0 %collective-permute-done.10 = bf16[2,128,256]{2,1,0:T(8,128)(2,1)S(1)} collective-permute-done((bf16[2,128,256]{2,1,0:T(8,128)(2,1)S(1)}, bf16[2,128,256]{2,1,0:T(8,128)(2,1)S(1)}, u32[]{:S(2)}, u32[]{:S(2)}) %collective-permute-start.10) | collective-permute-done | bytes 131104 | tf_op jit(solution)/shard_map/ppermute | solution.py:344
  25.2 4.2 %collective-permute-done.13 = bf16[2,128,256]{2,1,0:T(8,128)(2,1)S(1)} collective-permute-done((bf16[2,128,256]{2,1,0:T(8,128)(2,1)S(1)}, bf16[2,128,256]{2,1,0:T(8,128)(2,1)S(1)}, u32[]{:S(2)}, u32[]{:S(2)}) %collective-permute-start.13) | collective-permute-done | bytes 131104 | tf_op jit(solution)/shard_map/ppermute | solution.py:344
  29.5 0.1 pad_maximum_fusion
  29.6 0.8 %add_bitcast_fusion = f32[2,1,128,256]{3,2,1,0:T(8,128)} fusion(bf16[4,2,128,256]{3,2,1,0:T(8,128)(2,1)S(1)} %pad_maximum_fusion, s32[]{:T(128)S(6)} %select_n.82, s32[]{:T(128)S(6)} %select_n.76, pred[]{:T(512)S(6)} %eq.24, pred[]{:T(512)S(6)} %eq.10, bf16[3,2,128,256]{3,2,1,0:T(8,128)(2,1)S(1)} %collective-permute-done.8, ...), kind=kLoop, calls=%fused_computation.3 | loop fusion | flops 589824 | bytes 786442 | tf_op jit(solution)/shard_map/add | solution.py:354
  (15 shorter events, 0.1 us)
Async XLA Ops:
  0.0 11.4 %copy-start.2 = (bf16[5,2,128,128]{3,2,1,0:T(8,128)(2,1)S(1)}, bf16[5,2,128,128]{3,2,1,0:T(8,128)(2,1)}, u32[]{:S(2)}) copy-start(bf16[5,2,128,128]{3,2,1,0:T(8,128)(2,1)} %constant.28.clone.mats_ref) | copy-start | bytes 983044
  0.0 11.4 %copy-start.1 = (f32[2,128,128]{2,1,0:T(8,128)S(1)}, f32[2,128,128]{2,1,0:T(8,128)}, u32[]{:S(2)}) copy-start(f32[2,128,128]{2,1,0:T(8,128)} %probe_ref.5) | copy-start | bytes 393220
  1.0 6.8 %collective-permute-start = (bf16[1,2,128,256]{3,2,1,0:T(8,128)(2,1)S(1)}, bf16[1,2,128,256]{3,2,1,0:T(8,128)(2,1)S(1)}, u32[]{:S(2)}, u32[]{:S(2)}) collective-permute-start(bf16[1,2,128,256]{3,2,1,0:T(8,128)(2,1)S(1)} %fusion.2), channel_id=1, source_target_pairs={{0,23},{1,16},{2,17},{3,18},{4,19},{5,20},{6,21},{7,22},{8,0},{9,1... | collective-permute-start | bytes 393224 | tf_op jit(solution)/shard_map/ppermute | solution.py:285
  4.0 5.8 %collective-permute-start.1 = (bf16[1,2,128,256]{3,2,1,0:T(8,128)(2,1)S(1)}, bf16[1,2,128,256]{3,2,1,0:T(8,128)(2,1)S(1)}, u32[]{:S(2)}, u32[]{:S(2)}) collective-permute-start(bf16[1,2,128,256]{3,2,1,0:T(8,128)(2,1)S(1)} %fusion.2), channel_id=1, source_target_pairs={{0,8},{1,9},{2,10},{3,11},{4,12},{5,13},{6,14},{7,15},{8,0},{9,1},... | collective-permute-start | bytes 393224 | tf_op jit(solution)/shard_map/ppermute | solution.py:285
  4.0 5.9 %collective-permute-start.4 = (bf16[1,2,128,256]{3,2,1,0:T(8,128)(2,1)S(1)}, bf16[1,2,128,256]{3,2,1,0:T(8,128)(2,1)S(1)}, u32[]{:S(2)}, u32[]{:S(2)}) collective-permute-start(bf16[1,2,128,256]{3,2,1,0:T(8,128)(2,1)S(1)} %fusion.2), channel_id=1, source_target_pairs={{0,1},{1,0},{2,3},{3,2},{4,5},{5,4},{6,7},{7,6},{8,9},{9,8},{10,11... | collective-permute-start | bytes 393224 | tf_op jit(solution)/shard_map/ppermute | solution.py:285
  4.0 6.0 %collective-permute-start.5 = (bf16[1,2,128,256]{3,2,1,0:T(8,128)(2,1)S(1)}, bf16[1,2,128,256]{3,2,1,0:T(8,128)(2,1)S(1)}, u32[]{:S(2)}, u32[]{:S(2)}) collective-permute-start(bf16[1,2,128,256]{3,2,1,0:T(8,128)(2,1)S(1)} %fusion.2), channel_id=1, source_target_pairs={{0,1},{1,0},{2,3},{3,2},{4,5},{5,4},{6,7},{7,6},{8,23},{9,16},{10,... | collective-permute-start | bytes 393224 | tf_op jit(solution)/shard_map/ppermute | solution.py:285
  5.9 3.9 %collective-permute-start.2 = (s32[1,128]{1,0:T(1,128)S(1)}, s32[1,128]{1,0:T(1,128)S(1)}, u32[]{:S(2)}, u32[]{:S(2)}) collective-permute-start(s32[1,128]{1,0:T(1,128)S(1)} %pad_bitcast_fusion.mine_ref), channel_id=1, source_target_pairs={{0,1},{1,0},{2,3},{3,2},{4,5},{5,4},{6,7},{7,6},{8,9},{9,8},{10,11... | collective-permute-start | bytes 1544 | tf_op jit(solution)/shard_map/ppermute | solution.py:290
  7.9 4.7 %collective-permute-start.7 = (f32[8,128,128]{2,1,0:T(8,128)}, f32[8,128,128]{2,1,0:T(8,128)S(1)}, u32[]{:S(2)}, u32[]{:S(2)}) collective-permute-start(f32[8,128,128]{2,1,0:T(8,128)} %meas_ref.1), channel_id=1, source_target_pairs={{0,1},{1,0},{2,3},{3,2},{4,5},{5,4},{6,7},{7,6},{8,9},{9,8},{10,11... | collective-permute-start | bytes 1572872 | tf_op jit(solution)/shard_map/ppermute | solution.py:291
  9.8 1.6 %collective-permute-start.3 = (bf16[2,2,128,256]{3,2,1,0:T(8,128)(2,1)S(1)}, bf16[2,2,128,256]{3,2,1,0:T(8,128)(2,1)S(1)}, u32[]{:S(2)}, u32[]{:S(2)}) collective-permute-start(bf16[2,2,128,256]{3,2,1,0:T(8,128)(2,1)S(1)} %pad_maximum_fusion.1.own_ref), channel_id=1, source_target_pairs={{0,1},{1,0},{2,3},{3,2},{4,5},{5,4},{6,7},{7,6},{8,9},{9,8},{10,11... | collective-permute-start | bytes 786440 | tf_op jit(solution)/shard_map/ppermute | solution.py:293
  10.0 2.6 %copy-start = (f32[8,128,128]{2,1,0:T(8,128)S(1)}, f32[8,128,128]{2,1,0:T(8,128)}, u32[]{:S(2)}) copy-start(f32[8,128,128]{2,1,0:T(8,128)} %meas_ref.1) | copy-start | bytes 1572868
  10.0 2.5 %collective-permute-start.6 = (bf16[2,2,128,256]{3,2,1,0:T(8,128)(2,1)S(1)}, bf16[2,2,128,256]{3,2,1,0:T(8,128)(2,1)S(1)}, u32[]{:S(2)}, u32[]{:S(2)}) collective-permute-start(bf16[2,2,128,256]{3,2,1,0:T(8,128)(2,1)S(1)} %constant_dynamic-update-slice_fusion.own_ref), channel_id=1, source_target_pairs={{0,1},{1,0},{2,3},{3,2},{4,5},{5,4},{6,7},{7,6},{8,9},{9,8},{10,11... | collective-permute-start | bytes 786440 | tf_op jit(solution)/shard_map/ppermute | solution.py:294
  15.7 1.8 %collective-permute-start.8 = (bf16[3,2,128,256]{3,2,1,0:T(8,128)(2,1)S(1)}, bf16[3,2,128,256]{3,2,1,0:T(8,128)(2,1)S(1)}, u32[]{:S(2)}, u32[]{:S(2)}) collective-permute-start(bf16[3,2,128,256]{3,2,1,0:T(8,128)(2,1)S(1)} %get-tuple-element.23), channel_id=1, source_target_pairs={{0,1},{1,0},{2,3},{3,2},{4,5},{5,4},{6,7},{7,6},{8,9},{9,8},{10,11... | collective-permute-start | bytes 1179656 | tf_op jit(solution)/shard_map/ppermute | solution.py:329
  16.9 1.4 %collective-permute-start.9 = (bf16[2,128,256]{2,1,0:T(8,128)(2,1)S(1)}, bf16[2,128,256]{2,1,0:T(8,128)(2,1)S(1)}, u32[]{:S(2)}, u32[]{:S(2)}) collective-permute-start(bf16[2,128,256]{2,1,0:T(8,128)(2,1)S(1)} %get-tuple-element.26), channel_id=1, source_target_pairs={{0,1},{1,0},{2,3},{3,2},{4,5},{5,4},{6,7},{7,6},{8,9},{9,8},{10,11... | collective-permute-start | bytes 393224 | tf_op jit(solution)/shard_map/ppermute | solution.py:338
  17.6 3.7 %collective-permute-start.11 = (bf16[2,128,256]{2,1,0:T(8,128)(2,1)S(1)}, bf16[2,128,256]{2,1,0:T(8,128)(2,1)S(1)}, u32[]{:S(2)}, u32[]{:S(2)}) collective-permute-start(bf16[2,128,256]{2,1,0:T(8,128)(2,1)S(1)} %get-tuple-element.29), channel_id=1, source_target_pairs={{1,0},{0,1},{3,2},{2,3},{5,4},{4,5},{7,6},{6,7},{23,8},{16,9},{17,... | collective-permute-start | bytes 393224 | tf_op jit(solution)/shard_map/ppermute | solution.py:344
  17.8 3.5 %collective-permute-start.12 = (bf16[2,128,256]{2,1,0:T(8,128)(2,1)S(1)}, bf16[2,128,256]{2,1,0:T(8,128)(2,1)S(1)}, u32[]{:S(2)}, u32[]{:S(2)}) collective-permute-start(bf16[2,128,256]{2,1,0:T(8,128)(2,1)S(1)} %get-tuple-element.30), channel_id=1, source_target_pairs={{1,0},{0,1},{3,2},{2,3},{5,4},{4,5},{7,6},{6,7},{9,8},{8,9},{11,10... | collective-permute-start | bytes 393224 | tf_op jit(solution)/shard_map/ppermute | solution.py:344
  18.4 6.8 %collective-permute-start.10 = (bf16[2,128,256]{2,1,0:T(8,128)(2,1)S(1)}, bf16[2,128,256]{2,1,0:T(8,128)(2,1)S(1)}, u32[]{:S(2)}, u32[]{:S(2)}) collective-permute-start(bf16[2,128,256]{2,1,0:T(8,128)(2,1)S(1)} %get-tuple-element.27), channel_id=1, source_target_pairs={{8,0},{9,1},{10,2},{11,3},{12,4},{13,5},{14,6},{15,7},{0,8},{1,9},... | collective-permute-start | bytes 393224 | tf_op jit(solution)/shard_map/ppermute | solution.py:344
  21.1 8.3 %collective-permute-start.13 = (bf16[2,128,256]{2,1,0:T(8,128)(2,1)S(1)}, bf16[2,128,256]{2,1,0:T(8,128)(2,1)S(1)}, u32[]{:S(2)}, u32[]{:S(2)}) collective-permute-start(bf16[2,128,256]{2,1,0:T(8,128)(2,1)S(1)} %get-tuple-element.28), channel_id=1, source_target_pairs={{2,0},{16,1},{17,2},{18,3},{19,4},{20,5},{21,6},{22,7},{0,8},{1,9}... | collective-permute-start | bytes 393224 | tf_op jit(solution)/shard_map/ppermute | solution.py:344
